TPU v7x, 32 devices: a whole 2x2x4 slice. The times are simulated.
32 devices in a mesh: grp: 8 (over z, y), head: 4 (over x, core).
Axes of the slice: x: 2, y: 2, z: 4, core: 2. Of those that a mesh axis runs over, the one named last changes fastest.
Arguments:
- long_queries: bfloat16 [4096, 64, 128], P(('grp', 'head')), may hold values from -24 to 24
- long_pairs: bfloat16 [4096, 8, 256], P(('grp', 'head')), may hold values from -24 to 24
- short_queries: bfloat16 [4096, 64, 128], P(('grp', 'head')), may hold values from -24 to 24
- short_pairs: bfloat16 [4096, 8, 256], P(('grp', 'head')), may hold values from -24 to 24
- doc_lengths: int32 [8, 8], replicated, may hold values from 1 to 128, 512 in all within a row
- destinations: int32 [8, 8], replicated, may hold values from 0 to 7, each once within a row
Outputs:
- long_result: bfloat16 [4096, 8192], P(('grp', 'head'))
- short_placed: bfloat16 [8192, 8192], P('grp', 'head')
Inputs may be any that keep to these rules, and one draw needn't show every extreme that they name: `doc_lengths`: each row sums to 512, and each row has a document of exactly 128 tokens. `destinations`: each row is a permutation, so every group receives exactly one short document from every group.
All inputs are finite; a program needn't handle non-finite values.
Results may differ from a plain program's by a relative error of at most 0.0047.
Values may be sent and summed in bfloat16 or wider, within the bound.
No kernel may reach another device: no remote copies, remote signals or barrier semaphores. Data moves between devices by JAX's collectives and lax.ppermute only.
A program may use at most 128 MiB of HBM per device.

v0:
```python
import math

import jax
import jax.numpy as jnp
from jax import lax
from jax.sharding import PartitionSpec as P


def attend_rows(queries, pair_rows, allowed):
    row_count = queries.shape[0]
    pair_heads = pair_rows.shape[1]
    head_size = queries.shape[2]
    group_size = queries.shape[1] // pair_heads
    grouped = queries.reshape(row_count, pair_heads, group_size, head_size)
    key_part = pair_rows[:, :, :head_size]
    value_part = pair_rows[:, :, head_size:]
    score_scale = 1.0 / math.sqrt(head_size)
    scores = (
        jnp.einsum("qhgd,khd->hgqk", grouped, key_part, preferred_element_type=jnp.float32)
        * score_scale
    )
    scores = jnp.where(allowed[None, None], scores, -1e30)
    row_max = jnp.max(scores, axis=-1, keepdims=True)
    raised = jnp.exp(scores - row_max)
    weights = (raised / jnp.sum(raised, axis=-1, keepdims=True)).astype(jnp.bfloat16)
    head_mix = jnp.einsum("hgqk,khd->qhgd", weights, value_part, preferred_element_type=jnp.float32)
    return head_mix.reshape(row_count, queries.shape[1], head_size)


def doc_attend(queries, pair_rows, length):
    position = jnp.arange(queries.shape[0], dtype=jnp.int32)
    allowed = (position[None, :] <= position[:, None]) & (position[None, :] < length)
    head_mix = attend_rows(queries, pair_rows, allowed)
    valid_rows = (position < length)[:, None, None]
    return jnp.where(valid_rows, head_mix, 0.0).astype(jnp.bfloat16)


def on_device(long_queries, long_pairs, short_queries, short_pairs, doc_lengths, destinations):
    head_queries, head_pairs = (
        lax.all_to_all(long_queries, "head", split_axis=1, concat_axis=0, tiled=True),
        lax.all_to_all(long_pairs, "head", split_axis=1, concat_axis=0, tiled=True),
    )
    span_rows = head_queries.shape[0]
    block_rows = min(512, span_rows)
    pieces = []
    for first_row in range(0, span_rows, block_rows):
        last_row = first_row + block_rows
        query_pos = first_row + jnp.arange(block_rows, dtype=jnp.int32)
        key_pos = jnp.arange(last_row, dtype=jnp.int32)
        allowed = key_pos[None, :] <= query_pos[:, None]
        pieces.append(
            attend_rows(head_queries[first_row:last_row], head_pairs[:last_row], allowed).astype(
                jnp.bfloat16
            )
        )
    head_mix = jnp.concatenate(pieces, axis=0)
    returned = lax.all_to_all(head_mix, "head", split_axis=0, concat_axis=1, tiled=True)
    long_result = returned.reshape(returned.shape[0], -1)
    group_count = lax.axis_size("grp")
    local_rows = short_queries.shape[0]
    doc_span = 2 * local_rows * lax.axis_size("head") // group_count
    own_group = lax.axis_index("grp")
    own_lengths = lax.dynamic_index_in_dim(doc_lengths, own_group, 0, keepdims=False)
    own_targets = lax.dynamic_index_in_dim(destinations, own_group, 0, keepdims=False)
    starts = jnp.cumsum(own_lengths) - own_lengths
    slot_ids = jnp.arange(group_count, dtype=jnp.int32)
    chosen = (own_targets[None, :] == slot_ids[:, None]).astype(jnp.int32)
    slot_length = jnp.sum(chosen * own_lengths[None, :], axis=1)
    slot_start = jnp.sum(chosen * starts[None, :], axis=1)
    position = jnp.arange(doc_span, dtype=jnp.int32)
    valid_rows = position[None, :] < slot_length[:, None]
    row_index = jnp.where(valid_rows, slot_start[:, None] + position[None, :], 0)
    group_queries, group_pairs = (
        lax.all_to_all(short_queries, "head", split_axis=1, concat_axis=0, tiled=True),
        lax.all_to_all(short_pairs, "head", split_axis=1, concat_axis=0, tiled=True),
    )
    slot_queries = group_queries[row_index]
    slot_pairs = group_pairs[row_index]
    got_queries, got_pairs = (
        lax.all_to_all(slot_queries, "grp", split_axis=0, concat_axis=0, tiled=True),
        lax.all_to_all(slot_pairs, "grp", split_axis=0, concat_axis=0, tiled=True),
    )
    arriving = (destinations == own_group).astype(jnp.int32)
    got_lengths = jnp.sum(arriving * doc_lengths, axis=1)
    placed = jax.vmap(doc_attend)(got_queries, got_pairs, got_lengths)
    short_placed = placed.reshape(placed.shape[0] * placed.shape[1], -1)
    return (long_result, short_placed)


def solution(mesh):
    placed = (
        P(("grp", "head"), None, None),
        P(("grp", "head"), None, None),
        P(("grp", "head"), None, None),
        P(("grp", "head"), None, None),
        P(),
        P(),
    )
    return jax.shard_map(
        on_device,
        mesh=mesh,
        in_specs=placed,
        out_specs=(P(("grp", "head"), None), P("grp", "head")),
        check_vma=False,
    )
```

profile of v0, /device:TPU:0, one launch (start us, length us, event | category | flops | bytes accessed | tf_op | source)
XLA Modules:
  0.0 280.2 jit_solution(8477645445139898320)
XLA Ops:
  0.6 1.9 copy.37
  2.6 4.2 %all-to-all-start = ((bf16[128,8,256]{2,0,1:T(8,128)(2,1)}), bf16[128,8,256]{2,0,1:T(8,128)(2,1)S(1)}, u32[]{:S(2)}, u32[]{:S(2)}) async-start(bf16[128,8,256]{2,0,1:T(8,128)(2,1)} %copy.37), calls=%async_computation | async-start | bytes 1048576 | tf_op jit(solution)/shard_map/all_to_all | solution.py:41
  6.8 4.3 %copy.39 = bf16[128,64,128]{2,0,1:T(8,128)(2,1)} copy(bf16[128,64,128]{2,1,0:T(8,128)(2,1)} %param.6) | data formatting | bytes 4194304 | tf_op args[0]
  11.0 4.6 %all-to-all-done = bf16[128,8,256]{2,0,1:T(8,128)(2,1)S(1)} async-done(((bf16[128,8,256]{2,0,1:T(8,128)(2,1)}), bf16[128,8,256]{2,0,1:T(8,128)(2,1)S(1)}, u32[]{:S(2)}, u32[]{:S(2)}) %all-to-all-start) | async-done | bytes 524320 | tf_op jit(solution)/shard_map/all_to_all | solution.py:41
  15.6 3.6 %all-to-all-start.1 = ((bf16[128,64,128]{2,0,1:T(8,128)(2,1)}), bf16[128,64,128]{2,0,1:T(8,128)(2,1)S(1)}, u32[]{:S(2)}, u32[]{:S(2)}) async-start(bf16[128,64,128]{2,0,1:T(8,128)(2,1)} %copy.39), calls=%async_computation.1 | async-start | bytes 4194304 | tf_op jit(solution)/shard_map/all_to_all | solution.py:40
  19.2 4.3 %copy.49 = bf16[128,64,128]{2,0,1:T(8,128)(2,1)} copy(bf16[128,64,128]{2,1,0:T(8,128)(2,1)} %param.8) | data formatting | bytes 4194304 | tf_op args[2]
  24.5 20.4 %all-to-all-done.1 = bf16[128,64,128]{2,0,1:T(8,128)(2,1)S(1)} async-done(((bf16[128,64,128]{2,0,1:T(8,128)(2,1)}), bf16[128,64,128]{2,0,1:T(8,128)(2,1)S(1)}, u32[]{:S(2)}, u32[]{:S(2)}) %all-to-all-start.1) | async-done | bytes 2097184 | tf_op jit(solution)/shard_map/all_to_all | solution.py:40
  44.9 3.5 %all-to-all-start.3 = ((bf16[128,8,256]{2,0,1:T(8,128)(2,1)}), bf16[128,8,256]{2,0,1:T(8,128)(2,1)S(1)}, u32[]{:S(2)}, u32[]{:S(2)}) async-start(bf16[128,8,256]{2,0,1:T(8,128)(2,1)} %copy.44), calls=%async_computation.3 | async-start | bytes 1048576 | tf_op jit(solution)/shard_map/all_to_all | solution.py:75
  48.4 1.5 copy.40
  49.8 13.3 %fusion.25 = (f32[2,8,512]{2,1,0:T(8,128)S(1)}, f32[2,8,512,512]{2,3,1,0:T(8,128)}) fusion(pred[512,512]{0,1:T(8,128)(4,1)S(1)} %iota_compare_fusion, bf16[512,2,8,128]{3,0,2,1:T(8,128)(2,1)} %bitcast.108, bf16[512,2,256]{2,0,1:T(8,128)(2,1)S(1)} %bitcast.113), kind=kOutput, calls=%fused_computation.51 | convolution fusion | flops 1090519552 | bytes 19431424 | tf_op jit(solution)/shard_map/sub | solution.py:24
  63.2 3.8 %all-to-all-start.5 = ((bf16[128,64,128]{2,0,1:T(8,128)(2,1)}), bf16[128,64,128]{2,0,1:T(8,128)(2,1)S(1)}, u32[]{:S(2)}, u32[]{:S(2)}) async-start(bf16[128,64,128]{2,0,1:T(8,128)(2,1)} %copy.49), calls=%async_computation.5 | async-start | bytes 4194304 | tf_op jit(solution)/shard_map/all_to_all | solution.py:74
  67.0 10.6 %fusion.13 = bf16[2,8,512,128]{3,2,1,0:T(8,128)(2,1)} fusion(f32[2,8,512,512]{2,3,1,0:T(8,128)} %get-tuple-element.7, f32[2,8,512]{2,1,0:T(8,128)S(1)} %get-tuple-element.6, bf16[512,2,256]{2,0,1:T(8,128)(2,1)S(1)} %bitcast.114), kind=kOutput, calls=%fused_computation.23 | convolution fusion | flops 1083179008 | bytes 19169280 | tf_op jit(solution)/shard_map/hgqk,khd->qhgd/dot_general | solution.py:26
  77.5 4.3 %copy.42 = bf16[512,16,128]{2,1,0:T(8,128)(2,1)} copy(bf16[512,16,128]{2,0,1:T(8,128)(2,1)} %bitcast.109) | data formatting | bytes 4194304 | tf_op jit(solution)/shard_map/convert_element_type | solution.py:52
  81.9 10.7 %all-to-all-done.5 = bf16[128,64,128]{2,0,1:T(8,128)(2,1)S(1)} async-done(((bf16[128,64,128]{2,0,1:T(8,128)(2,1)}), bf16[128,64,128]{2,0,1:T(8,128)(2,1)S(1)}, u32[]{:S(2)}, u32[]{:S(2)}) %all-to-all-start.5) | async-done | bytes 2097184 | tf_op jit(solution)/shard_map/all_to_all | solution.py:74
  92.6 4.4 %all-to-all-start.2 = ((bf16[512,16,128]{2,1,0:T(8,128)(2,1)}), bf16[512,16,128]{2,1,0:T(8,128)(2,1)}, u32[]{:S(2)}, u32[]{:S(2)}) async-start(bf16[512,16,128]{2,1,0:T(8,128)(2,1)} %copy.42), calls=%async_computation.2 | async-start | bytes 4194304 | tf_op jit(solution)/shard_map/all_to_all | solution.py:57
  97.5 3.0 %copy.51 = bf16[4,128,16,128]{3,2,1,0:T(8,128)(2,1)S(1)} copy(bf16[4,128,16,128]{3,1,2,0:T(8,128)(2,1)} %bitcast.103) | data formatting | bytes 4194304 | tf_op jit(solution)/shard_map/all_to_all | solution.py:74
  100.5 8.3 %gather_fusion.1 = bf16[1024,16,128]{2,1,0:T(8,128)(2,1)} fusion(bf16[512,16,128]{2,1,0:T(8,128)(2,1)S(1)} %bitcast.100, s32[1024]{0:T(1024)S(1)} %fusion.19), kind=kCustom, calls=%fused_computation.1 | custom fusion | bytes 8392704 | tf_op jit(solution)/shard_map/gather | solution.py:77
  108.8 14.1 %all-to-all-done.2 = bf16[512,16,128]{2,1,0:T(8,128)(2,1)} async-done(((bf16[512,16,128]{2,1,0:T(8,128)(2,1)}), bf16[512,16,128]{2,1,0:T(8,128)(2,1)}, u32[]{:S(2)}, u32[]{:S(2)}) %all-to-all-start.2) | async-done | bytes 2097184 | tf_op jit(solution)/shard_map/all_to_all | solution.py:57
  122.8 6.5 %all-to-all-start.6 = ((bf16[8,128,16,128]{3,2,1,0:T(8,128)(2,1)}), bf16[8,128,16,128]{3,2,1,0:T(8,128)(2,1)}, u32[]{:S(2)}, u32[]{:S(2)}) async-start(bf16[8,128,16,128]{3,2,1,0:T(8,128)(2,1)} %bitcast.102), calls=%async_computation.6 | async-start | bytes 8388608 | tf_op jit(solution)/shard_map/all_to_all | solution.py:80
  129.9 4.2 %gather_fusion = bf16[1024,2,256]{2,1,0:T(2,128)(2,1)S(1)} fusion(bf16[512,2,256]{2,1,0:T(2,128)(2,1)S(1)} %copy.46, s32[1024]{0:T(1024)S(1)} %fusion.19), kind=kCustom, calls=%fused_computation | custom fusion | bytes 2101248 | tf_op jit(solution)/shard_map/gather | solution.py:78
  135.3 87.2 %all-to-all-done.6 = bf16[8,128,16,128]{3,2,1,0:T(8,128)(2,1)} async-done(((bf16[8,128,16,128]{3,2,1,0:T(8,128)(2,1)}), bf16[8,128,16,128]{3,2,1,0:T(8,128)(2,1)}, u32[]{:S(2)}, u32[]{:S(2)}) %all-to-all-start.6) | async-done | bytes 4194336 | tf_op jit(solution)/shard_map/all_to_all | solution.py:80
  222.4 3.8 %all-to-all-start.4 = ((bf16[8,128,2,256]{3,1,2,0:T(8,128)(2,1)}), bf16[8,128,2,256]{3,1,2,0:T(8,128)(2,1)S(1)}, u32[]{:S(2)}, u32[]{:S(2)}) async-start(bf16[8,128,2,256]{3,1,2,0:T(8,128)(2,1)} %copy.48), calls=%async_computation.4 | async-start | bytes 2097152 | tf_op jit(solution)/shard_map/all_to_all | solution.py:81
  226.6 2.2 copy.43
  228.9 3.1 %copy.69 = bf16[16,8,64,128]{3,1,2,0:T(8,128)(2,1)} copy(bf16[16,8,64,128]{3,2,1,0:T(8,128)(2,1)S(1)} %bitcast.105) | data formatting | bytes 4194304
  232.0 5.4 %copy.52 = bf16[8,128,16,128]{3,1,2,0:T(8,128)(2,1)} copy(bf16[8,128,16,128]{3,2,1,0:T(8,128)(2,1)} %all-to-all-done.6) | data formatting | bytes 8388608 | tf_op jit(solution)/shard_map/all_to_all | solution.py:80
  237.4 14.7 %all-to-all-done.4 = bf16[8,128,2,256]{3,1,2,0:T(8,128)(2,1)S(1)} async-done(((bf16[8,128,2,256]{3,1,2,0:T(8,128)(2,1)}), bf16[8,128,2,256]{3,1,2,0:T(8,128)(2,1)S(1)}, u32[]{:S(2)}, u32[]{:S(2)}) %all-to-all-start.4) | async-done | bytes 1048608 | tf_op jit(solution)/shard_map/all_to_all | solution.py:81
  252.0 3.4 %fusion.16 = f32[8,2,128,128,8]{3,2,4,1,0:T(8,128)S(1)} fusion(bf16[8,128,2,8,128]{4,1,3,2,0:T(8,128)(2,1)} %bitcast.101, bf16[8,128,2,256]{3,1,2,0:T(8,128)(2,1)S(1)} %all-to-all-done.4), kind=kOutput, calls=%fused_computation.27 | convolution fusion | flops 536870912 | bytes 13107200 | tf_op jit(solution)/shard_map/vmap(qhgd,khd->hgqk)/dot_general | solution.py:19
  255.5 2.4 fusion.26
  257.9 3.4 %fusion.12 = bf16[8,128,2,8,128]{1,4,3,2,0:T(8,128)(2,1)} fusion(f32[8,2,8,128,128]{3,4,2,1,0:T(8,128)S(1)} %get-tuple-element.9, f32[8,2,8,128]{3,2,1,0:T(8,128)S(1)} %get-tuple-element.8, bf16[8,128,2,256]{3,1,2,0:T(8,128)(2,1)S(1)} %all-to-all-done.4), kind=kOutput, calls=%fused_computation.21 | convolution fusion | flops 541065216 | bytes 13172736 | tf_op jit(solution)/shard_map/vmap(hgqk,khd->qhgd)/dot_general | solution.py:26
  261.2 6.7 %copy.55 = bf16[8,128,2,8,128]{4,3,2,1,0:T(8,128)(2,1)} copy(bf16[8,128,2,8,128]{1,4,3,2,0:T(8,128)(2,1)} %fusion.12) | data formatting | bytes 8388608 | tf_op jit(solution)/shard_map/vmap(hgqk,khd->qhgd)/transpose | solution.py:26
  268.0 7.3 %reshape.176 = bf16[1024,2048]{1,0:T(8,128)(2,1)} reshape(bf16[8,128,2,8,128]{4,3,2,1,0:T(8,128)(2,1)} %copy.55) | data formatting | bytes 8388608 | tf_op jit(solution)/shard_map/vmap()/reshape | solution.py:27
  275.2 5.0 %select_convert_fusion = bf16[1024,2048]{1,0:T(8,128)(2,1)} fusion(bf16[1024,2048]{1,0:T(8,128)(2,1)} %reshape.176, pred[1024]{0:T(1024)(128)(4,1)S(1)} %get-tuple-element.4), kind=kLoop, calls=%fused_computation.9 | loop fusion | flops 2097152 | bytes 8389632 | tf_op jit(solution)/shard_map/vmap()/convert_element_type | solution.py:35
  (25 shorter events, 3.6 us)
Async XLA Ops:
  2.6 13.1 %all-to-all-start = ((bf16[128,8,256]{2,0,1:T(8,128)(2,1)}), bf16[128,8,256]{2,0,1:T(8,128)(2,1)S(1)}, u32[]{:S(2)}, u32[]{:S(2)}) async-start(bf16[128,8,256]{2,0,1:T(8,128)(2,1)} %copy.37), calls=%async_computation | async-start | bytes 1048576 | tf_op jit(solution)/shard_map/all_to_all | solution.py:41
  11.0 12.5 %copy-start.1 = (bf16[128,8,256]{2,1,0:T(8,128)(2,1)S(1)}, bf16[128,8,256]{2,1,0:T(8,128)(2,1)}, u32[]{:S(2)}) copy-start(bf16[128,8,256]{2,1,0:T(8,128)(2,1)} %param.9) | copy-start | bytes 1572868
  15.6 29.3 %all-to-all-start.1 = ((bf16[128,64,128]{2,0,1:T(8,128)(2,1)}), bf16[128,64,128]{2,0,1:T(8,128)(2,1)S(1)}, u32[]{:S(2)}, u32[]{:S(2)}) async-start(bf16[128,64,128]{2,0,1:T(8,128)(2,1)} %copy.39), calls=%async_computation.1 | async-start | bytes 4194304 | tf_op jit(solution)/shard_map/all_to_all | solution.py:40
  44.9 18.3 %all-to-all-start.3 = ((bf16[128,8,256]{2,0,1:T(8,128)(2,1)}), bf16[128,8,256]{2,0,1:T(8,128)(2,1)S(1)}, u32[]{:S(2)}, u32[]{:S(2)}) async-start(bf16[128,8,256]{2,0,1:T(8,128)(2,1)} %copy.44), calls=%async_computation.3 | async-start | bytes 1048576 | tf_op jit(solution)/shard_map/all_to_all | solution.py:75
  63.2 29.4 %all-to-all-start.5 = ((bf16[128,64,128]{2,0,1:T(8,128)(2,1)}), bf16[128,64,128]{2,0,1:T(8,128)(2,1)S(1)}, u32[]{:S(2)}, u32[]{:S(2)}) async-start(bf16[128,64,128]{2,0,1:T(8,128)(2,1)} %copy.49), calls=%async_computation.5 | async-start | bytes 4194304 | tf_op jit(solution)/shard_map/all_to_all | solution.py:74
  77.5 19.5 %copy-start.2 = (s32[8,8]{1,0:T(8,128)S(1)}, s32[8,8]{1,0:T(8,128)}, u32[]{:S(2)}) copy-start(s32[8,8]{1,0:T(8,128)} %param.10) | copy-start | bytes 772
  77.5 19.7 %copy-start.3 = (s32[8,8]{1,0:T(8,128)S(1)}, s32[8,8]{1,0:T(8,128)}, u32[]{:S(2)}) copy-start(s32[8,8]{1,0:T(8,128)} %param.11) | copy-start | bytes 772
  92.6 4.9 %copy-start = (bf16[128,64,128]{2,0,1:T(8,128)(2,1)}, bf16[128,64,128]{2,0,1:T(8,128)(2,1)S(1)}, u32[]{:S(2)}) copy-start(bf16[128,64,128]{2,0,1:T(8,128)(2,1)S(1)} %all-to-all-done.5) | copy-start | bytes 6291460
  92.6 30.2 %all-to-all-start.2 = ((bf16[512,16,128]{2,1,0:T(8,128)(2,1)}), bf16[512,16,128]{2,1,0:T(8,128)(2,1)}, u32[]{:S(2)}, u32[]{:S(2)}) async-start(bf16[512,16,128]{2,1,0:T(8,128)(2,1)} %copy.42), calls=%async_computation.2 | async-start | bytes 4194304 | tf_op jit(solution)/shard_map/all_to_all | solution.py:57
  122.8 99.6 %all-to-all-start.6 = ((bf16[8,128,16,128]{3,2,1,0:T(8,128)(2,1)}), bf16[8,128,16,128]{3,2,1,0:T(8,128)(2,1)}, u32[]{:S(2)}, u32[]{:S(2)}) async-start(bf16[8,128,16,128]{3,2,1,0:T(8,128)(2,1)} %bitcast.102), calls=%async_computation.6 | async-start | bytes 8388608 | tf_op jit(solution)/shard_map/all_to_all | solution.py:80
  222.4 29.6 %all-to-all-start.4 = ((bf16[8,128,2,256]{3,1,2,0:T(8,128)(2,1)}), bf16[8,128,2,256]{3,1,2,0:T(8,128)(2,1)S(1)}, u32[]{:S(2)}, u32[]{:S(2)}) async-start(bf16[8,128,2,256]{3,1,2,0:T(8,128)(2,1)} %copy.48), calls=%async_computation.4 | async-start | bytes 2097152 | tf_op jit(solution)/shard_map/all_to_all | solution.py:81
where the time goes:
time: 281 us; the launch traced here: 280 us
  waiting for transfers between devices  152 us (54%)
  local copies, waits for them, and re-layouts  59.1 us (21%)
  matrix products  30.7 us (11%)
  starting transfers between devices  29.8 us (11%)
  other arithmetic  8.24 us (3%)
    all_to_all x1, waiting for transfers between devices, on_device(): lax.all_to_all(slot_queries, 'grp', split_axis=0, concat_axis=0, tiled=True)  87.2 us
    all_to_all x1, waiting for transfers between devices, on_device(): lax.all_to_all(long_queries, 'head', split_axis=1, concat_axis=0, tiled=T...  20.4 us
    all_to_all x1, waiting for transfers between devices, on_device(): lax.all_to_all(slot_pairs, 'grp', split_axis=0, concat_axis=0, tiled=True)  14.7 us
    unnamed x13, local copies, waits for them, and re-layouts  14.5 us
    all_to_all x1, waiting for transfers between devices, on_device(): lax.all_to_all(head_mix, 'head', split_axis=0, concat_axis=1, tiled=True)  14.1 us
    dot_general x2, matrix products, attend_rows(): jnp.einsum('hgqk,khd->qhgd', weights, value_part, preferred_element_type=...  13.9 us
    sub x1, matrix products, attend_rows(): raised = jnp.exp(scores - row_max)  13.3 us
    all_to_all x1, waiting for transfers between devices, on_device(): lax.all_to_all(short_queries, 'head', split_axis=1, concat_axis=0, tiled=...  10.7 us
  transfers between devices with their start and end apart: 7, of which 6 were waited for; matrix products, arithmetic and copies ran while one was open for 24% of the time, Pallas kernels for 0%

commit v1 on v0

v1 whole, which is shorter than its diff:
```python
import functools
import math

import jax
import jax.numpy as jnp
from jax import lax
from jax.experimental import pallas as pl
from jax.experimental.pallas import tpu as pltpu
from jax.sharding import PartitionSpec as P

LOG2_E = 1.4426950408889634
VMEM_LIMIT = 48 * 1024 * 1024


def softmax_mix(queries, keys, values_and_ones, allowed, scale):
    scores = lax.dot_general(queries, keys, (((1,), (1,)), ((), ())), preferred_element_type=jnp.float32)
    scores = jnp.where(allowed, scores, -1e30)
    row_max = jnp.max(scores, axis=-1, keepdims=True)
    raised = jnp.exp2((scores - row_max) * scale).astype(jnp.bfloat16)
    both = jnp.dot(raised, values_and_ones, preferred_element_type=jnp.float32)
    size = keys.shape[1]
    return both[:, :size] / both[:, size:]


def with_ones(values):
    return jnp.concatenate([values, jnp.ones_like(values)], axis=1)


def long_kernel(first_ref, q_ref, kv_ref, out_ref, *, scale):
    rows, key_rows = q_ref.shape[0], kv_ref.shape[0]
    size = kv_ref.shape[1] // 2
    position = first_ref[0] + lax.broadcasted_iota(jnp.int32, (rows, key_rows), 0)
    allowed = lax.broadcasted_iota(jnp.int32, (rows, key_rows), 1) <= position
    keys, values = kv_ref[:, :size], with_ones(kv_ref[:, size:])
    for h in range(q_ref.shape[1] // size):
        columns = slice(h * size, (h + 1) * size)
        mixed = softmax_mix(q_ref[:, columns], keys, values, allowed, scale)
        out_ref[:, columns] = mixed.astype(out_ref.dtype)


def long_attend(queries, pairs, first_row, size):
    rows, width = queries.shape
    key_rows, pair_width = pairs.shape
    kv_heads = pair_width // (2 * size)
    share = width // kv_heads
    scores = rows * key_rows * (width // size)
    return pl.pallas_call(
        functools.partial(long_kernel, scale=LOG2_E / math.sqrt(size)),
        out_shape=jax.ShapeDtypeStruct((rows, width), jnp.bfloat16),
        grid=(kv_heads,),
        in_specs=[
            pl.BlockSpec(memory_space=pltpu.SMEM),
            pl.BlockSpec((rows, share), lambda c: (0, c)),
            pl.BlockSpec((key_rows, 2 * size), lambda c: (0, c)),
        ],
        out_specs=pl.BlockSpec((rows, share), lambda c: (0, c)),
        compiler_params=pltpu.CompilerParams(vmem_limit_bytes=VMEM_LIMIT),
        cost_estimate=pl.CostEstimate(
            flops=4 * scores * size, bytes_accessed=4 * rows * width + 2 * key_rows * pair_width, transcendentals=scores
        ),
        name="long_attend",
    )(first_row, queries, pairs)


def short_kernel(place_ref, lengths_ref, targets_ref, *refs, blocks, scale, size):
    q_blocks, kv_blocks = refs[:blocks], refs[blocks : 2 * blocks]
    out_ref, q_ref, kv_ref, mixed_ref, start_ref, length_ref = refs[2 * blocks :]
    slots, span, width = out_ref.shape
    rows = q_ref.shape[0]
    block_rows = rows // blocks
    group, own = place_ref[0], place_ref[1]
    for k in range(blocks):
        at = pl.ds(pl.multiple_of((own ^ k) * block_rows, block_rows), block_rows)
        q_ref[at, :] = q_blocks[k][:, :width]
        kv_ref[at, :] = kv_blocks[k][:, kv_blocks[k].shape[1] - 2 * size :]
    row = lax.broadcasted_iota(jnp.int32, (rows, 1), 0)
    begin = jnp.zeros((rows, 1), jnp.int32)
    start = jnp.int32(0)
    for j in range(slots):
        slot, length = targets_ref[group, j], lengths_ref[group, j]
        start_ref[slot] = start
        length_ref[slot] = length
        begin = jnp.where(row >= start, start, begin)
        start = start + length
    for first in range(0, rows, span):
        low = max(0, first - span)
        here = slice(first, first + span)
        window = slice(low, first + span)
        key_rows = first + span - low
        key_row = low + lax.broadcasted_iota(jnp.int32, (span, key_rows), 1)
        allowed = (key_row >= begin[here]) & (key_row <= row[here])
        keys, values = kv_ref[window, :size], with_ones(kv_ref[window, size:])
        for h in range(width // size):
            columns = slice(h * size, (h + 1) * size)
            mixed = softmax_mix(q_ref[here, columns], keys, values, allowed, scale)
            mixed_ref[here, columns] = mixed.astype(mixed_ref.dtype)
    place = lax.broadcasted_iota(jnp.int32, (span, rows), 0)
    source = lax.broadcasted_iota(jnp.int32, (span, rows), 1)
    for d in range(slots):
        chosen = (source == place + start_ref[d]) & (place < length_ref[d])
        picked = jnp.dot(chosen.astype(jnp.bfloat16), mixed_ref[...], preferred_element_type=jnp.float32)
        out_ref[d] = picked.astype(out_ref.dtype)


def short_attend(place, lengths, targets, query_blocks, pair_blocks, width, span, size):
    blocks = len(query_blocks)
    rows = blocks * query_blocks[0].shape[0]
    slots = lengths.shape[0]
    scores = 2 * rows * span * (width // size)
    smem = pl.BlockSpec(memory_space=pltpu.SMEM)
    vmem = pl.BlockSpec(memory_space=pltpu.VMEM)
    return pl.pallas_call(
        functools.partial(short_kernel, blocks=blocks, scale=LOG2_E / math.sqrt(size), size=size),
        out_shape=jax.ShapeDtypeStruct((slots, span, width), jnp.bfloat16),
        in_specs=[smem, smem, smem] + [vmem] * (2 * blocks),
        out_specs=vmem,
        scratch_shapes=[
            pltpu.VMEM((rows, width), jnp.bfloat16),
            pltpu.VMEM((rows, 2 * size), jnp.bfloat16),
            pltpu.VMEM((rows, width), jnp.bfloat16),
            pltpu.SMEM((slots,), jnp.int32),
            pltpu.SMEM((slots,), jnp.int32),
        ],
        compiler_params=pltpu.CompilerParams(vmem_limit_bytes=VMEM_LIMIT),
        cost_estimate=pl.CostEstimate(
            flops=16 * scores * size + 2 * slots * span * rows * width,
            bytes_accessed=2 * (rows * (width + 2 * size) + slots * span * width),
            transcendentals=scores,
        ),
        name="short_attend",
    )(place, lengths, targets, *query_blocks, *pair_blocks)


def swap_blocks(parts, axis):
    count = lax.axis_size(axis)
    own = lax.axis_index(axis)
    got = [lax.dynamic_index_in_dim(parts, own, 0, keepdims=False)]
    for k in range(1, count):
        sent = lax.dynamic_index_in_dim(parts, own ^ k, 0, keepdims=False)
        got.append(lax.ppermute(sent, axis, [(i, i ^ k) for i in range(count)]))
    return got


CHUNKS = ((0, 0, 2), (0, 2, 8), (1, 0, 8))


def on_device(long_queries, long_pairs, short_queries, short_pairs, doc_lengths, destinations):
    local_rows, heads, size = short_queries.shape
    kv_heads = short_pairs.shape[1]
    head_count, group_count = lax.axis_size("head"), lax.axis_size("grp")
    place = jnp.stack([lax.axis_index("grp"), lax.axis_index("head")]).astype(jnp.int32)
    span = 2 * local_rows * head_count // group_count
    own_heads, own_kv, share = heads // head_count, kv_heads // head_count, heads // kv_heads
    split_queries = short_queries.reshape(local_rows, head_count, own_heads * size)
    split_pairs = short_pairs.reshape(local_rows, head_count, own_kv * 2 * size)

    placed = []
    pair_blocks = {}
    for c, low, high in CHUNKS:
        if c >= own_kv:
            continue
        part = split_queries[:, :, (c * share + low) * size : (c * share + high) * size]
        if c not in pair_blocks:
            part = jnp.concatenate([part, split_pairs[:, :, c * 2 * size : (c + 1) * 2 * size]], axis=2)
        blocks = swap_blocks(jnp.swapaxes(part, 0, 1), "head")
        pair_blocks.setdefault(c, blocks)
        slots = short_attend(
            place, doc_lengths, destinations, blocks, pair_blocks[c], (high - low) * size, span, size
        )
        placed.append(lax.all_to_all(slots, "grp", split_axis=0, concat_axis=0, tiled=True))
    short_placed = jnp.concatenate(placed, axis=2).reshape(group_count * span, own_heads * size)

    all_pairs = lax.all_gather(long_pairs.reshape(local_rows, -1), "head", axis=0, tiled=True)
    first_row = (lax.axis_index("head") * local_rows).astype(jnp.int32).reshape(1)
    long_result = long_attend(long_queries.reshape(local_rows, -1), all_pairs, first_row, size)
    return (long_result, short_placed)


def solution(mesh):
    rows = P(("grp", "head"), None, None)
    return jax.shard_map(
        on_device,
        mesh=mesh,
        in_specs=(rows, rows, rows, rows, P(), P()),
        out_specs=(P(("grp", "head"), None), P("grp", "head")),
        check_vma=False,
    )
```

time: 281 us -> 169 us (0.60)
  waiting for transfers between devices: 152 us -> 77.2 us
  local copies, waits for them, and re-layouts: 59.1 us -> 25.4 us
  matrix products: 30.7 us -> 0 us
  Pallas kernels: 0 us -> 23.9 us
  between operations: 0.78 us -> 14.2 us
  starting transfers between devices: 29.8 us -> 23.6 us
  other arithmetic: 8.24 us -> 3.86 us
    all_to_all x7 -> x3, waiting for transfers between devices: 152 us -> 24.2 us  [on_device(): lax.all_to_all(slots, 'grp', split_axis=0, concat_axis=0, tiled=True)]
    ppermute x0 -> x9, waiting for transfers between devices: none -> 30.5 us  [swap_blocks(): got.append(lax.ppermute(sent, axis, [(i, i ^ k) for i in range(count)]))]
    pallas_call x0 -> x4, Pallas kernels: none -> 23.9 us  [the longest x3 14.8 us: short_attend(): pl.pallas_call(functools.partial(short_kernel, blocks=blocks, scale=LOG2_...]
    all_gather x0 -> x1, waiting for transfers between devices: none -> 22.5 us  [on_device(): lax.all_gather(long_pairs.reshape(local_rows, -1), 'head', axis=0, tiled=...]
    dot_general x3 -> x0, matrix products: 17.4 us -> none  [the longest x2 13.9 us: attend_rows(): jnp.einsum('hgqk,khd->qhgd', weights, value_part, preferred_element_type=...]
    gather x3 -> x0, local copies, waits for them, and re-layouts: 13.6 us -> none  [the longest x1 8.28 us: on_device(): slot_queries = group_queries[row_index]]
    all_to_all x7 -> x3, starting transfers between devices: 29.8 us -> 16.4 us  [on_device(): lax.all_to_all(slots, 'grp', split_axis=0, concat_axis=0, tiled=True)]
    sub x1 -> x0, matrix products: 13.3 us -> none  [attend_rows(): raised = jnp.exp(scores - row_max)]
  transfers between devices with their start and end apart: 7 -> 13, of which waited for: 6 -> 9; matrix products, arithmetic and copies ran while one was open for 24% -> 4% of each run, Pallas kernels for 0% -> 12%
where the time goes in v1:
time: 169 us; the launch traced here: 168 us
  waiting for transfers between devices  77.2 us (46%)
  local copies, waits for them, and re-layouts  25.4 us (15%)
  Pallas kernels  23.9 us (14%)
  starting transfers between devices  23.6 us (14%)
  between operations  14.2 us (8%)
  other arithmetic  3.86 us (2%)
    ppermute x9, waiting for transfers between devices, swap_blocks(): got.append(lax.ppermute(sent, axis, [(i, i ^ k) for i in range(count)]))  30.5 us
    all_to_all x3, waiting for transfers between devices, on_device(): lax.all_to_all(slots, 'grp', split_axis=0, concat_axis=0, tiled=True)  24.2 us
    all_gather x1, waiting for transfers between devices, on_device(): lax.all_gather(long_pairs.reshape(local_rows, -1), 'head', axis=0, tiled=...  22.5 us
    all_to_all x3, starting transfers between devices, on_device(): lax.all_to_all(slots, 'grp', split_axis=0, concat_axis=0, tiled=True)  16.4 us
    pallas_call x3, Pallas kernels, short_attend(): pl.pallas_call(functools.partial(short_kernel, blocks=blocks, scale=LOG2_...  14.8 us
    unnamed x22, local copies, waits for them, and re-layouts  11.4 us
    pallas_call x1, Pallas kernels, long_attend(): pl.pallas_call(functools.partial(long_kernel, scale=LOG2_E / math.sqrt(si...  9.18 us
    ppermute x9, starting transfers between devices, swap_blocks(): got.append(lax.ppermute(sent, axis, [(i, i ^ k) for i in range(count)]))  7.13 us
  transfers between devices with their start and end apart: 13, of which 9 were waited for; matrix products, arithmetic and copies ran while one was open for 4% of the time, Pallas kernels for 12%

profile of v1, /device:TPU:0, one launch (start us, length us, event | category | flops | bytes accessed | tf_op | source)
XLA Modules:
  0.0 168.1 jit_solution(4933702499067319305)
XLA Ops:
  7.2 2.5 %reshape.49 = bf16[128,4,2048]{2,1,0:T(4,128)(2,1)S(1)} reshape(bf16[128,64,128]{2,1,0:T(8,128)(2,1)} %param.8) | data formatting | bytes 4194304 | tf_op jit(solution)/shard_map/reshape | solution.py:154
  9.7 1.4 slice.23
  12.0 1.5 copy_dynamic-update-slice_fusion
  13.5 2.2 %reshape.50 = bf16[128,4,512]{2,1,0:T(4,128)(2,1)} reshape(bf16[128,8,256]{2,1,0:T(8,128)(2,1)} %param.9) | data formatting | bytes 1048576 | tf_op jit(solution)/shard_map/reshape | solution.py:155
  15.7 2.0 %fusion = (bf16[128,4,256]{2,1,0:T(4,128)(2,1)}, bf16[128,4,256]{2,1,0:T(4,128)(2,1)}) fusion(bf16[128,4,512]{2,1,0:T(4,128)(2,1)} %reshape.50), kind=kLoop, calls=%fused_computation.23 | loop fusion | bytes 1048576 | tf_op jit(solution)/shard_map/slice | solution.py:164
  17.7 1.7 copy_dynamic-update-slice_fusion.3
  19.4 1.8 %copy_dynamic-update-slice_fusion.1 = (bf16[128,4,1280]{2,0,1:T(8,128)(2,1)S(1)}, bf16[128,4,512]{2,0,1:T(8,128)(2,1)}) fusion(bf16[128,4,1280]{2,0,1:T(8,128)(2,1)S(1)} %copy_dynamic-update-slice_fusion, bf16[128,4,256]{2,1,0:T(4,128)(2,1)} %get-tuple-element.15, bf16[128,4,512]{2,0,1:T(8,128)(2,1)} %copy_dynamic-update-slice_fusion.3, ...), kind=kLoop, calls=%fused_computation.7 | loop fusion | bytes 1048576 | tf_op jit(solution)/shard_map/concatenate | solution.py:164
  22.3 1.1 dynamic-slice_bitcast_fusion.4
  23.9 2.6 %collective-permute-start.1 = (bf16[128,512]{1,0:T(8,128)(2,1)S(1)}, bf16[128,512]{1,0:T(8,128)(2,1)S(1)}, u32[]{:S(2)}, u32[]{:S(2)}) collective-permute-start(bf16[128,512]{1,0:T(8,128)(2,1)S(1)} %get-tuple-element.11), channel_id=1, source_target_pairs={{0,2},{1,3},{2,0},{3,1},{4,6},{5,7},{6,4},{7,5},{8,10},{9,11},{10,... | collective-permute-start | bytes 393224 | tf_op jit(solution)/shard_map/ppermute | solution.py:140
  26.6 4.2 %collective-permute-done.1.refs_2_.refs_6_ = bf16[128,512]{1,0:T(8,128)(2,1)S(1)} collective-permute-done((bf16[128,512]{1,0:T(8,128)(2,1)S(1)}, bf16[128,512]{1,0:T(8,128)(2,1)S(1)}, u32[]{:S(2)}, u32[]{:S(2)}) %collective-permute-start.1) | collective-permute-done | bytes 131104 | tf_op jit(solution)/shard_map/ppermute | solution.py:140
  30.8 2.3 %collective-permute-done.2.refs_3_.refs_7_ = bf16[128,512]{1,0:T(8,128)(2,1)S(1)} collective-permute-done((bf16[128,512]{1,0:T(8,128)(2,1)S(1)}, bf16[128,512]{1,0:T(8,128)(2,1)S(1)}, u32[]{:S(2)}, u32[]{:S(2)}) %collective-permute-start.2) | collective-permute-done | bytes 131104 | tf_op jit(solution)/shard_map/ppermute | solution.py:140
  33.1 3.0 %short_attend.3 = bf16[8,128,256]{2,1,0:T(8,128)(2,1)} custom-call(s32[2]{0:T(128)S(1)} %pad_add_fusion.place_ref, s32[8,8]{1,0:T(8,128)S(1)} %copy-done.1, s32[8,8]{1,0:T(8,128)S(1)} %copy-done.2, bf16[128,512]{1,0:T(8,128)(2,1)S(1)} %get-tuple-element.13.refs_0_.refs_4_, bf16[128,512]{1,0:T(8,128)(2,1)S(1)} %collective-permute-done.refs_1_.refs_5_, ...), custom_call_target="tpu_custom_call" | custom-call | flops 805306368 | bytes 1048576 | tf_op jit(solution)/shard_map/short_attend/pallas_call | solution.py:112
  36.2 5.9 %all-to-all-start = ((bf16[8,128,256]{2,1,0:T(8,128)(2,1)}), bf16[8,128,256]{2,1,0:T(8,128)(2,1)}, u32[]{:S(2)}, u32[]{:S(2)}) async-start(bf16[8,128,256]{2,1,0:T(8,128)(2,1)} %short_attend.3), calls=%async_computation | async-start | bytes 1048576 | tf_op jit(solution)/shard_map/all_to_all | solution.py:170
  42.4 1.6 constant_dynamic-slice_fusion
  44.2 1.6 collective-permute-start.4
  46.3 5.7 %collective-permute-done.4.refs_2_ = bf16[128,768]{1,0:T(8,128)(2,1)S(1)} collective-permute-done((bf16[128,768]{1,0:T(8,128)(2,1)S(1)}, bf16[128,768]{1,0:T(8,128)(2,1)S(1)}, u32[]{:S(2)}, u32[]{:S(2)}) %collective-permute-start.4) | collective-permute-done | bytes 196640 | tf_op jit(solution)/shard_map/ppermute | solution.py:140
  52.0 3.4 %collective-permute-done.5.refs_3_ = bf16[128,768]{1,0:T(8,128)(2,1)S(1)} collective-permute-done((bf16[128,768]{1,0:T(8,128)(2,1)S(1)}, bf16[128,768]{1,0:T(8,128)(2,1)S(1)}, u32[]{:S(2)}, u32[]{:S(2)}) %collective-permute-start.5) | collective-permute-done | bytes 196640 | tf_op jit(solution)/shard_map/ppermute | solution.py:140
  55.4 5.2 %short_attend.4 = bf16[8,128,768]{2,1,0:T(8,128)(2,1)} custom-call(s32[2]{0:T(128)S(1)} %pad_add_fusion.place_ref, s32[8,8]{1,0:T(8,128)S(1)} %copy-done.1, s32[8,8]{1,0:T(8,128)S(1)} %copy-done.2, bf16[128,768]{1,0:T(8,128)(2,1)S(1)} %bitcast.39, bf16[128,768]{1,0:T(8,128)(2,1)S(1)} %collective-permute-done.3.refs_1_, ...), custom_call_target="tpu_custom_call" | custom-call | flops 2415919104 | bytes 2621440 | tf_op jit(solution)/shard_map/short_attend/pallas_call | solution.py:112
  60.7 6.1 %all-to-all-start.1 = ((bf16[8,128,768]{2,1,0:T(8,128)(2,1)}), bf16[8,128,768]{2,1,0:T(8,128)(2,1)S(1)}, u32[]{:S(2)}, u32[]{:S(2)}) async-start(bf16[8,128,768]{2,1,0:T(8,128)(2,1)} %short_attend.4), calls=%async_computation.1 | async-start | bytes 3145728 | tf_op jit(solution)/shard_map/all_to_all | solution.py:170
  67.0 1.6 collective-permute-start.7
  68.8 8.7 %collective-permute-done.7.refs_2_.refs_6_ = bf16[128,1280]{1,0:T(8,128)(2,1)S(1)} collective-permute-done((bf16[128,1280]{1,0:T(8,128)(2,1)S(1)}, bf16[128,1280]{1,0:T(8,128)(2,1)S(1)}, u32[]{:S(2)}, u32[]{:S(2)}) %collective-permute-start.7) | collective-permute-done | bytes 327712 | tf_op jit(solution)/shard_map/ppermute | solution.py:140
  77.5 6.1 %collective-permute-done.8.refs_3_.refs_7_ = bf16[128,1280]{1,0:T(8,128)(2,1)S(1)} collective-permute-done((bf16[128,1280]{1,0:T(8,128)(2,1)S(1)}, bf16[128,1280]{1,0:T(8,128)(2,1)S(1)}, u32[]{:S(2)}, u32[]{:S(2)}) %collective-permute-start.8) | collective-permute-done | bytes 327712 | tf_op jit(solution)/shard_map/ppermute | solution.py:140
  83.7 6.5 %short_attend.5 = bf16[8,128,1024]{2,1,0:T(8,128)(2,1)} custom-call(s32[2]{0:T(128)S(1)} %pad_add_fusion.place_ref, s32[8,8]{1,0:T(8,128)S(1)} %copy-done.1, s32[8,8]{1,0:T(8,128)S(1)} %copy-done.2, bf16[128,1280]{1,0:T(8,128)(2,1)S(1)} %get-tuple-element.5.refs_0_.refs_4_, bf16[128,1280]{1,0:T(8,128)(2,1)S(1)} %collective-permute-done.6.refs_1_.refs_5_, ...), custom_call_target="tpu_custom_call" | custom-call | flops 3221225472 | bytes 3407872 | tf_op jit(solution)/shard_map/short_attend/pallas_call | solution.py:112
  90.1 14.0 %all-to-all-done.1 = bf16[8,128,768]{2,1,0:T(8,128)(2,1)S(1)} async-done(((bf16[8,128,768]{2,1,0:T(8,128)(2,1)}), bf16[8,128,768]{2,1,0:T(8,128)(2,1)S(1)}, u32[]{:S(2)}, u32[]{:S(2)}) %all-to-all-start.1) | async-done | bytes 1572896 | tf_op jit(solution)/shard_map/all_to_all | solution.py:170
  104.2 1.2 copy-done.3
  105.3 4.3 %all-to-all-start.2 = ((bf16[8,128,1024]{2,1,0:T(8,128)(2,1)}), bf16[8,128,1024]{2,1,0:T(8,128)(2,1)}, u32[]{:S(2)}, u32[]{:S(2)}) async-start(bf16[8,128,1024]{2,1,0:T(8,128)(2,1)} %short_attend.5), calls=%async_computation.2 | async-start | bytes 4194304 | tf_op jit(solution)/shard_map/all_to_all | solution.py:170
  110.7 3.4 %copy.33 = bf16[16,8,64,128]{3,1,2,0:T(8,128)(2,1)S(1)} copy(bf16[16,8,64,128]{3,2,1,0:T(8,128)(2,1)} %bitcast.41) | data formatting | bytes 4194304
  114.1 22.5 %all-gather.2.cloned.1.call-done.kv_ref = bf16[512,2048]{1,0:T(8,128)(2,1)} async-done(((bf16[128,2048]{1,0:T(8,128)(2,1)}), bf16[512,2048]{1,0:T(8,128)(2,1)}) %all-gather.2.cloned.1.call-update) | async-done | bytes 2097168 | tf_op jit(solution)/shard_map/all_gather | solution.py:173
  136.6 1.6 copy-done
  138.2 9.2 %long_attend.1 = bf16[128,8192]{1,0:T(8,128)(2,1)} custom-call(s32[1]{0:T(128)} %bitcast.first_ref, bf16[128,8192]{1,0:T(8,128)(2,1)S(1)} %bitcast.38, bf16[512,2048]{1,0:T(8,128)(2,1)S(1)} %copy-done), custom_call_target="tpu_custom_call" | custom-call | flops 2147483648 | bytes 6291456 | tf_op jit(solution)/shard_map/long_attend/pallas_call | solution.py:47
  147.4 10.1 %all-to-all-done.2 = bf16[8,128,1024]{2,1,0:T(8,128)(2,1)} async-done(((bf16[8,128,1024]{2,1,0:T(8,128)(2,1)}), bf16[8,128,1024]{2,1,0:T(8,128)(2,1)}, u32[]{:S(2)}, u32[]{:S(2)}) %all-to-all-start.2) | async-done | bytes 2097184 | tf_op jit(solution)/shard_map/all_to_all | solution.py:170
  157.5 3.8 %pad_maximum_fusion = bf16[8,128,2048]{2,1,0:T(8,128)(2,1)} fusion(bf16[8,128,1024]{2,1,0:T(8,128)(2,1)} %all-to-all-done.2, bf16[8,128,768]{2,1,0:T(8,128)(2,1)} %copy-done.3, bf16[8,128,256]{2,1,0:T(8,128)(2,1)} %all-to-all-done), kind=kLoop, calls=%fused_computation | loop fusion | flops 12582912 | bytes 8388608 | tf_op jit(solution)/shard_map/concatenate | solution.py:171
  (33 shorter events, 5.0 us)
Async XLA Ops:
  15.7 17.4 %copy-start.1 = (s32[8,8]{1,0:T(8,128)S(1)}, s32[8,8]{1,0:T(8,128)}, u32[]{:S(2)}) copy-start(s32[8,8]{1,0:T(8,128)} %lengths_ref.5) | copy-start | bytes 772
  15.7 17.4 %copy-start.2 = (s32[8,8]{1,0:T(8,128)S(1)}, s32[8,8]{1,0:T(8,128)}, u32[]{:S(2)}) copy-start(s32[8,8]{1,0:T(8,128)} %targets_ref.5) | copy-start | bytes 772
  21.2 1.1 copy-start.4
  23.4 3.2 %collective-permute-start = (bf16[128,512]{1,0:T(8,128)(2,1)S(1)}, bf16[128,512]{1,0:T(8,128)(2,1)S(1)}, u32[]{:S(2)}, u32[]{:S(2)}) collective-permute-start(bf16[128,512]{1,0:T(8,128)(2,1)S(1)} %get-tuple-element.12), channel_id=1, source_target_pairs={{0,1},{1,0},{2,3},{3,2},{4,5},{5,4},{6,7},{7,6},{8,9},{9,8},{10,11... | collective-permute-start | bytes 393224 | tf_op jit(solution)/shard_map/ppermute | solution.py:140
  23.9 6.9 %collective-permute-start.1 = (bf16[128,512]{1,0:T(8,128)(2,1)S(1)}, bf16[128,512]{1,0:T(8,128)(2,1)S(1)}, u32[]{:S(2)}, u32[]{:S(2)}) collective-permute-start(bf16[128,512]{1,0:T(8,128)(2,1)S(1)} %get-tuple-element.11), channel_id=1, source_target_pairs={{0,2},{1,3},{2,0},{3,1},{4,6},{5,7},{6,4},{7,5},{8,10},{9,11},{10,... | collective-permute-start | bytes 393224 | tf_op jit(solution)/shard_map/ppermute | solution.py:140
  26.5 6.6 %collective-permute-start.2 = (bf16[128,512]{1,0:T(8,128)(2,1)S(1)}, bf16[128,512]{1,0:T(8,128)(2,1)S(1)}, u32[]{:S(2)}, u32[]{:S(2)}) collective-permute-start(bf16[128,512]{1,0:T(8,128)(2,1)S(1)} %get-tuple-element.10), channel_id=1, source_target_pairs={{0,3},{1,2},{2,1},{3,0},{4,7},{5,6},{6,5},{7,4},{8,11},{9,10},{10,... | collective-permute-start | bytes 393224 | tf_op jit(solution)/shard_map/ppermute | solution.py:140
  36.2 24.5 %all-to-all-start = ((bf16[8,128,256]{2,1,0:T(8,128)(2,1)}), bf16[8,128,256]{2,1,0:T(8,128)(2,1)}, u32[]{:S(2)}, u32[]{:S(2)}) async-start(bf16[8,128,256]{2,1,0:T(8,128)(2,1)} %short_attend.3), calls=%async_computation | async-start | bytes 1048576 | tf_op jit(solution)/shard_map/all_to_all | solution.py:170
  44.1 2.1 %collective-permute-start.3 = (bf16[128,768]{1,0:T(8,128)(2,1)S(1)}, bf16[128,768]{1,0:T(8,128)(2,1)S(1)}, u32[]{:S(2)}, u32[]{:S(2)}) collective-permute-start(bf16[128,768]{1,0:T(8,128)(2,1)S(1)} %bitcast.44), channel_id=1, source_target_pairs={{0,1},{1,0},{2,3},{3,2},{4,5},{5,4},{6,7},{7,6},{8,9},{9,8},{10,11... | collective-permute-start | bytes 589832 | tf_op jit(solution)/shard_map/ppermute | solution.py:140
  44.2 7.8 %collective-permute-start.4 = (bf16[128,768]{1,0:T(8,128)(2,1)S(1)}, bf16[128,768]{1,0:T(8,128)(2,1)S(1)}, u32[]{:S(2)}, u32[]{:S(2)}) collective-permute-start(bf16[128,768]{1,0:T(8,128)(2,1)S(1)} %bitcast.45), channel_id=1, source_target_pairs={{0,2},{1,3},{2,0},{3,1},{4,6},{5,7},{6,4},{7,5},{8,10},{9,11},{10,... | collective-permute-start | bytes 589832 | tf_op jit(solution)/shard_map/ppermute | solution.py:140
  45.8 9.6 %collective-permute-start.5 = (bf16[128,768]{1,0:T(8,128)(2,1)S(1)}, bf16[128,768]{1,0:T(8,128)(2,1)S(1)}, u32[]{:S(2)}, u32[]{:S(2)}) collective-permute-start(bf16[128,768]{1,0:T(8,128)(2,1)S(1)} %bitcast.46), channel_id=1, source_target_pairs={{0,3},{1,2},{2,1},{3,0},{4,7},{5,6},{6,5},{7,4},{8,11},{9,10},{10,... | collective-permute-start | bytes 589832 | tf_op jit(solution)/shard_map/ppermute | solution.py:140
  60.6 6.1 %copy-start.5 = (bf16[128,4,1280]{2,0,1:T(8,128)(2,1)S(1)}, bf16[128,4,1280]{2,0,1:T(8,128)(2,1)}, u32[]{:S(2)}) copy-start(bf16[128,4,1280]{2,0,1:T(8,128)(2,1)} %copy-done.4) | copy-start | bytes 3932164
  60.7 43.5 %all-to-all-start.1 = ((bf16[8,128,768]{2,1,0:T(8,128)(2,1)}), bf16[8,128,768]{2,1,0:T(8,128)(2,1)S(1)}, u32[]{:S(2)}, u32[]{:S(2)}) async-start(bf16[8,128,768]{2,1,0:T(8,128)(2,1)} %short_attend.4), calls=%async_computation.1 | async-start | bytes 3145728 | tf_op jit(solution)/shard_map/all_to_all | solution.py:170
  66.9 1.9 %collective-permute-start.6 = (bf16[128,1280]{1,0:T(8,128)(2,1)S(1)}, bf16[128,1280]{1,0:T(8,128)(2,1)S(1)}, u32[]{:S(2)}, u32[]{:S(2)}) collective-permute-start(bf16[128,1280]{1,0:T(8,128)(2,1)S(1)} %get-tuple-element.4), channel_id=1, source_target_pairs={{0,1},{1,0},{2,3},{3,2},{4,5},{5,4},{6,7},{7,6},{8,9},{9,8},{10,11... | collective-permute-start | bytes 983048 | tf_op jit(solution)/shard_map/ppermute | solution.py:140
  67.0 10.6 %collective-permute-start.7 = (bf16[128,1280]{1,0:T(8,128)(2,1)S(1)}, bf16[128,1280]{1,0:T(8,128)(2,1)S(1)}, u32[]{:S(2)}, u32[]{:S(2)}) collective-permute-start(bf16[128,1280]{1,0:T(8,128)(2,1)S(1)} %get-tuple-element.3), channel_id=1, source_target_pairs={{0,2},{1,3},{2,0},{3,1},{4,6},{5,7},{6,4},{7,5},{8,10},{9,11},{10,... | collective-permute-start | bytes 983048 | tf_op jit(solution)/shard_map/ppermute | solution.py:140
  68.5 15.1 %collective-permute-start.8 = (bf16[128,1280]{1,0:T(8,128)(2,1)S(1)}, bf16[128,1280]{1,0:T(8,128)(2,1)S(1)}, u32[]{:S(2)}, u32[]{:S(2)}) collective-permute-start(bf16[128,1280]{1,0:T(8,128)(2,1)S(1)} %get-tuple-element.2), channel_id=1, source_target_pairs={{0,3},{1,2},{2,1},{3,0},{4,7},{5,6},{6,5},{7,4},{8,11},{9,10},{10,... | collective-permute-start | bytes 983048 | tf_op jit(solution)/shard_map/ppermute | solution.py:140
  90.1 19.6 %copy-start.6 = (bf16[128,8,256]{2,1,0:T(8,128)(2,1)S(1)}, bf16[128,8,256]{2,1,0:T(8,128)(2,1)}, u32[]{:S(2)}) copy-start(bf16[128,8,256]{2,1,0:T(8,128)(2,1)} %param.7) | copy-start | bytes 1572868
  104.2 1.2 copy-start.3
  105.3 52.2 %all-to-all-start.2 = ((bf16[8,128,1024]{2,1,0:T(8,128)(2,1)}), bf16[8,128,1024]{2,1,0:T(8,128)(2,1)}, u32[]{:S(2)}, u32[]{:S(2)}) async-start(bf16[8,128,1024]{2,1,0:T(8,128)(2,1)} %short_attend.5), calls=%async_computation.2 | async-start | bytes 4194304 | tf_op jit(solution)/shard_map/all_to_all | solution.py:170
  109.7 26.9 %all-gather.2.cloned.1.call-start = ((), (), s32[]{:S(2)}) async-start(), calls=%async_computation.3 | async-start | bytes 2621440 | tf_op jit(solution)/shard_map/all_gather | solution.py:173
  136.6 1.6 copy-start
Sparse Core Ops, SparseCore 0:
  112.7 23.8 all-gather.1

commit v2 on v1

v2 whole, which is shorter than its diff:
```python
import functools
import math

import jax
import jax.numpy as jnp
from jax import lax
from jax.experimental import pallas as pl
from jax.experimental.pallas import tpu as pltpu
from jax.sharding import PartitionSpec as P

LOG2_E = 1.4426950408889634
VMEM_LIMIT = 24 * 1024 * 1024


def softmax_mix(queries, keys, values_and_ones, allowed, scale):
    scores = lax.dot_general(queries, keys, (((1,), (1,)), ((), ())), preferred_element_type=jnp.float32)
    scores = jnp.where(allowed, scores, -1e30)
    row_max = jnp.max(scores, axis=-1, keepdims=True)
    raised = jnp.exp2((scores - row_max) * scale).astype(jnp.bfloat16)
    both = jnp.dot(raised, values_and_ones, preferred_element_type=jnp.float32)
    size = keys.shape[1]
    return both[:, :size] / both[:, size:]


def with_ones(values):
    return jnp.concatenate([values, jnp.ones_like(values)], axis=1)


def split_heads(scratch_ref, block):
    tokens, heads, size = block.shape
    scratch_ref[...] = block.astype(jnp.float32).reshape(tokens * heads, size)


def long_kernel(own_ref, q_ref, *refs, order, scale):
    kv_refs, (out_ref, scratch_ref) = refs[:-2], refs[-2:]
    rows, heads, size = q_ref.shape
    kv_here = kv_refs[0].shape[0]
    share = heads // kv_here
    own = own_ref[0]
    split_heads(scratch_ref, q_ref[...])
    row = lax.broadcasted_iota(jnp.int32, (rows, rows), 0)
    column = lax.broadcasted_iota(jnp.int32, (rows, rows), 1)
    allowed = jnp.concatenate(
        [column + ((own ^ k) - own) * rows <= row for k in order], axis=1
    )
    for c in range(kv_here):
        keys = jnp.concatenate([ref[c, :, :size] for ref in kv_refs], axis=0)
        values = with_ones(jnp.concatenate([ref[c, :, size:] for ref in kv_refs], axis=0))
        for h in range(c * share, (c + 1) * share):
            queries = scratch_ref[pl.ds(h, rows, stride=heads), :].astype(jnp.bfloat16)
            mixed = softmax_mix(queries, keys, values, allowed, scale)
            out_ref[:, h * size : (h + 1) * size] = mixed.astype(out_ref.dtype)


def long_attend(own, queries, pair_blocks, order):
    rows, heads, size = queries.shape
    kv_heads = pair_blocks[0].shape[0]
    kv_here = 2
    here = heads * kv_here // kv_heads
    scores = rows * rows * len(pair_blocks) * heads
    return pl.pallas_call(
        functools.partial(long_kernel, order=order, scale=LOG2_E / math.sqrt(size)),
        out_shape=jax.ShapeDtypeStruct((rows, heads * size), jnp.bfloat16),
        grid=(kv_heads // kv_here,),
        in_specs=[
            pl.BlockSpec(memory_space=pltpu.SMEM),
            pl.BlockSpec((rows, here, size), lambda c: (0, c, 0)),
        ]
        + [pl.BlockSpec((kv_here, rows, 2 * size), lambda c: (c, 0, 0))] * len(pair_blocks),
        out_specs=pl.BlockSpec((rows, here * size), lambda c: (0, c)),
        scratch_shapes=[pltpu.VMEM((rows * here, size), jnp.float32)],
        compiler_params=pltpu.CompilerParams(vmem_limit_bytes=VMEM_LIMIT),
        cost_estimate=pl.CostEstimate(flops=0, bytes_accessed=0, transcendentals=0),
        name="long_attend",
    )(own, queries, *pair_blocks)


def long_part(long_queries, long_pairs):
    own = lax.axis_index("head").astype(jnp.int32).reshape(1)
    return long_attend(own, long_queries, *share_blocks(jnp.swapaxes(long_pairs, 0, 1), "head"))


def share_blocks(block, axis):
    count = lax.axis_size(axis)
    blocks, order = [block], [0]
    step = count // 2
    while step:
        pairs = [(i, i ^ step) for i in range(count)]
        blocks += [lax.ppermute(b, axis, pairs) for b in blocks]
        order += [k ^ step for k in order]
        step //= 2
    return blocks, order


HEAD_CHUNKS = ((0, 6), (6, 16))


def prepare_kernel(own_ref, q_ref, kv_ref, *refs, count, low, high, kv_low, kv_high):
    out_refs, (q_scratch, kv_scratch) = refs[:-2], refs[-2:]
    tokens, heads, size = q_ref.shape
    kv_heads = kv_ref.shape[1]
    here, kv_here = heads // count, kv_heads // count
    if kv_low < kv_high:
        for part in range(2):
            split_heads(kv_scratch.at[part], kv_ref[:, :, part * size : (part + 1) * size])
    for k, out_ref in enumerate(out_refs):
        to = own_ref[0] ^ k
        split_heads(q_scratch, q_ref[:, pl.ds(pl.multiple_of(to * here, here), here), :])
        at = 0
        for h in range(low, high):
            picked = q_scratch[pl.ds(h, tokens, stride=here), :]
            out_ref[:, at : at + size] = picked.astype(out_ref.dtype)
            at += size
        for c in range(kv_low, kv_high):
            for part in range(2):
                picked = kv_scratch[part, pl.ds(to * kv_here + c, tokens, stride=kv_heads), :]
                out_ref[:, at : at + size] = picked.astype(out_ref.dtype)
                at += size


def prepare(own, queries, pairs, count, low, high, kv_low, kv_high):
    tokens, heads, size = queries.shape
    kv_heads = pairs.shape[1]
    width = (high - low + 2 * (kv_high - kv_low)) * size
    vmem = pl.BlockSpec(memory_space=pltpu.VMEM)
    return pl.pallas_call(
        functools.partial(prepare_kernel, count=count, low=low, high=high, kv_low=kv_low, kv_high=kv_high),
        out_shape=[jax.ShapeDtypeStruct((tokens, width), jnp.bfloat16)] * count,
        in_specs=[pl.BlockSpec(memory_space=pltpu.SMEM), vmem, vmem],
        out_specs=[vmem] * count,
        scratch_shapes=[
            pltpu.VMEM((tokens * heads // count, size), jnp.float32),
            pltpu.VMEM((2, tokens * kv_heads, size), jnp.float32),
        ],
        compiler_params=pltpu.CompilerParams(vmem_limit_bytes=VMEM_LIMIT),
        cost_estimate=pl.CostEstimate(flops=0, bytes_accessed=0, transcendentals=0),
        name="prepare",
    )(own, queries, pairs)


def slots_kernel(place_ref, lengths_ref, targets_ref, *refs, blocks, parts, scale):
    sources, (out_ref, q_ref, kv_ref, mixed_ref, start_ref, length_ref) = refs[:-6], refs[-6:]
    slots, span, width = out_ref.shape
    rows = q_ref.shape[0]
    size = kv_ref.shape[2] // 2
    block_rows = rows // blocks
    group, own = place_ref[0], place_ref[1]
    for k in range(blocks):
        at = pl.ds(pl.multiple_of((own ^ k) * block_rows, block_rows), block_rows)
        q_ref[at, :] = sources[k][:, :width]
        for c, (home, column, _, _) in enumerate(parts):
            kv_ref[c, at, :] = sources[home * blocks + k][:, column : column + 2 * size]
    row = lax.broadcasted_iota(jnp.int32, (rows, 1), 0)
    begin = jnp.zeros((rows, 1), jnp.int32)
    start = jnp.int32(0)
    for j in range(slots):
        slot, length = targets_ref[group, j], lengths_ref[group, j]
        start_ref[slot] = start
        length_ref[slot] = length
        begin = jnp.where(row >= start, start, begin)
        start = start + length
    for first in range(0, rows, span):
        low = max(0, first - span)
        here = slice(first, first + span)
        window = slice(low, first + span)
        key_row = low + lax.broadcasted_iota(jnp.int32, (span, first + span - low), 1)
        allowed = (key_row >= begin[here]) & (key_row <= row[here])
        for c, (_, _, head_low, head_high) in enumerate(parts):
            keys, values = kv_ref[c, window, :size], with_ones(kv_ref[c, window, size:])
            for h in range(head_low, head_high):
                columns = slice(h * size, (h + 1) * size)
                mixed = softmax_mix(q_ref[here, columns], keys, values, allowed, scale)
                mixed_ref[here, columns] = mixed.astype(mixed_ref.dtype)
    place = lax.broadcasted_iota(jnp.int32, (span, rows), 0)
    source = lax.broadcasted_iota(jnp.int32, (span, rows), 1)
    for d in range(slots):
        chosen = (source == place + start_ref[d]) & (place < length_ref[d])
        picked = jnp.dot(chosen.astype(jnp.bfloat16), mixed_ref[...], preferred_element_type=jnp.float32)
        out_ref[d] = picked.astype(out_ref.dtype)


def slots_attend(place, lengths, targets, sources, parts, blocks, width, span, size):
    rows = blocks * sources[0].shape[0]
    slots = lengths.shape[0]
    smem = pl.BlockSpec(memory_space=pltpu.SMEM)
    vmem = pl.BlockSpec(memory_space=pltpu.VMEM)
    return pl.pallas_call(
        functools.partial(slots_kernel, blocks=blocks, parts=parts, scale=LOG2_E / math.sqrt(size)),
        out_shape=jax.ShapeDtypeStruct((slots, span, width), jnp.bfloat16),
        in_specs=[smem, smem, smem] + [vmem] * len(sources),
        out_specs=vmem,
        scratch_shapes=[
            pltpu.VMEM((rows, width), jnp.bfloat16),
            pltpu.VMEM((len(parts), rows, 2 * size), jnp.bfloat16),
            pltpu.VMEM((rows, width), jnp.bfloat16),
            pltpu.SMEM((slots,), jnp.int32),
            pltpu.SMEM((slots,), jnp.int32),
        ],
        compiler_params=pltpu.CompilerParams(vmem_limit_bytes=VMEM_LIMIT),
        cost_estimate=pl.CostEstimate(flops=0, bytes_accessed=0, transcendentals=0),
        name="slots_attend",
    )(place, lengths, targets, *sources)


def lay_kernel(*refs, lows):
    pieces, (out_ref, sems) = refs[: len(lows)], refs[-2:]
    copies = []
    for i, (ref, low) in enumerate(zip(pieces, lows)):
        to = out_ref.at[:, :, low : low + ref.shape[2]]
        copies.append(pltpu.make_async_copy(ref, to, sems.at[i]))
        copies[-1].start()
    for copy in copies:
        copy.wait()


def lay(pieces, lows, columns, whole=None):
    anywhere = pl.BlockSpec(memory_space=pl.ANY)
    operands = pieces + ([] if whole is None else [whole])
    slots, span, _ = pieces[0].shape
    return pl.pallas_call(
        functools.partial(lay_kernel, lows=lows),
        out_shape=jax.ShapeDtypeStruct((slots, span, columns), jnp.bfloat16),
        in_specs=[anywhere] * len(operands),
        out_specs=anywhere,
        input_output_aliases={} if whole is None else {len(operands) - 1: 0},
        scratch_shapes=[pltpu.SemaphoreType.DMA((len(pieces),))],
        compiler_params=pltpu.CompilerParams(vmem_limit_bytes=VMEM_LIMIT),
        cost_estimate=pl.CostEstimate(flops=0, bytes_accessed=0, transcendentals=0),
        name="lay",
    )(*operands)


def after(value, *earlier):
    return lax.optimization_barrier((value, earlier))[0]


def on_device(long_queries, long_pairs, short_queries, short_pairs, doc_lengths, destinations):
    local_rows, heads, size = short_queries.shape
    kv_heads = short_pairs.shape[1]
    head_count, group_count = lax.axis_size("head"), lax.axis_size("grp")
    own = lax.axis_index("head").astype(jnp.int32).reshape(1)
    place = jnp.stack([lax.axis_index("grp"), lax.axis_index("head")]).astype(jnp.int32)
    span = 2 * local_rows * head_count // group_count
    own_heads, own_kv, share = heads // head_count, kv_heads // head_count, heads // kv_heads
    columns = own_heads * size
    chunks = [(low * own_heads // 16, high * own_heads // 16) for low, high in HEAD_CHUNKS]

    sent, homes = [], {}
    for i, (low, high) in enumerate(chunks):
        new = [c for c in range(own_kv) if c not in homes and c * share < high and low < (c + 1) * share]
        for j, c in enumerate(new):
            homes[c] = (i, (high - low + 2 * j) * size)
        kv_low, kv_high = (new[0], new[-1] + 1) if new else (0, 0)
        sent.append(prepare(own, short_queries, short_pairs, head_count, low, high, kv_low, kv_high))

    def swap(blocks):
        moved = [blocks[0]]
        for k in range(1, head_count):
            moved.append(lax.ppermute(blocks[k], "head", [(i, i ^ k) for i in range(head_count)]))
        return moved

    pairs_by_head = jnp.swapaxes(long_pairs, 0, 1)
    got, slots, whole = [], [], None
    for i, (low, high) in enumerate(chunks):
        if i:
            sent[i] = after(sent[i], got[i - 1][1:])
        got.append(swap(sent[i]))
        if i == 0:
            got[0] = after(got[0], sent[1:], pairs_by_head)
        else:
            got[i] = after(got[i], slots[i - 1])
        touched = [c for c in range(own_kv) if c * share < high and low < (c + 1) * share]
        order = [i] + sorted({homes[c][0] for c in touched} - {i})
        parts = [
            (order.index(homes[c][0]), homes[c][1], max(low, c * share) - low, min(high, (c + 1) * share) - low)
            for c in touched
        ]
        sources = [block for j in order for block in got[j]]
        slots.append(
            slots_attend(
                place, doc_lengths, destinations, sources, parts, head_count, (high - low) * size, span, size
            )
        )
    pairs_by_head = after(pairs_by_head, got[-1])
    shared, order = share_blocks(pairs_by_head, "head")
    long_queries = after(long_queries, slots[-1])
    long_result = long_attend(own, long_queries, shared, order)
    for i, (low, high) in enumerate(chunks):
        moved = lax.all_to_all(slots[i], "grp", split_axis=0, concat_axis=0, tiled=True)
        if i == len(chunks) - 1:
            moved = after(moved, long_result)
        whole = lay([moved], [low * size], columns, whole)
    return long_result, whole.reshape(group_count * span, columns)


def solution(mesh):
    rows = P(("grp", "head"), None, None)
    return jax.shard_map(
        on_device,
        mesh=mesh,
        in_specs=(rows, rows, rows, rows, P(), P()),
        out_specs=(P(("grp", "head"), None), P("grp", "head")),
        check_vma=False,
    )
```

time: 169 us -> 135 us (0.80)
  local copies, waits for them, and re-layouts: 25.4 us -> 7.69 us
  between operations: 14.2 us -> 0.73 us
  starting transfers between devices: 23.6 us -> 16.1 us
  waiting for transfers between devices: 77.2 us -> 83.5 us
  other arithmetic: 3.86 us -> 0.08 us
  Pallas kernels: 23.9 us -> 26 us
    all_gather x1 -> x0, waiting for transfers between devices: 22.5 us -> none  [on_device(): lax.all_gather(long_pairs.reshape(local_rows, -1), 'head', axis=0, tiled=...]
    all_to_all x3 -> x2, waiting for transfers between devices: 24.2 us -> 43.3 us  [on_device(): lax.all_to_all(slots[i], 'grp', split_axis=0, concat_axis=0, tiled=True)]
    ppermute x9, waiting for transfers between devices: 30.5 us -> 40.2 us  [the longest x6 26.2 us: swap(): lax.ppermute(blocks[k], 'head', [(i, i ^ k) for i in range(head_count)])]
    all_to_all x3 -> x2, starting transfers between devices: 16.4 us -> 9.55 us  [on_device(): lax.all_to_all(slots[i], 'grp', split_axis=0, concat_axis=0, tiled=True)]
    reshape x2 -> x0, local copies, waits for them, and re-layouts: 4.71 us -> none  [the longest x1 2.54 us: on_device(): short_queries.reshape(local_rows, head_count, own_heads * size)]
    slice x4 -> x0, local copies, waits for them, and re-layouts: 4.67 us -> none  [the longest x3 2.64 us: on_device(): split_queries[:, :, (c * share + low) * size:(c * share + high) * size]]
    concatenate x1 -> x0, other arithmetic: 3.78 us -> none  [on_device(): jnp.concatenate(placed, axis=2)]
    unnamed x22 -> x23, local copies, waits for them, and re-layouts: 11.4 us -> 7.69 us
  transfers between devices with their start and end apart: 13 -> 11, of which waited for: 9 -> 9; matrix products, arithmetic and copies ran while one was open for 4% -> 0% of each run, Pallas kernels for 12% -> 14%
where the time goes in v2:
time: 135 us; the launch traced here: 134 us
  waiting for transfers between devices  83.5 us (62%)
  Pallas kernels  26 us (19%)
  starting transfers between devices  16.1 us (12%)
  local copies, waits for them, and re-layouts  7.69 us (6%)
    all_to_all x2, waiting for transfers between devices, on_device(): lax.all_to_all(slots[i], 'grp', split_axis=0, concat_axis=0, tiled=True)  43.3 us
    ppermute x6, waiting for transfers between devices, swap(): lax.ppermute(blocks[k], 'head', [(i, i ^ k) for i in range(head_count)])  26.2 us
    ppermute x3, waiting for transfers between devices, share_blocks(): blocks += [lax.ppermute(b, axis, pairs) for b in blocks]  14 us
    pallas_call x2, Pallas kernels, slots_attend(): pl.pallas_call(functools.partial(slots_kernel, blocks=blocks, parts=parts...  12.8 us
    all_to_all x2, starting transfers between devices, on_device(): lax.all_to_all(slots[i], 'grp', split_axis=0, concat_axis=0, tiled=True)  9.55 us
    pallas_call x1, Pallas kernels, long_attend(): pl.pallas_call(functools.partial(long_kernel, order=order, scale=LOG2_E /...  8.22 us
    unnamed x23, local copies, waits for them, and re-layouts  7.69 us
    ppermute x6, starting transfers between devices, swap(): lax.ppermute(blocks[k], 'head', [(i, i ^ k) for i in range(head_count)])  5.01 us
  transfers between devices with their start and end apart: 11, of which 9 were waited for; matrix products, arithmetic and copies ran while one was open for 0% of the time, Pallas kernels for 14%

profile of v2, /device:TPU:0, one launch (start us, length us, event | category | flops | bytes accessed | tf_op | source)
XLA Modules:
  0.0 134.2 jit_solution(9508607299071628964)
XLA Ops:
  0.6 1.6 %copy-done = bf16[128,64,128]{2,1,0:T(8,128)(2,1)S(1)} copy-done((bf16[128,64,128]{2,1,0:T(8,128)(2,1)S(1)}, bf16[128,64,128]{2,1,0:T(8,128)(2,1)}, u32[]{:S(2)}) %copy-start) | copy-done | bytes 2097176
  2.2 1.0 copy-done.4
  3.3 1.0 prepare.3
  4.3 0.5 collective-permute-start
  4.8 2.6 %collective-permute-start.1 = (bf16[128,1024]{1,0:T(8,128)(2,1)S(1)}, bf16[128,1024]{1,0:T(8,128)(2,1)S(1)}, u32[]{:S(2)}, u32[]{:S(2)}) collective-permute-start(bf16[128,1024]{1,0:T(8,128)(2,1)S(1)} %get-tuple-element.31), channel_id=1, source_target_pairs={{0,2},{1,3},{2,0},{3,1},{4,6},{5,7},{6,4},{7,5},{8,10},{9,11},{10,... | collective-permute-start | bytes 786440 | tf_op jit(solution)/shard_map/ppermute | solution.py:259
  7.4 1.4 %prepare.2 = (bf16[128,1536]{1,0:T(8,128)(2,1)S(1)}, bf16[128,1536]{1,0:T(8,128)(2,1)S(1)}, bf16[128,1536]{1,0:T(8,128)(2,1)S(1)}, bf16[128,1536]{1,0:T(8,128)(2,1)S(1)}) custom-call(s32[1]{0:T(128)} %bitcast.own_ref, bf16[128,64,128]{2,1,0:T(8,128)(2,1)S(1)} %copy-done, bf16[128,8,256]{2,1,0:T(8,128)(2,1)S(1)} %copy-done.4), custom_call_target="tpu_custom_call" | custom-call | tf_op jit(solution)/shard_map/prepare/pallas_call | solution.py:126
  8.8 0.7 copy-done.7
  9.5 0.7 copy-done.8
  10.3 0.7 copy-done.9
  11.0 0.1 copy.11
  11.1 0.1 pad_add_fusion.place_ref
  11.2 3.3 %collective-permute-done.1.refs_2_.refs_6_ = bf16[128,1024]{1,0:T(8,128)(2,1)S(1)} collective-permute-done((bf16[128,1024]{1,0:T(8,128)(2,1)S(1)}, bf16[128,1024]{1,0:T(8,128)(2,1)S(1)}, u32[]{:S(2)}, u32[]{:S(2)}) %collective-permute-start.1) | collective-permute-done | bytes 262176 | tf_op jit(solution)/shard_map/ppermute | solution.py:259
  14.5 5.1 %collective-permute-done.2.refs_3_.refs_7_ = bf16[128,1024]{1,0:T(8,128)(2,1)S(1)} collective-permute-done((bf16[128,1024]{1,0:T(8,128)(2,1)S(1)}, bf16[128,1024]{1,0:T(8,128)(2,1)S(1)}, u32[]{:S(2)}, u32[]{:S(2)}) %collective-permute-start.2) | collective-permute-done | bytes 262176 | tf_op jit(solution)/shard_map/ppermute | solution.py:259
  19.6 5.2 %slots_attend.2 = bf16[8,128,768]{2,1,0:T(8,128)(2,1)} custom-call(s32[2]{0:T(128)S(1)} %pad_add_fusion.place_ref, s32[8,8]{1,0:T(8,128)S(1)} %copy-done.5, s32[8,8]{1,0:T(8,128)S(1)} %copy-done.6, bf16[128,1024]{1,0:T(8,128)(2,1)S(1)} %get-tuple-element.40.refs_0_.refs_4_, bf16[128,1024]{1,0:T(8,128)(2,1)S(1)} %collective-permute-done.refs_1_.refs_5_, ...), custom_call_target="tpu_custom_call" | custom-call | tf_op jit(solution)/shard_map/slots_attend/pallas_call | solution.py:187
  24.9 5.9 %all-to-all-start.1 = ((bf16[8,128,768]{2,1,0:T(8,128)(2,1)}), bf16[8,128,768]{2,1,0:T(8,128)(2,1)S(1)}, u32[]{:S(2)}, u32[]{:S(2)}) async-start(bf16[8,128,768]{2,1,0:T(8,128)(2,1)} %slots_attend.2), calls=%async_computation.1 | async-start | bytes 3145728 | tf_op jit(solution)/shard_map/all_to_all | solution.py:289
  30.8 1.6 %collective-permute-start.4 = (bf16[128,1536]{1,0:T(8,128)(2,1)}, bf16[128,1536]{1,0:T(8,128)(2,1)S(1)}, u32[]{:S(2)}, u32[]{:S(2)}) collective-permute-start(bf16[128,1536]{1,0:T(8,128)(2,1)} %copy-done.8), channel_id=1, source_target_pairs={{0,2},{1,3},{2,0},{3,1},{4,6},{5,7},{6,4},{7,5},{8,10},{9,11},{10,... | collective-permute-start | bytes 1179656 | tf_op jit(solution)/shard_map/ppermute | solution.py:259
  32.4 0.3 collective-permute-start.5
  32.7 0.1 collective-permute-done.3.refs_1_
  32.7 10.3 %collective-permute-done.4.refs_2_ = bf16[128,1536]{1,0:T(8,128)(2,1)S(1)} collective-permute-done((bf16[128,1536]{1,0:T(8,128)(2,1)}, bf16[128,1536]{1,0:T(8,128)(2,1)S(1)}, u32[]{:S(2)}, u32[]{:S(2)}) %collective-permute-start.4) | collective-permute-done | bytes 393248 | tf_op jit(solution)/shard_map/ppermute | solution.py:259
  43.0 7.5 %collective-permute-done.5.refs_3_ = bf16[128,1536]{1,0:T(8,128)(2,1)S(1)} collective-permute-done((bf16[128,1536]{1,0:T(8,128)(2,1)}, bf16[128,1536]{1,0:T(8,128)(2,1)S(1)}, u32[]{:S(2)}, u32[]{:S(2)}) %collective-permute-start.5) | collective-permute-done | bytes 393248 | tf_op jit(solution)/shard_map/ppermute | solution.py:259
  50.5 7.6 %slots_attend.3 = bf16[8,128,1280]{2,1,0:T(8,128)(2,1)} custom-call(s32[2]{0:T(128)S(1)} %pad_add_fusion.place_ref, s32[8,8]{1,0:T(8,128)S(1)} %copy-done.5, s32[8,8]{1,0:T(8,128)S(1)} %copy-done.6, bf16[128,1536]{1,0:T(8,128)(2,1)S(1)} %get-tuple-element.41.refs_0_, bf16[128,1536]{1,0:T(8,128)(2,1)S(1)} %collective-permute-done.3.refs_1_, ...), custom_call_target="tpu_custom_call" | custom-call | tf_op jit(solution)/shard_map/slots_attend/pallas_call | solution.py:187
  58.1 10.2 %all-to-all-done.1.refs_0_ = bf16[8,128,768]{2,1,0:T(8,128)(2,1)S(1)} async-done(((bf16[8,128,768]{2,1,0:T(8,128)(2,1)}), bf16[8,128,768]{2,1,0:T(8,128)(2,1)S(1)}, u32[]{:S(2)}, u32[]{:S(2)}) %all-to-all-start.1) | async-done | bytes 1572896 | tf_op jit(solution)/shard_map/all_to_all | solution.py:289
  68.2 1.1 copy-done.1
  69.4 3.6 %all-to-all-start = ((bf16[8,128,1280]{2,1,0:T(8,128)(2,1)}), bf16[8,128,1280]{2,1,0:T(8,128)(2,1)S(1)}, u32[]{:S(2)}, u32[]{:S(2)}) async-start(bf16[8,128,1280]{2,1,0:T(8,128)(2,1)} %slots_attend.3), calls=%async_computation | async-start | bytes 5242880 | tf_op jit(solution)/shard_map/all_to_all | solution.py:289
  73.0 1.6 %collective-permute-start.6 = (bf16[8,128,256]{2,1,0:T(8,128)(2,1)S(1)}, bf16[8,128,256]{2,1,0:T(8,128)(2,1)S(1)}, u32[]{:S(2)}, u32[]{:S(2)}) collective-permute-start(bf16[8,128,256]{2,1,0:T(8,128)(2,1)S(1)} %bitcast.6), channel_id=1, source_target_pairs={{0,2},{1,3},{2,0},{3,1},{4,6},{5,7},{6,4},{7,5},{8,10},{9,11},{10,... | collective-permute-start | bytes 1572872 | tf_op jit(solution)/shard_map/ppermute | solution.py:89
  74.6 12.1 %collective-permute-done.6.refs_1_ = bf16[8,128,256]{2,1,0:T(8,128)(2,1)S(1)} collective-permute-done((bf16[8,128,256]{2,1,0:T(8,128)(2,1)S(1)}, bf16[8,128,256]{2,1,0:T(8,128)(2,1)S(1)}, u32[]{:S(2)}, u32[]{:S(2)}) %collective-permute-start.6) | collective-permute-done | bytes 524320 | tf_op jit(solution)/shard_map/ppermute | solution.py:89
  86.7 1.9 %collective-permute-done.8.refs_3_ = bf16[8,128,256]{2,1,0:T(8,128)(2,1)S(1)} collective-permute-done((bf16[8,128,256]{2,1,0:T(8,128)(2,1)S(1)}, bf16[8,128,256]{2,1,0:T(8,128)(2,1)S(1)}, u32[]{:S(2)}, u32[]{:S(2)}) %collective-permute-start.8) | collective-permute-done | bytes 524320 | tf_op jit(solution)/shard_map/ppermute | solution.py:89
  88.6 1.6 %copy-done.3 = bf16[128,64,128]{2,1,0:T(8,128)(2,1)S(1)} copy-done((bf16[128,64,128]{2,1,0:T(8,128)(2,1)S(1)}, bf16[128,64,128]{2,1,0:T(8,128)(2,1)}, u32[]{:S(2)}) %copy-start.3) | copy-done | bytes 2097176
  90.2 8.2 %long_attend.1 = bf16[128,8192]{1,0:T(8,128)(2,1)} custom-call(s32[1]{0:T(128)} %bitcast.own_ref, bf16[128,64,128]{2,1,0:T(8,128)(2,1)S(1)} %copy-done.3, bf16[8,128,256]{2,1,0:T(8,128)(2,1)S(1)} %bitcast.8, bf16[8,128,256]{2,1,0:T(8,128)(2,1)S(1)} %collective-permute-done.6.refs_1_, bf16[8,128,256]{2,1,0:T(8,128)(2,1)S(1)} %collective-permute-done.7.refs_2_, ...), custom_call_target="tpu_custom_call" | custom-call | tf_op jit(solution)/shard_map/long_attend/pallas_call | solution.py:61
  98.4 1.1 lay.2.refs_1_
  99.5 33.1 %all-to-all-done.refs_0_ = bf16[8,128,1280]{2,1,0:T(8,128)(2,1)S(1)} async-done(((bf16[8,128,1280]{2,1,0:T(8,128)(2,1)}), bf16[8,128,1280]{2,1,0:T(8,128)(2,1)S(1)}, u32[]{:S(2)}, u32[]{:S(2)}) %all-to-all-start) | async-done | bytes 2621472 | tf_op jit(solution)/shard_map/all_to_all | solution.py:289
  132.7 1.5 %lay.3 = bf16[8,128,2048]{2,1,0:T(8,128)(2,1)} custom-call(bf16[8,128,1280]{2,1,0:T(8,128)(2,1)S(1)} %all-to-all-done.refs_0_, bf16[8,128,2048]{2,1,0:T(8,128)(2,1)} %lay.2.refs_1_), custom_call_target="tpu_custom_call", output_to_operand_aliasing={{}: (1, {})} | custom-call | tf_op jit(solution)/shard_map/lay/pallas_call | solution.py:220
  (21 shorter events, 0.1 us)
Async XLA Ops:
  0.6 1.6 %copy-start = (bf16[128,64,128]{2,1,0:T(8,128)(2,1)S(1)}, bf16[128,64,128]{2,1,0:T(8,128)(2,1)}, u32[]{:S(2)}) copy-start(bf16[128,64,128]{2,1,0:T(8,128)(2,1)} %q_ref.3) | copy-start | bytes 6291460
  2.2 1.0 copy-start.4
  3.3 7.8 %copy-start.10 = (bf16[128,8,256]{2,1,0:T(8,128)(2,1)S(1)}, bf16[128,8,256]{2,1,0:T(8,128)(2,1)}, u32[]{:S(2)}) copy-start(bf16[128,8,256]{2,1,0:T(8,128)(2,1)} %param.7) | copy-start | bytes 1572868
  4.3 15.4 %copy-start.5 = (s32[8,8]{1,0:T(8,128)S(1)}, s32[8,8]{1,0:T(8,128)}, u32[]{:S(2)}) copy-start(s32[8,8]{1,0:T(8,128)} %lengths_ref.3) | copy-start | bytes 772
  4.3 15.4 %copy-start.6 = (s32[8,8]{1,0:T(8,128)S(1)}, s32[8,8]{1,0:T(8,128)}, u32[]{:S(2)}) copy-start(s32[8,8]{1,0:T(8,128)} %targets_ref.3) | copy-start | bytes 772
  4.3 6.9 %collective-permute-start = (bf16[128,1024]{1,0:T(8,128)(2,1)S(1)}, bf16[128,1024]{1,0:T(8,128)(2,1)S(1)}, u32[]{:S(2)}, u32[]{:S(2)}) collective-permute-start(bf16[128,1024]{1,0:T(8,128)(2,1)S(1)} %get-tuple-element.30), channel_id=1, source_target_pairs={{0,1},{1,0},{2,3},{3,2},{4,5},{5,4},{6,7},{7,6},{8,9},{9,8},{10,11... | collective-permute-start | bytes 786440 | tf_op jit(solution)/shard_map/ppermute | solution.py:259
  4.8 9.7 %collective-permute-start.1 = (bf16[128,1024]{1,0:T(8,128)(2,1)S(1)}, bf16[128,1024]{1,0:T(8,128)(2,1)S(1)}, u32[]{:S(2)}, u32[]{:S(2)}) collective-permute-start(bf16[128,1024]{1,0:T(8,128)(2,1)S(1)} %get-tuple-element.31), channel_id=1, source_target_pairs={{0,2},{1,3},{2,0},{3,1},{4,6},{5,7},{6,4},{7,5},{8,10},{9,11},{10,... | collective-permute-start | bytes 786440 | tf_op jit(solution)/shard_map/ppermute | solution.py:259
  7.4 12.3 %collective-permute-start.2 = (bf16[128,1024]{1,0:T(8,128)(2,1)S(1)}, bf16[128,1024]{1,0:T(8,128)(2,1)S(1)}, u32[]{:S(2)}, u32[]{:S(2)}) collective-permute-start(bf16[128,1024]{1,0:T(8,128)(2,1)S(1)} %get-tuple-element.32), channel_id=1, source_target_pairs={{0,3},{1,2},{2,1},{3,0},{4,7},{5,6},{6,5},{7,4},{8,11},{9,10},{10,... | collective-permute-start | bytes 786440 | tf_op jit(solution)/shard_map/ppermute | solution.py:259
  8.8 0.7 copy-start.7
  9.5 0.7 copy-start.8
  10.3 0.7 copy-start.9
  24.9 43.4 %all-to-all-start.1 = ((bf16[8,128,768]{2,1,0:T(8,128)(2,1)}), bf16[8,128,768]{2,1,0:T(8,128)(2,1)S(1)}, u32[]{:S(2)}, u32[]{:S(2)}) async-start(bf16[8,128,768]{2,1,0:T(8,128)(2,1)} %slots_attend.2), calls=%async_computation.1 | async-start | bytes 3145728 | tf_op jit(solution)/shard_map/all_to_all | solution.py:289
  30.8 1.9 %collective-permute-start.3 = (bf16[128,1536]{1,0:T(8,128)(2,1)}, bf16[128,1536]{1,0:T(8,128)(2,1)S(1)}, u32[]{:S(2)}, u32[]{:S(2)}) collective-permute-start(bf16[128,1536]{1,0:T(8,128)(2,1)} %copy-done.9), channel_id=1, source_target_pairs={{0,1},{1,0},{2,3},{3,2},{4,5},{5,4},{6,7},{7,6},{8,9},{9,8},{10,11... | collective-permute-start | bytes 1179656 | tf_op jit(solution)/shard_map/ppermute | solution.py:259
  30.8 12.2 %collective-permute-start.4 = (bf16[128,1536]{1,0:T(8,128)(2,1)}, bf16[128,1536]{1,0:T(8,128)(2,1)S(1)}, u32[]{:S(2)}, u32[]{:S(2)}) collective-permute-start(bf16[128,1536]{1,0:T(8,128)(2,1)} %copy-done.8), channel_id=1, source_target_pairs={{0,2},{1,3},{2,0},{3,1},{4,6},{5,7},{6,4},{7,5},{8,10},{9,11},{10,... | collective-permute-start | bytes 1179656 | tf_op jit(solution)/shard_map/ppermute | solution.py:259
  32.4 18.1 %collective-permute-start.5 = (bf16[128,1536]{1,0:T(8,128)(2,1)}, bf16[128,1536]{1,0:T(8,128)(2,1)S(1)}, u32[]{:S(2)}, u32[]{:S(2)}) collective-permute-start(bf16[128,1536]{1,0:T(8,128)(2,1)} %copy-done.7), channel_id=1, source_target_pairs={{0,3},{1,2},{2,1},{3,0},{4,7},{5,6},{6,5},{7,4},{8,11},{9,10},{10,... | collective-permute-start | bytes 1179656 | tf_op jit(solution)/shard_map/ppermute | solution.py:259
  68.2 1.1 copy-start.1
  69.4 63.3 %all-to-all-start = ((bf16[8,128,1280]{2,1,0:T(8,128)(2,1)}), bf16[8,128,1280]{2,1,0:T(8,128)(2,1)S(1)}, u32[]{:S(2)}, u32[]{:S(2)}) async-start(bf16[8,128,1280]{2,1,0:T(8,128)(2,1)} %slots_attend.3), calls=%async_computation | async-start | bytes 5242880 | tf_op jit(solution)/shard_map/all_to_all | solution.py:289
  73.0 25.4 %copy-start.2 = (bf16[8,128,768]{2,1,0:T(8,128)(2,1)S(1)}, bf16[8,128,768]{2,1,0:T(8,128)(2,1)}, u32[]{:S(2)}) copy-start(bf16[8,128,768]{2,1,0:T(8,128)(2,1)} %copy-done.1) | copy-start | bytes 4718596
  73.0 13.6 %collective-permute-start.6 = (bf16[8,128,256]{2,1,0:T(8,128)(2,1)S(1)}, bf16[8,128,256]{2,1,0:T(8,128)(2,1)S(1)}, u32[]{:S(2)}, u32[]{:S(2)}) collective-permute-start(bf16[8,128,256]{2,1,0:T(8,128)(2,1)S(1)} %bitcast.6), channel_id=1, source_target_pairs={{0,2},{1,3},{2,0},{3,1},{4,6},{5,7},{6,4},{7,5},{8,10},{9,11},{10,... | collective-permute-start | bytes 1572872 | tf_op jit(solution)/shard_map/ppermute | solution.py:89
  74.6 12.1 %collective-permute-start.7 = (bf16[8,128,256]{2,1,0:T(8,128)(2,1)S(1)}, bf16[8,128,256]{2,1,0:T(8,128)(2,1)S(1)}, u32[]{:S(2)}, u32[]{:S(2)}) collective-permute-start(bf16[8,128,256]{2,1,0:T(8,128)(2,1)S(1)} %bitcast.7), channel_id=1, source_target_pairs={{0,1},{1,0},{2,3},{3,2},{4,5},{5,4},{6,7},{7,6},{8,9},{9,8},{10,11... | collective-permute-start | bytes 1572872 | tf_op jit(solution)/shard_map/ppermute | solution.py:89
  86.7 1.9 %collective-permute-start.8 = (bf16[8,128,256]{2,1,0:T(8,128)(2,1)S(1)}, bf16[8,128,256]{2,1,0:T(8,128)(2,1)S(1)}, u32[]{:S(2)}, u32[]{:S(2)}) collective-permute-start(bf16[8,128,256]{2,1,0:T(8,128)(2,1)S(1)} %collective-permute-done.6.refs_1_), channel_id=1, source_target_pairs={{0,1},{1,0},{2,3},{3,2},{4,5},{5,4},{6,7},{7,6},{8,9},{9,8},{10,11... | collective-permute-start | bytes 1572872 | tf_op jit(solution)/shard_map/ppermute | solution.py:89
  88.6 1.6 %copy-start.3 = (bf16[128,64,128]{2,1,0:T(8,128)(2,1)S(1)}, bf16[128,64,128]{2,1,0:T(8,128)(2,1)}, u32[]{:S(2)}) copy-start(bf16[128,64,128]{2,1,0:T(8,128)(2,1)} %q_ref.4) | copy-start | bytes 6291460

commit v3 on v2

--- a/solution.py
+++ b/solution.py
@@ -9,6 +9,7 @@
 from jax.sharding import PartitionSpec as P
 
 LOG2_E = 1.4426950408889634
+COST = 10**11
 VMEM_LIMIT = 24 * 1024 * 1024
 
 
@@ -92,7 +93,7 @@
     return blocks, order
 
 
-HEAD_CHUNKS = ((0, 6), (6, 16))
+HEAD_CHUNKS = ((0, 4), (4, 16))
 
 
 def prepare_kernel(own_ref, q_ref, kv_ref, *refs, count, low, high, kv_low, kv_high):
@@ -103,9 +104,12 @@
     if kv_low < kv_high:
         for part in range(2):
             split_heads(kv_scratch.at[part], kv_ref[:, :, part * size : (part + 1) * size])
-    for k, out_ref in enumerate(out_refs):
-        to = own_ref[0] ^ k
-        split_heads(q_scratch, q_ref[:, pl.ds(pl.multiple_of(to * here, here), here), :])
+    for k in range(count):
+        if len(out_refs) == 1:
+            to, out_ref = k, out_refs[0].at[k]
+        else:
+            to, out_ref = own_ref[0] ^ k, out_refs[k]
+        split_heads(q_scratch, q_ref[:, pl.ds(to * here if len(out_refs) == 1 else pl.multiple_of(to * here, here), here), :])
         at = 0
         for h in range(low, high):
             picked = q_scratch[pl.ds(h, tokens, stride=here), :]
@@ -118,16 +122,18 @@
                 at += size
 
 
-def prepare(own, queries, pairs, count, low, high, kv_low, kv_high):
+def prepare(own, queries, pairs, count, low, high, kv_low, kv_high, stacked):
     tokens, heads, size = queries.shape
     kv_heads = pairs.shape[1]
     width = (high - low + 2 * (kv_high - kv_low)) * size
     vmem = pl.BlockSpec(memory_space=pltpu.VMEM)
     return pl.pallas_call(
         functools.partial(prepare_kernel, count=count, low=low, high=high, kv_low=kv_low, kv_high=kv_high),
-        out_shape=[jax.ShapeDtypeStruct((tokens, width), jnp.bfloat16)] * count,
+        out_shape=[jax.ShapeDtypeStruct((count, tokens, width), jnp.bfloat16)]
+        if stacked
+        else [jax.ShapeDtypeStruct((tokens, width), jnp.bfloat16)] * count,
         in_specs=[pl.BlockSpec(memory_space=pltpu.SMEM), vmem, vmem],
-        out_specs=[vmem] * count,
+        out_specs=[vmem] if stacked else [vmem] * count,
         scratch_shapes=[
             pltpu.VMEM((tokens * heads // count, size), jnp.float32),
             pltpu.VMEM((2, tokens * kv_heads, size), jnp.float32),
@@ -138,18 +144,31 @@
     )(own, queries, pairs)
 
 
-def slots_kernel(place_ref, lengths_ref, targets_ref, *refs, blocks, parts, scale):
-    sources, (out_ref, q_ref, kv_ref, mixed_ref, start_ref, length_ref) = refs[:-6], refs[-6:]
-    slots, span, width = out_ref.shape
+def slots_kernel(place_ref, lengths_ref, targets_ref, *refs, sets, outs, parts, scale):
+    count = sum(sets)
+    sources, out_refs = refs[:count], refs[count : count + outs]
+    q_ref, kv_ref, mixed_ref, start_ref, length_ref = refs[count + outs :]
+    slots = lengths_ref.shape[1]
+    span, width = out_refs[0].shape[-2:]
     rows = q_ref.shape[0]
     size = kv_ref.shape[2] // 2
-    block_rows = rows // blocks
     group, own = place_ref[0], place_ref[1]
-    for k in range(blocks):
-        at = pl.ds(pl.multiple_of((own ^ k) * block_rows, block_rows), block_rows)
-        q_ref[at, :] = sources[k][:, :width]
-        for c, (home, column, _, _) in enumerate(parts):
-            kv_ref[c, at, :] = sources[home * blocks + k][:, column : column + 2 * size]
+    firsts = [sum(sets[:i]) for i in range(len(sets))]
+
+    def fill(to_ref, home, columns):
+        if sets[home] == 1:
+            ref = sources[firsts[home]]
+            for m in range(ref.shape[0]):
+                to_ref[m * ref.shape[1] : (m + 1) * ref.shape[1], :] = ref[m, :, columns]
+        else:
+            for k in range(sets[home]):
+                ref = sources[firsts[home] + k]
+                at = pl.ds(pl.multiple_of((own ^ k) * ref.shape[0], ref.shape[0]), ref.shape[0])
+                to_ref[at, :] = ref[:, columns]
+
+    fill(q_ref, 0, slice(0, width))
+    for c, (home, column, _, _) in enumerate(parts):
+        fill(kv_ref.at[c], home, slice(column, column + 2 * size))
     row = lax.broadcasted_iota(jnp.int32, (rows, 1), 0)
     begin = jnp.zeros((rows, 1), jnp.int32)
     start = jnp.int32(0)
@@ -173,22 +192,28 @@
                 mixed_ref[here, columns] = mixed.astype(mixed_ref.dtype)
     place = lax.broadcasted_iota(jnp.int32, (span, rows), 0)
     source = lax.broadcasted_iota(jnp.int32, (span, rows), 1)
-    for d in range(slots):
+    for k in range(slots):
+        d, out_ref = (k, out_refs[0].at[k]) if outs == 1 else (group ^ k, out_refs[k])
         chosen = (source == place + start_ref[d]) & (place < length_ref[d])
         picked = jnp.dot(chosen.astype(jnp.bfloat16), mixed_ref[...], preferred_element_type=jnp.float32)
-        out_ref[d] = picked.astype(out_ref.dtype)
-
-
-def slots_attend(place, lengths, targets, sources, parts, blocks, width, span, size):
-    rows = blocks * sources[0].shape[0]
+        out_ref[...] = picked.astype(out_ref.dtype)
+
+
+def slots_attend(place, lengths, targets, source_sets, parts, rows, width, span, size, split):
     slots = lengths.shape[0]
     smem = pl.BlockSpec(memory_space=pltpu.SMEM)
     vmem = pl.BlockSpec(memory_space=pltpu.VMEM)
+    sets = tuple(len(blocks) for blocks in source_sets)
+    sources = [block for blocks in source_sets for block in blocks]
+    shape = (span, width) if split else (slots, span, width)
+    outs = slots if split else 1
     return pl.pallas_call(
-        functools.partial(slots_kernel, blocks=blocks, parts=parts, scale=LOG2_E / math.sqrt(size)),
-        out_shape=jax.ShapeDtypeStruct((slots, span, width), jnp.bfloat16),
+        functools.partial(
+            slots_kernel, sets=sets, outs=outs, parts=parts, scale=LOG2_E / math.sqrt(size)
+        ),
+        out_shape=[jax.ShapeDtypeStruct(shape, jnp.bfloat16)] * outs,
         in_specs=[smem, smem, smem] + [vmem] * len(sources),
-        out_specs=vmem,
+        out_specs=[vmem] * outs,
         scratch_shapes=[
             pltpu.VMEM((rows, width), jnp.bfloat16),
             pltpu.VMEM((len(parts), rows, 2 * size), jnp.bfloat16),
@@ -197,30 +222,31 @@
             pltpu.SMEM((slots,), jnp.int32),
         ],
         compiler_params=pltpu.CompilerParams(vmem_limit_bytes=VMEM_LIMIT),
-        cost_estimate=pl.CostEstimate(flops=0, bytes_accessed=0, transcendentals=0),
+        cost_estimate=pl.CostEstimate(flops=COST, bytes_accessed=0, transcendentals=0),
         name="slots_attend",
     )(place, lengths, targets, *sources)
 
 
-def lay_kernel(*refs, lows):
-    pieces, (out_ref, sems) = refs[: len(lows)], refs[-2:]
+def lay_kernel(place_ref, *refs, count, low):
+    pieces, (out_ref, sems) = refs[:count], refs[-2:]
+    width = pieces[0].shape[-1]
     copies = []
-    for i, (ref, low) in enumerate(zip(pieces, lows)):
-        to = out_ref.at[:, :, low : low + ref.shape[2]]
-        copies.append(pltpu.make_async_copy(ref, to, sems.at[i]))
+    for k, ref in enumerate(pieces):
+        at = slice(low, low + width)
+        to = out_ref.at[:, :, at] if count == 1 else out_ref.at[place_ref[0] ^ k, :, at]
+        copies.append(pltpu.make_async_copy(ref, to, sems.at[k]))
         copies[-1].start()
     for copy in copies:
         copy.wait()
 
 
-def lay(pieces, lows, columns, whole=None):
+def lay(place, pieces, low, shape, whole=None):
     anywhere = pl.BlockSpec(memory_space=pl.ANY)
-    operands = pieces + ([] if whole is None else [whole])
-    slots, span, _ = pieces[0].shape
+    operands = [place, *pieces] + ([] if whole is None else [whole])
     return pl.pallas_call(
-        functools.partial(lay_kernel, lows=lows),
-        out_shape=jax.ShapeDtypeStruct((slots, span, columns), jnp.bfloat16),
-        in_specs=[anywhere] * len(operands),
+        functools.partial(lay_kernel, count=len(pieces), low=low),
+        out_shape=jax.ShapeDtypeStruct(shape, jnp.bfloat16),
+        in_specs=[pl.BlockSpec(memory_space=pltpu.SMEM)] + [anywhere] * (len(operands) - 1),
         out_specs=anywhere,
         input_output_aliases={} if whole is None else {len(operands) - 1: 0},
         scratch_shapes=[pltpu.SemaphoreType.DMA((len(pieces),))],
@@ -251,46 +277,64 @@
         for j, c in enumerate(new):
             homes[c] = (i, (high - low + 2 * j) * size)
         kv_low, kv_high = (new[0], new[-1] + 1) if new else (0, 0)
-        sent.append(prepare(own, short_queries, short_pairs, head_count, low, high, kv_low, kv_high))
-
-    def swap(blocks):
-        moved = [blocks[0]]
-        for k in range(1, head_count):
-            moved.append(lax.ppermute(blocks[k], "head", [(i, i ^ k) for i in range(head_count)]))
-        return moved
+        sent.append(
+            prepare(own, short_queries, short_pairs, head_count, low, high, kv_low, kv_high, stacked=i > 0)
+        )
+
+    def swap(blocks, axis, count):
+        return [blocks[0]] + [
+            lax.ppermute(blocks[k], axis, [(i, i ^ k) for i in range(count)]) for k in range(1, count)
+        ]
 
     pairs_by_head = jnp.swapaxes(long_pairs, 0, 1)
-    got, slots, whole = [], [], None
+    got, slots = [], []
+    split = [i == 0 and group_count <= 8 for i in range(len(chunks))]
     for i, (low, high) in enumerate(chunks):
-        if i:
-            sent[i] = after(sent[i], got[i - 1][1:])
-        got.append(swap(sent[i]))
         if i == 0:
-            got[0] = after(got[0], sent[1:], pairs_by_head)
-        else:
-            got[i] = after(got[i], slots[i - 1])
+            moved = swap(sent[0], "head", head_count)
+            got.append([after(block, sent[1:], pairs_by_head) for block in moved])
+        else:
+            if i > 1:
+                sent[i] = [after(sent[i][0], slots[i - 2])]
+            moved = lax.all_to_all(sent[i][0], "head", split_axis=0, concat_axis=0, tiled=True)
+            got.append([after(moved, slots[i - 1])])
         touched = [c for c in range(own_kv) if c * share < high and low < (c + 1) * share]
         order = [i] + sorted({homes[c][0] for c in touched} - {i})
         parts = [
             (order.index(homes[c][0]), homes[c][1], max(low, c * share) - low, min(high, (c + 1) * share) - low)
             for c in touched
         ]
-        sources = [block for j in order for block in got[j]]
         slots.append(
             slots_attend(
-                place, doc_lengths, destinations, sources, parts, head_count, (high - low) * size, span, size
+                place,
+                doc_lengths,
+                destinations,
+                [got[j] for j in order],
+                parts,
+                head_count * local_rows,
+                (high - low) * size,
+                span,
+                size,
+                split[i],
             )
         )
-    pairs_by_head = after(pairs_by_head, got[-1])
-    shared, order = share_blocks(pairs_by_head, "head")
-    long_queries = after(long_queries, slots[-1])
-    long_result = long_attend(own, long_queries, shared, order)
+    shared, order = share_blocks(after(pairs_by_head, got[-1]), "head")
+    long_result = long_attend(own, after(long_queries, slots[-1]), shared, order)
+    whole, far = None, None
+    shape = (group_count, span, own_heads * size)
     for i, (low, high) in enumerate(chunks):
-        moved = lax.all_to_all(slots[i], "grp", split_axis=0, concat_axis=0, tiled=True)
+        if split[i]:
+            near = [after(piece, slots[-1]) for piece in slots[i][: group_count // 2]]
+            moved = swap([*near, *slots[i][group_count // 2 :]], "grp", group_count)
+            far = moved[group_count // 2 :]
+        else:
+            moved = [lax.all_to_all(after(slots[i][0], far), "grp", split_axis=0, concat_axis=0, tiled=True)]
         if i == len(chunks) - 1:
-            moved = after(moved, long_result)
-        whole = lay([moved], [low * size], columns, whole)
-    return long_result, whole.reshape(group_count * span, columns)
+            moved = [after(moved[0], long_result)]
+        else:
+            moved[0] = after(moved[0], long_result)
+        whole = lay(place, moved, low * size, shape, whole)
+    return long_result, whole.reshape(group_count * span, own_heads * size)
 
 
 def solution(mesh):

time: 135 us -> 128 us (0.948)
  waiting for transfers between devices: 83.5 us -> 61.6 us
  starting transfers between devices: 16.1 us -> 26.8 us
  local copies, waits for them, and re-layouts: 7.69 us -> 10.8 us
    all_to_all x2, waiting for transfers between devices: 43.3 us -> 19.3 us  [the longest x1 11.6 us: on_device(): lax.all_to_all(after(slots[i][0], far), 'grp', split_axis=0, concat_axis=...]
    ppermute x6 -> x10, starting transfers between devices: 5.01 us -> 14.9 us  [swap(): lax.ppermute(blocks[k], axis, [(i, i ^ k) for i in range(count)])]
    ppermute x6 -> x10, waiting for transfers between devices: 26.2 us -> 30.1 us  [swap(): lax.ppermute(blocks[k], axis, [(i, i ^ k) for i in range(count)])]
    unnamed x23 -> x31, local copies, waits for them, and re-layouts: 7.69 us -> 10.8 us
    ppermute x3, waiting for transfers between devices: 14 us -> 12.3 us  [share_blocks(): blocks += [lax.ppermute(b, axis, pairs) for b in blocks]]
  transfers between devices with their start and end apart: 11 -> 15, of which waited for: 9 -> 7; matrix products, arithmetic and copies ran while one was open for 0% -> 2% of each run, Pallas kernels for 14% -> 18%
where the time goes in v3:
time: 128 us; the launch traced here: 127 us
  waiting for transfers between devices  61.6 us (48%)
  starting transfers between devices  26.8 us (21%)
  Pallas kernels  26.4 us (21%)
  local copies, waits for them, and re-layouts  10.8 us (8%)
    ppermute x10, waiting for transfers between devices, swap(): lax.ppermute(blocks[k], axis, [(i, i ^ k) for i in range(count)])  30.1 us
    ppermute x10, starting transfers between devices, swap(): lax.ppermute(blocks[k], axis, [(i, i ^ k) for i in range(count)])  14.9 us
    ppermute x3, waiting for transfers between devices, share_blocks(): blocks += [lax.ppermute(b, axis, pairs) for b in blocks]  12.3 us
    all_to_all x1, waiting for transfers between devices, on_device(): lax.all_to_all(after(slots[i][0], far), 'grp', split_axis=0, concat_axis=...  11.6 us
    unnamed x31, local copies, waits for them, and re-layouts  10.8 us
    pallas_call x2, Pallas kernels, slots_attend(): pl.pallas_call(functools.partial(slots_kernel, sets=sets, outs=outs, part...  10.7 us
    pallas_call x1, Pallas kernels, long_attend(): pl.pallas_call(functools.partial(long_kernel, order=order, scale=LOG2_E /...  8.37 us
    all_to_all x1, waiting for transfers between devices, on_device(): lax.all_to_all(sent[i][0], 'head', split_axis=0, concat_axis=0, tiled=True)  7.66 us
  transfers between devices with their start and end apart: 15, of which 7 were waited for; matrix products, arithmetic and copies ran while one was open for 2% of the time, Pallas kernels for 18%

profile of v3, /device:TPU:0, one launch (start us, length us, event | category | flops | bytes accessed | tf_op | source)
XLA Modules:
  0.0 126.5 jit_solution(14679664414950873314)
XLA Ops:
  0.6 1.6 %copy-done = bf16[128,64,128]{2,1,0:T(8,128)(2,1)S(1)} copy-done((bf16[128,64,128]{2,1,0:T(8,128)(2,1)S(1)}, bf16[128,64,128]{2,1,0:T(8,128)(2,1)}, u32[]{:S(2)}) %copy-start) | copy-done | bytes 2097176
  2.2 1.0 copy-done.4
  3.3 0.8 prepare.3
  4.1 2.4 %collective-permute-start.2 = (bf16[128,768]{1,0:T(8,128)(2,1)S(1)}, bf16[128,768]{1,0:T(8,128)(2,1)S(1)}, u32[]{:S(2)}, u32[]{:S(2)}) collective-permute-start(bf16[128,768]{1,0:T(8,128)(2,1)S(1)} %get-tuple-element.34), channel_id=1, source_target_pairs={{0,3},{1,2},{2,1},{3,0},{4,7},{5,6},{6,5},{7,4},{8,11},{9,10},{10,... | collective-permute-start | bytes 589832 | tf_op jit(solution)/shard_map/ppermute | solution.py:286
  6.5 0.6 collective-permute-start.1
  7.2 2.7 %prepare.2 = bf16[4,128,1792]{2,1,0:T(8,128)(2,1)} custom-call(s32[1]{0:T(128)} %bitcast.own_ref, bf16[128,64,128]{2,1,0:T(8,128)(2,1)S(1)} %copy-done, bf16[128,8,256]{2,1,0:T(8,128)(2,1)S(1)} %copy-done.5), custom_call_target="tpu_custom_call" | custom-call | tf_op jit(solution)/shard_map/prepare/pallas_call | solution.py:130
  10.0 3.7 %all-to-all-start = ((bf16[4,128,1792]{2,1,0:T(8,128)(2,1)}), bf16[4,128,1792]{2,1,0:T(8,128)(2,1)S(1)}, u32[]{:S(2)}, u32[]{:S(2)}) async-start(bf16[4,128,1792]{2,1,0:T(8,128)(2,1)} %prepare.2), calls=%async_computation | async-start | bytes 3670016 | tf_op jit(solution)/shard_map/all_to_all | solution.py:299
  13.7 1.9 %copy.11 = bf16[128,8,256]{2,0,1:T(8,128)(2,1)} copy(bf16[128,8,256]{2,1,0:T(8,128)(2,1)} %param.7) | data formatting | bytes 1048576 | tf_op args[1]
  16.2 3.7 %slots_attend.2 = (bf16[128,512]{1,0:T(8,128)(2,1)S(1)}, bf16[128,512]{1,0:T(8,128)(2,1)S(1)}, bf16[128,512]{1,0:T(8,128)(2,1)S(1)}, bf16[128,512]{1,0:T(8,128)(...) custom-call(s32[2]{0:T(128)S(1)} %pad_add_fusion.place_ref, ...), custom_call_target="tpu_custom_call" | custom-call | flops 99999997952 | tf_op jit(solution)/shard_map/slots_attend/pallas_call | solution.py:210
  19.9 0.6 copy-done.12
  20.6 3.4 %collective-permute-start.6 = (bf16[128,512]{1,0:T(8,128)(2,1)}, bf16[128,512]{1,0:T(8,128)(2,1)S(1)}, u32[]{:S(2)}, u32[]{:S(2)}) collective-permute-start(bf16[128,512]{1,0:T(8,128)(2,1)} %get-tuple-element.40), channel_id=1, source_target_pairs={{0,16},{4,20},{8,24},{12,28},{16,0},{20,4},{24,8},{28,12},{1,17},{... | collective-permute-start | bytes 393224 | tf_op jit(solution)/shard_map/ppermute | solution.py:286
  24.0 1.3 %collective-permute-start.7 = (bf16[128,512]{1,0:T(8,128)(2,1)}, bf16[128,512]{1,0:T(8,128)(2,1)S(1)}, u32[]{:S(2)}, u32[]{:S(2)}) collective-permute-start(bf16[128,512]{1,0:T(8,128)(2,1)} %get-tuple-element.41), channel_id=1, source_target_pairs={{0,20},{4,16},{8,28},{12,24},{16,4},{20,0},{24,12},{28,8},{1,21},{... | collective-permute-start | bytes 393224 | tf_op jit(solution)/shard_map/ppermute | solution.py:286
  25.3 3.6 %collective-permute-start.8 = (bf16[128,512]{1,0:T(8,128)(2,1)S(1)}, bf16[128,512]{1,0:T(8,128)(2,1)S(1)}, u32[]{:S(2)}, u32[]{:S(2)}) collective-permute-start(bf16[128,512]{1,0:T(8,128)(2,1)S(1)} %get-tuple-element.42), channel_id=1, source_target_pairs={{0,24},{4,28},{8,16},{12,20},{16,8},{20,12},{24,0},{28,4},{1,25},{... | collective-permute-start | bytes 393224 | tf_op jit(solution)/shard_map/ppermute | solution.py:286
  28.9 7.7 %all-to-all-done.refs_0_ = bf16[4,128,1792]{2,1,0:T(8,128)(2,1)S(1)} async-done(((bf16[4,128,1792]{2,1,0:T(8,128)(2,1)}), bf16[4,128,1792]{2,1,0:T(8,128)(2,1)S(1)}, u32[]{:S(2)}, u32[]{:S(2)}) %all-to-all-start) | async-done | bytes 1835040 | tf_op jit(solution)/shard_map/all_to_all | solution.py:299
  36.5 7.0 %slots_attend.3 = bf16[8,128,1536]{2,1,0:T(8,128)(2,1)S(1)} custom-call(s32[2]{0:T(128)S(1)} %pad_add_fusion.place_ref, s32[8,8]{1,0:T(8,128)S(1)} %copy-done.13, s32[8,8]{1,0:T(8,128)S(1)} %copy-done.14, bf16[4,128,1792]{2,1,0:T(8,128)(2,1)S(1)} %all-to-all-done.refs_0_, bf16[128,768]{1,0:T(8,128)(2,1)S(1)} %get-tuple-element.29.refs_0_.refs_1_, ...), custom_call_target="tpu_custom_call" | custom-call | flops 99999997952 | tf_op jit(solution)/shard_map/slots_attend/pallas_call | solution.py:210
  43.5 1.6 %copy-done.1 = bf16[8,128,1536]{2,1,0:T(8,128)(2,1)} copy-done((bf16[8,128,1536]{2,1,0:T(8,128)(2,1)}, bf16[8,128,1536]{2,1,0:T(8,128)(2,1)S(1)}, u32[]{:S(2)}) %copy-start.1) | copy-done | bytes 3145752
  45.2 0.6 copy-done.6
  45.8 0.6 copy-done.8
  46.5 6.6 %all-to-all-start.1 = ((bf16[8,128,1536]{2,1,0:T(8,128)(2,1)}), bf16[8,128,1536]{2,1,0:T(8,128)(2,1)S(1)}, u32[]{:S(2)}, u32[]{:S(2)}) async-start(bf16[8,128,1536]{2,1,0:T(8,128)(2,1)} %copy-done.1), calls=%async_computation.1 | async-start | bytes 6291456 | tf_op jit(solution)/shard_map/all_to_all | solution.py:331
  53.1 1.5 %collective-permute-start.3 = (bf16[8,128,256]{2,1,0:T(8,128)(2,1)}, bf16[8,128,256]{2,1,0:T(8,128)(2,1)S(1)}, u32[]{:S(2)}, u32[]{:S(2)}) collective-permute-start(bf16[8,128,256]{2,1,0:T(8,128)(2,1)} %bitcast.6), channel_id=1, source_target_pairs={{0,2},{1,3},{2,0},{3,1},{4,6},{5,7},{6,4},{7,5},{8,10},{9,11},{10,... | collective-permute-start | bytes 1572872 | tf_op jit(solution)/shard_map/ppermute | solution.py:90
  54.6 12.3 %collective-permute-done.3.refs_1_ = bf16[8,128,256]{2,1,0:T(8,128)(2,1)S(1)} collective-permute-done((bf16[8,128,256]{2,1,0:T(8,128)(2,1)}, bf16[8,128,256]{2,1,0:T(8,128)(2,1)S(1)}, u32[]{:S(2)}, u32[]{:S(2)}) %collective-permute-start.3) | collective-permute-done | bytes 524320 | tf_op jit(solution)/shard_map/ppermute | solution.py:90
  66.9 1.7 %collective-permute-start.10 = (bf16[128,512]{1,0:T(8,128)(2,1)}, bf16[128,512]{1,0:T(8,128)(2,1)S(1)}, u32[]{:S(2)}, u32[]{:S(2)}) collective-permute-start(bf16[128,512]{1,0:T(8,128)(2,1)} %copy-done.12), channel_id=1, source_target_pairs={{0,4},{4,0},{8,12},{12,8},{16,20},{20,16},{24,28},{28,24},{1,5},{5... | collective-permute-start | bytes 393224 | tf_op jit(solution)/shard_map/ppermute | solution.py:286
  68.6 1.5 %collective-permute-start.11 = (bf16[128,512]{1,0:T(8,128)(2,1)}, bf16[128,512]{1,0:T(8,128)(2,1)S(1)}, u32[]{:S(2)}, u32[]{:S(2)}) collective-permute-start(bf16[128,512]{1,0:T(8,128)(2,1)} %copy-done.11), channel_id=1, source_target_pairs={{0,8},{4,12},{8,0},{12,4},{16,24},{20,28},{24,16},{28,20},{1,9},{5... | collective-permute-start | bytes 393224 | tf_op jit(solution)/shard_map/ppermute | solution.py:286
  70.4 1.6 %copy-done.2 = bf16[128,64,128]{2,1,0:T(8,128)(2,1)S(1)} copy-done((bf16[128,64,128]{2,1,0:T(8,128)(2,1)S(1)}, bf16[128,64,128]{2,1,0:T(8,128)(2,1)}, u32[]{:S(2)}) %copy-start.2) | copy-done | bytes 2097176
  72.0 1.0 copy-done.3
  73.0 8.4 %long_attend.1 = bf16[128,8192]{1,0:T(8,128)(2,1)} custom-call(s32[1]{0:T(128)} %bitcast.own_ref, bf16[128,64,128]{2,1,0:T(8,128)(2,1)S(1)} %copy-done.2, bf16[8,128,256]{2,1,0:T(8,128)(2,1)S(1)} %bitcast.8, bf16[8,128,256]{2,1,0:T(8,128)(2,1)S(1)} %collective-permute-done.3.refs_1_, bf16[8,128,256]{2,1,0:T(8,128)(2,1)S(1)} %collective-permute-done.4.refs_2_, ...), custom_call_target="tpu_custom_call" | custom-call | tf_op jit(solution)/shard_map/long_attend/pallas_call | solution.py:62
  81.4 1.0 collective-permute-done.10.refs_1_
  82.4 26.8 %collective-permute-done.11.refs_2_ = bf16[128,512]{1,0:T(8,128)(2,1)S(1)} collective-permute-done((bf16[128,512]{1,0:T(8,128)(2,1)}, bf16[128,512]{1,0:T(8,128)(2,1)S(1)}, u32[]{:S(2)}, u32[]{:S(2)}) %collective-permute-start.11) | collective-permute-done | bytes 131104 | tf_op jit(solution)/shard_map/ppermute | solution.py:286
  109.1 1.9 %collective-permute-done.12.refs_3_ = bf16[128,512]{1,0:T(8,128)(2,1)S(1)} collective-permute-done((bf16[128,512]{1,0:T(8,128)(2,1)}, bf16[128,512]{1,0:T(8,128)(2,1)S(1)}, u32[]{:S(2)}, u32[]{:S(2)}) %collective-permute-start.12) | collective-permute-done | bytes 131104 | tf_op jit(solution)/shard_map/ppermute | solution.py:286
  111.0 1.6 %lay.2.refs_1_ = bf16[8,128,2048]{2,1,0:T(8,128)(2,1)} custom-call(s32[2]{0:T(128)S(1)} %pad_add_fusion.place_ref, bf16[128,512]{1,0:T(8,128)(2,1)S(1)} %get-tuple-element.50.refs_0_, bf16[128,512]{1,0:T(8,128)(2,1)S(1)} %collective-permute-done.10.refs_1_, bf16[128,512]{1,0:T(8,128)(2,1)S(1)} %collective-permute-done.11.refs_2_, ...), custom_call_target="tpu_custom_call" | custom-call | tf_op jit(solution)/shard_map/lay/pallas_call | solution.py:246
  112.6 11.6 %all-to-all-done.1.refs_0_ = bf16[8,128,1536]{2,1,0:T(8,128)(2,1)S(1)} async-done(((bf16[8,128,1536]{2,1,0:T(8,128)(2,1)}), bf16[8,128,1536]{2,1,0:T(8,128)(2,1)S(1)}, u32[]{:S(2)}, u32[]{:S(2)}) %all-to-all-start.1) | async-done | bytes 3145760 | tf_op jit(solution)/shard_map/all_to_all | solution.py:331
  124.2 2.2 %lay.3 = bf16[8,128,2048]{2,1,0:T(8,128)(2,1)} custom-call(s32[2]{0:T(128)S(1)} %pad_add_fusion.place_ref, bf16[8,128,1536]{2,1,0:T(8,128)(2,1)S(1)} %all-to-all-done.1.refs_0_, bf16[8,128,2048]{2,1,0:T(8,128)(2,1)} %lay.2.refs_1_), custom_call_target="tpu_custom_call", output_to_operand_aliasing={{}: (2, {})} | custom-call | tf_op jit(solution)/shard_map/lay/pallas_call | solution.py:246
  (37 shorter events, 1.0 us)
Async XLA Ops:
  0.6 1.6 %copy-start = (bf16[128,64,128]{2,1,0:T(8,128)(2,1)S(1)}, bf16[128,64,128]{2,1,0:T(8,128)(2,1)}, u32[]{:S(2)}) copy-start(bf16[128,64,128]{2,1,0:T(8,128)(2,1)} %q_ref.3) | copy-start | bytes 6291460
  2.2 1.0 copy-start.4
  3.3 3.9 %copy-start.5 = (bf16[128,8,256]{2,1,0:T(8,128)(2,1)S(1)}, bf16[128,8,256]{2,1,0:T(8,128)(2,1)}, u32[]{:S(2)}) copy-start(bf16[128,8,256]{2,1,0:T(8,128)(2,1)} %kv_ref.3) | copy-start | bytes 1572868
  4.1 11.6 %collective-permute-start.2 = (bf16[128,768]{1,0:T(8,128)(2,1)S(1)}, bf16[128,768]{1,0:T(8,128)(2,1)S(1)}, u32[]{:S(2)}, u32[]{:S(2)}) collective-permute-start(bf16[128,768]{1,0:T(8,128)(2,1)S(1)} %get-tuple-element.34), channel_id=1, source_target_pairs={{0,3},{1,2},{2,1},{3,0},{4,7},{5,6},{6,5},{7,4},{8,11},{9,10},{10,... | collective-permute-start | bytes 589832 | tf_op jit(solution)/shard_map/ppermute | solution.py:286
  6.5 9.7 %collective-permute-start.1 = (bf16[128,768]{1,0:T(8,128)(2,1)S(1)}, bf16[128,768]{1,0:T(8,128)(2,1)S(1)}, u32[]{:S(2)}, u32[]{:S(2)}) collective-permute-start(bf16[128,768]{1,0:T(8,128)(2,1)S(1)} %get-tuple-element.32), channel_id=1, source_target_pairs={{0,2},{1,3},{2,0},{3,1},{4,6},{5,7},{6,4},{7,5},{8,10},{9,11},{10,... | collective-permute-start | bytes 589832 | tf_op jit(solution)/shard_map/ppermute | solution.py:286
  7.2 9.0 %collective-permute-start = (bf16[128,768]{1,0:T(8,128)(2,1)S(1)}, bf16[128,768]{1,0:T(8,128)(2,1)S(1)}, u32[]{:S(2)}, u32[]{:S(2)}) collective-permute-start(bf16[128,768]{1,0:T(8,128)(2,1)S(1)} %get-tuple-element.30), channel_id=1, source_target_pairs={{0,1},{1,0},{2,3},{3,2},{4,5},{5,4},{6,7},{7,6},{8,9},{9,8},{10,11... | collective-permute-start | bytes 589832 | tf_op jit(solution)/shard_map/ppermute | solution.py:286
  10.0 6.3 %copy-start.13 = (s32[8,8]{1,0:T(8,128)S(1)}, s32[8,8]{1,0:T(8,128)}, u32[]{:S(2)}) copy-start(s32[8,8]{1,0:T(8,128)} %lengths_ref.3) | copy-start | bytes 772
  10.0 6.3 %copy-start.14 = (s32[8,8]{1,0:T(8,128)S(1)}, s32[8,8]{1,0:T(8,128)}, u32[]{:S(2)}) copy-start(s32[8,8]{1,0:T(8,128)} %targets_ref.3) | copy-start | bytes 772
  10.0 26.6 %all-to-all-start = ((bf16[4,128,1792]{2,1,0:T(8,128)(2,1)}), bf16[4,128,1792]{2,1,0:T(8,128)(2,1)S(1)}, u32[]{:S(2)}, u32[]{:S(2)}) async-start(bf16[4,128,1792]{2,1,0:T(8,128)(2,1)} %prepare.2), calls=%async_computation | async-start | bytes 3670016 | tf_op jit(solution)/shard_map/all_to_all | solution.py:299
  19.9 0.6 copy-start.12
  20.6 8.3 %copy-start.10 = (bf16[128,512]{1,0:T(8,128)(2,1)}, bf16[128,512]{1,0:T(8,128)(2,1)S(1)}, u32[]{:S(2)}) copy-start(bf16[128,512]{1,0:T(8,128)(2,1)S(1)} %get-tuple-element.53) | copy-start | bytes 393220
  20.6 8.3 %copy-start.11 = (bf16[128,512]{1,0:T(8,128)(2,1)}, bf16[128,512]{1,0:T(8,128)(2,1)S(1)}, u32[]{:S(2)}) copy-start(bf16[128,512]{1,0:T(8,128)(2,1)S(1)} %get-tuple-element.52) | copy-start | bytes 393220
  20.6 24.6 %collective-permute-start.6 = (bf16[128,512]{1,0:T(8,128)(2,1)}, bf16[128,512]{1,0:T(8,128)(2,1)S(1)}, u32[]{:S(2)}, u32[]{:S(2)}) collective-permute-start(bf16[128,512]{1,0:T(8,128)(2,1)} %get-tuple-element.40), channel_id=1, source_target_pairs={{0,16},{4,20},{8,24},{12,28},{16,0},{20,4},{24,8},{28,12},{1,17},{... | collective-permute-start | bytes 393224 | tf_op jit(solution)/shard_map/ppermute | solution.py:286
  24.0 21.2 %collective-permute-start.7 = (bf16[128,512]{1,0:T(8,128)(2,1)}, bf16[128,512]{1,0:T(8,128)(2,1)S(1)}, u32[]{:S(2)}, u32[]{:S(2)}) collective-permute-start(bf16[128,512]{1,0:T(8,128)(2,1)} %get-tuple-element.41), channel_id=1, source_target_pairs={{0,20},{4,16},{8,28},{12,24},{16,4},{20,0},{24,12},{28,8},{1,21},{... | collective-permute-start | bytes 393224 | tf_op jit(solution)/shard_map/ppermute | solution.py:286
  25.3 19.9 %collective-permute-start.8 = (bf16[128,512]{1,0:T(8,128)(2,1)S(1)}, bf16[128,512]{1,0:T(8,128)(2,1)S(1)}, u32[]{:S(2)}, u32[]{:S(2)}) collective-permute-start(bf16[128,512]{1,0:T(8,128)(2,1)S(1)} %get-tuple-element.42), channel_id=1, source_target_pairs={{0,24},{4,28},{8,16},{12,20},{16,8},{20,12},{24,0},{28,4},{1,25},{... | collective-permute-start | bytes 393224 | tf_op jit(solution)/shard_map/ppermute | solution.py:286
  28.9 17.0 %collective-permute-start.9 = (bf16[128,512]{1,0:T(8,128)(2,1)S(1)}, bf16[128,512]{1,0:T(8,128)(2,1)S(1)}, u32[]{:S(2)}, u32[]{:S(2)}) collective-permute-start(bf16[128,512]{1,0:T(8,128)(2,1)S(1)} %get-tuple-element.43), channel_id=1, source_target_pairs={{0,28},{4,24},{8,20},{12,16},{16,12},{20,8},{24,4},{28,0},{1,29},{... | collective-permute-start | bytes 393224 | tf_op jit(solution)/shard_map/ppermute | solution.py:286
  43.5 1.6 %copy-start.1 = (bf16[8,128,1536]{2,1,0:T(8,128)(2,1)}, bf16[8,128,1536]{2,1,0:T(8,128)(2,1)S(1)}, u32[]{:S(2)}) copy-start(bf16[8,128,1536]{2,1,0:T(8,128)(2,1)S(1)} %slots_attend.3) | copy-start | bytes 9437188
  45.2 0.6 copy-start.6
  45.8 0.6 copy-start.8
  46.5 77.7 %all-to-all-start.1 = ((bf16[8,128,1536]{2,1,0:T(8,128)(2,1)}), bf16[8,128,1536]{2,1,0:T(8,128)(2,1)S(1)}, u32[]{:S(2)}, u32[]{:S(2)}) async-start(bf16[8,128,1536]{2,1,0:T(8,128)(2,1)} %copy-done.1), calls=%async_computation.1 | async-start | bytes 6291456 | tf_op jit(solution)/shard_map/all_to_all | solution.py:331
  53.1 13.8 %collective-permute-start.3 = (bf16[8,128,256]{2,1,0:T(8,128)(2,1)}, bf16[8,128,256]{2,1,0:T(8,128)(2,1)S(1)}, u32[]{:S(2)}, u32[]{:S(2)}) collective-permute-start(bf16[8,128,256]{2,1,0:T(8,128)(2,1)} %bitcast.6), channel_id=1, source_target_pairs={{0,2},{1,3},{2,0},{3,1},{4,6},{5,7},{6,4},{7,5},{8,10},{9,11},{10,... | collective-permute-start | bytes 1572872 | tf_op jit(solution)/shard_map/ppermute | solution.py:90
  54.6 15.8 %collective-permute-start.4 = (bf16[8,128,256]{2,1,0:T(8,128)(2,1)}, bf16[8,128,256]{2,1,0:T(8,128)(2,1)S(1)}, u32[]{:S(2)}, u32[]{:S(2)}) collective-permute-start(bf16[8,128,256]{2,1,0:T(8,128)(2,1)} %bitcast.7), channel_id=1, source_target_pairs={{0,1},{1,0},{2,3},{3,2},{4,5},{5,4},{6,7},{7,6},{8,9},{9,8},{10,11... | collective-permute-start | bytes 1572872 | tf_op jit(solution)/shard_map/ppermute | solution.py:90
  66.9 3.5 %collective-permute-start.5 = (bf16[8,128,256]{2,1,0:T(8,128)(2,1)S(1)}, bf16[8,128,256]{2,1,0:T(8,128)(2,1)S(1)}, u32[]{:S(2)}, u32[]{:S(2)}) collective-permute-start(bf16[8,128,256]{2,1,0:T(8,128)(2,1)S(1)} %collective-permute-done.3.refs_1_), channel_id=1, source_target_pairs={{0,1},{1,0},{2,3},{3,2},{4,5},{5,4},{6,7},{7,6},{8,9},{9,8},{10,11... | collective-permute-start | bytes 1572872 | tf_op jit(solution)/shard_map/ppermute | solution.py:90
  66.9 15.5 %collective-permute-start.10 = (bf16[128,512]{1,0:T(8,128)(2,1)}, bf16[128,512]{1,0:T(8,128)(2,1)S(1)}, u32[]{:S(2)}, u32[]{:S(2)}) collective-permute-start(bf16[128,512]{1,0:T(8,128)(2,1)} %copy-done.12), channel_id=1, source_target_pairs={{0,4},{4,0},{8,12},{12,8},{16,20},{20,16},{24,28},{28,24},{1,5},{5... | collective-permute-start | bytes 393224 | tf_op jit(solution)/shard_map/ppermute | solution.py:286
  68.6 40.5 %collective-permute-start.11 = (bf16[128,512]{1,0:T(8,128)(2,1)}, bf16[128,512]{1,0:T(8,128)(2,1)S(1)}, u32[]{:S(2)}, u32[]{:S(2)}) collective-permute-start(bf16[128,512]{1,0:T(8,128)(2,1)} %copy-done.11), channel_id=1, source_target_pairs={{0,8},{4,12},{8,0},{12,4},{16,24},{20,28},{24,16},{28,20},{1,9},{5... | collective-permute-start | bytes 393224 | tf_op jit(solution)/shard_map/ppermute | solution.py:286
  70.1 40.9 %collective-permute-start.12 = (bf16[128,512]{1,0:T(8,128)(2,1)}, bf16[128,512]{1,0:T(8,128)(2,1)S(1)}, u32[]{:S(2)}, u32[]{:S(2)}) collective-permute-start(bf16[128,512]{1,0:T(8,128)(2,1)} %copy-done.10), channel_id=1, source_target_pairs={{0,12},{4,8},{8,4},{12,0},{16,28},{20,24},{24,20},{28,16},{1,13},{... | collective-permute-start | bytes 393224 | tf_op jit(solution)/shard_map/ppermute | solution.py:286
  70.4 1.6 %copy-start.2 = (bf16[128,64,128]{2,1,0:T(8,128)(2,1)S(1)}, bf16[128,64,128]{2,1,0:T(8,128)(2,1)}, u32[]{:S(2)}) copy-start(bf16[128,64,128]{2,1,0:T(8,128)(2,1)} %q_ref.4) | copy-start | bytes 6291460
  72.0 1.0 copy-start.3
  73.0 38.0 %copy-start.7 = (bf16[128,512]{1,0:T(8,128)(2,1)S(1)}, bf16[128,512]{1,0:T(8,128)(2,1)}, u32[]{:S(2)}) copy-start(bf16[128,512]{1,0:T(8,128)(2,1)} %copy-done.6) | copy-start | bytes 393220
  73.0 38.0 %copy-start.9 = (bf16[128,512]{1,0:T(8,128)(2,1)S(1)}, bf16[128,512]{1,0:T(8,128)(2,1)}, u32[]{:S(2)}) copy-start(bf16[128,512]{1,0:T(8,128)(2,1)} %copy-done.8) | copy-start | bytes 393220

commit v4 on v3

--- a/solution.py
+++ b/solution.py
@@ -93,23 +93,29 @@
     return blocks, order
 
 
-HEAD_CHUNKS = ((0, 4), (4, 16))
+HEAD_CHUNKS = ((0, 4), (4, 8), (8, 16))
 
 
 def prepare_kernel(own_ref, q_ref, kv_ref, *refs, count, low, high, kv_low, kv_high):
-    out_refs, (q_scratch, kv_scratch) = refs[:-2], refs[-2:]
-    tokens, heads, size = q_ref.shape
+    out_refs, (q_in, kv_in, q_scratch, kv_scratch, sems) = refs[:-5], refs[-5:]
+    _, tokens, here, size = q_in.shape
     kv_heads = kv_ref.shape[1]
-    here, kv_here = heads // count, kv_heads // count
+    kv_here = kv_heads // count
+    goes = [k if len(out_refs) == 1 else own_ref[0] ^ k for k in range(count)]
+    copies = [pltpu.make_async_copy(kv_ref, kv_in, sems.at[count])]
+    for k in range(count):
+        heads = pl.ds(pl.multiple_of(goes[k] * here, here), here)
+        copies.append(pltpu.make_async_copy(q_ref.at[:, heads, :], q_in.at[k], sems.at[k]))
+    for copy in copies:
+        copy.start()
+    copies[0].wait()
     if kv_low < kv_high:
         for part in range(2):
-            split_heads(kv_scratch.at[part], kv_ref[:, :, part * size : (part + 1) * size])
+            split_heads(kv_scratch.at[part], kv_in[:, :, part * size : (part + 1) * size])
     for k in range(count):
-        if len(out_refs) == 1:
-            to, out_ref = k, out_refs[0].at[k]
-        else:
-            to, out_ref = own_ref[0] ^ k, out_refs[k]
-        split_heads(q_scratch, q_ref[:, pl.ds(to * here if len(out_refs) == 1 else pl.multiple_of(to * here, here), here), :])
+        out_ref = out_refs[0].at[k] if len(out_refs) == 1 else out_refs[k]
+        copies[k + 1].wait()
+        split_heads(q_scratch, q_in[k])
         at = 0
         for h in range(low, high):
             picked = q_scratch[pl.ds(h, tokens, stride=here), :]
@@ -117,7 +123,7 @@
             at += size
         for c in range(kv_low, kv_high):
             for part in range(2):
-                picked = kv_scratch[part, pl.ds(to * kv_here + c, tokens, stride=kv_heads), :]
+                picked = kv_scratch[part, pl.ds(goes[k] * kv_here + c, tokens, stride=kv_heads), :]
                 out_ref[:, at : at + size] = picked.astype(out_ref.dtype)
                 at += size
 
@@ -132,19 +138,22 @@
         out_shape=[jax.ShapeDtypeStruct((count, tokens, width), jnp.bfloat16)]
         if stacked
         else [jax.ShapeDtypeStruct((tokens, width), jnp.bfloat16)] * count,
-        in_specs=[pl.BlockSpec(memory_space=pltpu.SMEM), vmem, vmem],
+        in_specs=[pl.BlockSpec(memory_space=pltpu.SMEM), pl.BlockSpec(memory_space=pltpu.HBM), pl.BlockSpec(memory_space=pltpu.HBM)],
         out_specs=[vmem] if stacked else [vmem] * count,
         scratch_shapes=[
+            pltpu.VMEM((count, tokens, heads // count, size), queries.dtype),
+            pltpu.VMEM(pairs.shape, pairs.dtype),
             pltpu.VMEM((tokens * heads // count, size), jnp.float32),
             pltpu.VMEM((2, tokens * kv_heads, size), jnp.float32),
+            pltpu.SemaphoreType.DMA((count + 1,)),
         ],
-        compiler_params=pltpu.CompilerParams(vmem_limit_bytes=VMEM_LIMIT),
+        compiler_params=pltpu.CompilerParams(vmem_limit_bytes=60 * 1024 * 1024),
         cost_estimate=pl.CostEstimate(flops=0, bytes_accessed=0, transcendentals=0),
         name="prepare",
     )(own, queries, pairs)
 
 
-def slots_kernel(place_ref, lengths_ref, targets_ref, *refs, sets, outs, parts, scale):
+def slots_kernel(place_ref, lengths_ref, targets_ref, *refs, sets, outs, parts, skip, scale):
     count = sum(sets)
     sources, out_refs = refs[:count], refs[count : count + outs]
     q_ref, kv_ref, mixed_ref, start_ref, length_ref = refs[count + outs :]
@@ -166,7 +175,7 @@
                 at = pl.ds(pl.multiple_of((own ^ k) * ref.shape[0], ref.shape[0]), ref.shape[0])
                 to_ref[at, :] = ref[:, columns]
 
-    fill(q_ref, 0, slice(0, width))
+    fill(q_ref, 0, slice(skip, skip + width))
     for c, (home, column, _, _) in enumerate(parts):
         fill(kv_ref.at[c], home, slice(column, column + 2 * size))
     row = lax.broadcasted_iota(jnp.int32, (rows, 1), 0)
@@ -199,7 +208,7 @@
         out_ref[...] = picked.astype(out_ref.dtype)
 
 
-def slots_attend(place, lengths, targets, source_sets, parts, rows, width, span, size, split):
+def slots_attend(place, lengths, targets, source_sets, parts, skip, rows, width, span, size, split):
     slots = lengths.shape[0]
     smem = pl.BlockSpec(memory_space=pltpu.SMEM)
     vmem = pl.BlockSpec(memory_space=pltpu.VMEM)
@@ -209,7 +218,7 @@
     outs = slots if split else 1
     return pl.pallas_call(
         functools.partial(
-            slots_kernel, sets=sets, outs=outs, parts=parts, scale=LOG2_E / math.sqrt(size)
+            slots_kernel, sets=sets, outs=outs, parts=parts, skip=skip * size, scale=LOG2_E / math.sqrt(size)
         ),
         out_shape=[jax.ShapeDtypeStruct(shape, jnp.bfloat16)] * outs,
         in_specs=[smem, smem, smem] + [vmem] * len(sources),
@@ -227,33 +236,33 @@
     )(place, lengths, targets, *sources)
 
 
-def lay_kernel(place_ref, *refs, count, low):
-    pieces, (out_ref, sems) = refs[:count], refs[-2:]
-    width = pieces[0].shape[-1]
+def lay_kernel(place_ref, *refs, plan):
+    pieces, (out_ref, sems) = refs[: len(plan)], refs[-2:]
     copies = []
-    for k, ref in enumerate(pieces):
-        at = slice(low, low + width)
-        to = out_ref.at[:, :, at] if count == 1 else out_ref.at[place_ref[0] ^ k, :, at]
-        copies.append(pltpu.make_async_copy(ref, to, sems.at[k]))
-        copies[-1].start()
+    for ref, (k, runs) in zip(pieces, plan):
+        for column, low, width in runs:
+            from_ref = ref.at[..., column : column + width]
+            to = out_ref.at[:, :, low : low + width]
+            if k is not None:
+                to = out_ref.at[place_ref[0] ^ k, :, low : low + width]
+            copies.append(pltpu.make_async_copy(from_ref, to, sems.at[len(copies)]))
+            copies[-1].start()
     for copy in copies:
         copy.wait()
 
 
-def lay(place, pieces, low, shape, whole=None):
+def lay(place, pieces, plan, shape):
     anywhere = pl.BlockSpec(memory_space=pl.ANY)
-    operands = [place, *pieces] + ([] if whole is None else [whole])
     return pl.pallas_call(
-        functools.partial(lay_kernel, count=len(pieces), low=low),
+        functools.partial(lay_kernel, plan=plan),
         out_shape=jax.ShapeDtypeStruct(shape, jnp.bfloat16),
-        in_specs=[pl.BlockSpec(memory_space=pltpu.SMEM)] + [anywhere] * (len(operands) - 1),
+        in_specs=[pl.BlockSpec(memory_space=pltpu.SMEM)] + [anywhere] * len(pieces),
         out_specs=anywhere,
-        input_output_aliases={} if whole is None else {len(operands) - 1: 0},
-        scratch_shapes=[pltpu.SemaphoreType.DMA((len(pieces),))],
+        scratch_shapes=[pltpu.SemaphoreType.DMA((sum(len(runs) for _, runs in plan),))],
         compiler_params=pltpu.CompilerParams(vmem_limit_bytes=VMEM_LIMIT),
         cost_estimate=pl.CostEstimate(flops=0, bytes_accessed=0, transcendentals=0),
         name="lay",
-    )(*operands)
+    )(place, *pieces)
 
 
 def after(value, *earlier):
@@ -271,35 +280,33 @@
     columns = own_heads * size
     chunks = [(low * own_heads // 16, high * own_heads // 16) for low, high in HEAD_CHUNKS]
 
+    travels = [chunks[0], (chunks[1][0], chunks[-1][1])]
     sent, homes = [], {}
-    for i, (low, high) in enumerate(chunks):
+    for i, (low, high) in enumerate(travels):
         new = [c for c in range(own_kv) if c not in homes and c * share < high and low < (c + 1) * share]
         for j, c in enumerate(new):
             homes[c] = (i, (high - low + 2 * j) * size)
         kv_low, kv_high = (new[0], new[-1] + 1) if new else (0, 0)
         sent.append(
-            prepare(own, short_queries, short_pairs, head_count, low, high, kv_low, kv_high, stacked=i > 0)
+            prepare(own, short_queries, short_pairs, head_count, low, high, kv_low, kv_high, stacked=i == 1)
         )
 
-    def swap(blocks, axis, count):
-        return [blocks[0]] + [
-            lax.ppermute(blocks[k], axis, [(i, i ^ k) for i in range(count)]) for k in range(1, count)
-        ]
+    def hop(block, axis, k):
+        return lax.ppermute(block, axis, [(i, i ^ k) for i in range(lax.axis_size(axis))])
 
     pairs_by_head = jnp.swapaxes(long_pairs, 0, 1)
-    got, slots = [], []
-    split = [i == 0 and group_count <= 8 for i in range(len(chunks))]
+    split = [i != 1 and group_count <= 8 for i in range(len(chunks))]
+    half = group_count // 2
+    first = [sent[0][0]] + [hop(sent[0][k], "head", k) for k in range(1, head_count)]
+    rest = lax.all_to_all(sent[1][0], "head", split_axis=0, concat_axis=0, tiled=True)
+    got = [[after(block, sent[1], pairs_by_head) for block in first], [rest]]
+    slots, far = [], []
     for i, (low, high) in enumerate(chunks):
-        if i == 0:
-            moved = swap(sent[0], "head", head_count)
-            got.append([after(block, sent[1:], pairs_by_head) for block in moved])
-        else:
-            if i > 1:
-                sent[i] = [after(sent[i][0], slots[i - 2])]
-            moved = lax.all_to_all(sent[i][0], "head", split_axis=0, concat_axis=0, tiled=True)
-            got.append([after(moved, slots[i - 1])])
+        part = min(i, 1)
+        if i:
+            got[1] = [after(got[1][0], slots[i - 1], *far[:1] if i == 2 else [])]
         touched = [c for c in range(own_kv) if c * share < high and low < (c + 1) * share]
-        order = [i] + sorted({homes[c][0] for c in touched} - {i})
+        order = [part] + sorted({homes[c][0] for c in touched} - {part})
         parts = [
             (order.index(homes[c][0]), homes[c][1], max(low, c * share) - low, min(high, (c + 1) * share) - low)
             for c in touched
@@ -311,6 +318,7 @@
                 destinations,
                 [got[j] for j in order],
                 parts,
+                low - travels[part][0],
                 head_count * local_rows,
                 (high - low) * size,
                 span,
@@ -318,22 +326,31 @@
                 split[i],
             )
         )
-    shared, order = share_blocks(after(pairs_by_head, got[-1]), "head")
+        far.append([hop(slots[i][k], "grp", k) for k in range(half, group_count)] if split[i] else [])
+    shared, order = share_blocks(after(pairs_by_head, slots[-1]), "head")
     long_result = long_attend(own, after(long_queries, slots[-1]), shared, order)
-    whole, far = None, None
-    shape = (group_count, span, own_heads * size)
-    for i, (low, high) in enumerate(chunks):
-        if split[i]:
-            near = [after(piece, slots[-1]) for piece in slots[i][: group_count // 2]]
-            moved = swap([*near, *slots[i][group_count // 2 :]], "grp", group_count)
-            far = moved[group_count // 2 :]
-        else:
-            moved = [lax.all_to_all(after(slots[i][0], far), "grp", split_axis=0, concat_axis=0, tiled=True)]
-        if i == len(chunks) - 1:
-            moved = [after(moved[0], long_result)]
-        else:
-            moved[0] = after(moved[0], long_result)
-        whole = lay(place, moved, low * size, shape, whole)
+    pieces, plan = [], []
+    for i in range(len(chunks)):
+        low, width = chunks[i][0] * size, (chunks[i][1] - chunks[i][0]) * size
+        if not split[i]:
+            pieces.append(lax.all_to_all(slots[i][0], "grp", split_axis=0, concat_axis=0, tiled=True))
+            plan.append((None, [(0, low, width)]))
+            continue
+        pieces += [slots[i][0], *far[i]]
+        plan += [(k, [(0, low, width)]) for k in (0, *range(half, group_count))]
+    if any(split):
+        spread = [i for i in range(len(chunks)) if split[i]]
+        runs, column = [], 0
+        for i in spread:
+            low, width = chunks[i][0] * size, (chunks[i][1] - chunks[i][0]) * size
+            runs.append((column, low, width))
+            column += width
+        for k in range(1, half):
+            both = jnp.concatenate([slots[i][k] for i in spread], axis=1)
+            pieces.append(hop(both, "grp", k))
+            plan.append((k, runs))
+    pieces[0] = after(pieces[0], long_result)
+    whole = lay(place, pieces, plan, (group_count, span, own_heads * size))
     return long_result, whole.reshape(group_count * span, own_heads * size)
 
 

time: 128 us -> 126 us (0.984)
  the two profiles are of different devices: /device:TPU:0 before, /device:TPU:27 now
where the time goes in v4:
time: 126 us
  waiting for transfers between devices  46.5 us (37%)
  starting transfers between devices  39 us (31%)
  Pallas kernels  29.7 us (24%)
  local copies, waits for them, and re-layouts  9.57 us (8%)
    ppermute x14, waiting for transfers between devices, hop(): lax.ppermute(block, axis, [(i, i ^ k) for i in range(lax.axis_size(axis))])  35.4 us
    ppermute x14, starting transfers between devices, hop(): lax.ppermute(block, axis, [(i, i ^ k) for i in range(lax.axis_size(axis))])  24.7 us
    pallas_call x3, Pallas kernels, slots_attend(): pl.pallas_call(functools.partial(slots_kernel, sets=sets, outs=outs, part...  12.2 us
    unnamed x47, local copies, waits for them, and re-layouts  9.57 us
    pallas_call x1, Pallas kernels, long_attend(): pl.pallas_call(functools.partial(long_kernel, order=order, scale=LOG2_E /...  8.37 us
    all_to_all x1, waiting for transfers between devices, on_device(): lax.all_to_all(sent[1][0], 'head', split_axis=0, concat_axis=0, tiled=True)  7.03 us
    pallas_call x2, Pallas kernels, prepare(): pl.pallas_call(functools.partial(prepare_kernel, count=count, low=low, hi...  6.5 us
    all_to_all x1, starting transfers between devices, on_device(): lax.all_to_all(slots[i][0], 'grp', split_axis=0, concat_axis=0, tiled=True)  5.49 us
  transfers between devices with their start and end apart: 19, of which 7 were waited for; matrix products, arithmetic and copies ran while one was open for 1% of the time, Pallas kernels for 19%

profile of v4, /device:TPU:27, one launch (start us, length us, event | category | flops | bytes accessed | tf_op | source)
XLA Modules:
  0.0 126.0 jit_solution(8119818224770844049)
XLA Ops:
  0.6 2.6 %prepare.3 = (bf16[128,768]{1,0:T(8,128)(2,1)}, bf16[128,768]{1,0:T(8,128)(2,1)}, bf16[128,768]{1,0:T(8,128)(2,1)}, bf16[128,768]{1,0:T(8,128)(2,1)}) custom-call(s32[1]{0:T(128)} %bitcast.own_ref, bf16[128,64,128]{2,1,0:T(8,128)(2,1)} %q_ref.3, bf16[128,8,256]{2,1,0:T(8,128)(2,1)} %kv_ref.3), custom_call_target="tpu_custom_call" | custom-call | tf_op jit(solution)/shard_map/prepare/pallas_call | solution.py:136
  3.3 0.9 collective-permute-start.2
  4.1 1.2 collective-permute-start.1
  5.5 3.9 %prepare.2 = bf16[4,128,1792]{2,1,0:T(8,128)(2,1)} custom-call(s32[1]{0:T(128)} %bitcast.own_ref, bf16[128,64,128]{2,1,0:T(8,128)(2,1)} %q_ref.3, bf16[128,8,256]{2,1,0:T(8,128)(2,1)} %kv_ref.3), custom_call_target="tpu_custom_call" | custom-call | tf_op jit(solution)/shard_map/prepare/pallas_call | solution.py:136
  9.4 4.3 %all-to-all-start = ((bf16[4,128,1792]{2,1,0:T(8,128)(2,1)}), bf16[4,128,1792]{2,1,0:T(8,128)(2,1)S(1)}, u32[]{:S(2)}, u32[]{:S(2)}) async-start(bf16[4,128,1792]{2,1,0:T(8,128)(2,1)} %prepare.2), calls=%async_computation | async-start | bytes 3670016 | tf_op jit(solution)/shard_map/all_to_all | solution.py:301
  13.7 0.9 copy.10
  15.2 3.9 %slots_attend.3 = (bf16[128,512]{1,0:T(8,128)(2,1)S(1)}, bf16[128,512]{1,0:T(8,128)(2,1)S(1)}, bf16[128,512]{1,0:T(8,128)(2,1)S(1)}, bf16[128,512]{1,0:T(8,128)(...) custom-call(s32[2]{0:T(128)S(1)} %pad_add_fusion.place_ref, ...), custom_call_target="tpu_custom_call" | custom-call | flops 99999997952 | tf_op jit(solution)/shard_map/slots_attend/pallas_call | solution.py:219
  21.1 3.3 %collective-permute-start.4 = (bf16[128,512]{1,0:T(8,128)(2,1)}, bf16[128,512]{1,0:T(8,128)(2,1)S(1)}, u32[]{:S(2)}, u32[]{:S(2)}) collective-permute-start(bf16[128,512]{1,0:T(8,128)(2,1)} %get-tuple-element.44), channel_id=1, source_target_pairs={{0,20},{4,16},{8,28},{12,24},{16,4},{20,0},{24,12},{28,8},{1,21},{... | collective-permute-start | bytes 393224 | tf_op jit(solution)/shard_map/ppermute | solution.py:295
  24.4 3.2 %collective-permute-start.6 = (bf16[128,512]{1,0:T(8,128)(2,1)}, bf16[128,512]{1,0:T(8,128)(2,1)S(1)}, u32[]{:S(2)}, u32[]{:S(2)}) collective-permute-start(bf16[128,512]{1,0:T(8,128)(2,1)} %get-tuple-element.46), channel_id=1, source_target_pairs={{0,28},{4,24},{8,20},{12,16},{16,12},{20,8},{24,4},{28,0},{1,29},{... | collective-permute-start | bytes 393224 | tf_op jit(solution)/shard_map/ppermute | solution.py:295
  27.6 7.0 %all-to-all-done.refs_0_ = bf16[4,128,1792]{2,1,0:T(8,128)(2,1)S(1)} async-done(((bf16[4,128,1792]{2,1,0:T(8,128)(2,1)}), bf16[4,128,1792]{2,1,0:T(8,128)(2,1)S(1)}, u32[]{:S(2)}, u32[]{:S(2)}) %all-to-all-start) | async-done | bytes 1835040 | tf_op jit(solution)/shard_map/all_to_all | solution.py:301
  34.6 3.2 %slots_attend.4 = bf16[8,128,512]{2,1,0:T(8,128)(2,1)S(1)} custom-call(s32[2]{0:T(128)S(1)} %pad_add_fusion.place_ref, s32[8,8]{1,0:T(8,128)S(1)} %copy-done.20, s32[8,8]{1,0:T(8,128)S(1)} %copy-done.21, bf16[4,128,1792]{2,1,0:T(8,128)(2,1)S(1)} %all-to-all-done.refs_0_, bf16[128,768]{1,0:T(8,128)(2,1)S(1)} %copy-done.19, ...), custom_call_target="tpu_custom_call" | custom-call | flops 99999997952 | tf_op jit(solution)/shard_map/slots_attend/pallas_call | solution.py:219
  37.8 1.0 copy-done.2
  38.8 5.5 %all-to-all-start.1 = ((bf16[8,128,512]{2,1,0:T(8,128)(2,1)}), bf16[8,128,512]{2,1,0:T(8,128)(2,1)S(1)}, u32[]{:S(2)}, u32[]{:S(2)}) async-start(bf16[8,128,512]{2,1,0:T(8,128)(2,1)} %copy-done.2), calls=%async_computation.1 | async-start | bytes 2097152 | tf_op jit(solution)/shard_map/all_to_all | solution.py:336
  45.7 5.1 %slots_attend.5 = (bf16[128,1024]{1,0:T(8,128)(2,1)S(1)}, bf16[128,1024]{1,0:T(8,128)(2,1)S(1)}, bf16[128,1024]{1,0:T(8,128)(2,1)S(1)}, bf16[128,1024]{1,0:T(8,1...) custom-call(s32[2]{0:T(128)S(1)} %pad_add_fusion.place_ref, ...), custom_call_target="tpu_custom_call" | custom-call | flops 99999997952 | tf_op jit(solution)/shard_map/slots_attend/pallas_call | solution.py:219
  50.8 1.2 collective-permute-start.7
  52.0 2.4 %collective-permute-start.10 = (bf16[128,1024]{1,0:T(8,128)(2,1)S(1)}, bf16[128,1024]{1,0:T(8,128)(2,1)S(1)}, u32[]{:S(2)}, u32[]{:S(2)}) collective-permute-start(bf16[128,1024]{1,0:T(8,128)(2,1)S(1)} %get-tuple-element.53), channel_id=1, source_target_pairs={{0,16},{4,20},{8,24},{12,28},{16,0},{20,4},{24,8},{28,12},{1,17},{... | collective-permute-start | bytes 786440 | tf_op jit(solution)/shard_map/ppermute | solution.py:295
  54.4 3.3 %collective-permute-start.11 = (bf16[128,1024]{1,0:T(8,128)(2,1)S(1)}, bf16[128,1024]{1,0:T(8,128)(2,1)S(1)}, u32[]{:S(2)}, u32[]{:S(2)}) collective-permute-start(bf16[128,1024]{1,0:T(8,128)(2,1)S(1)} %get-tuple-element.54), channel_id=1, source_target_pairs={{0,20},{4,16},{8,28},{12,24},{16,4},{20,0},{24,12},{28,8},{1,21},{... | collective-permute-start | bytes 786440 | tf_op jit(solution)/shard_map/ppermute | solution.py:295
  57.7 1.2 collective-permute-start.8
  59.0 4.1 %collective-permute-done.7.refs_1_ = bf16[8,128,256]{2,1,0:T(8,128)(2,1)S(1)} collective-permute-done((bf16[8,128,256]{2,1,0:T(8,128)(2,1)S(1)}, bf16[8,128,256]{2,1,0:T(8,128)(2,1)S(1)}, u32[]{:S(2)}, u32[]{:S(2)}) %collective-permute-start.7) | collective-permute-done | bytes 524320 | tf_op jit(solution)/shard_map/ppermute | solution.py:90
  63.1 2.1 %collective-permute-start.9 = (bf16[8,128,256]{2,1,0:T(8,128)(2,1)S(1)}, bf16[8,128,256]{2,1,0:T(8,128)(2,1)S(1)}, u32[]{:S(2)}, u32[]{:S(2)}) collective-permute-start(bf16[8,128,256]{2,1,0:T(8,128)(2,1)S(1)} %collective-permute-done.7.refs_1_), channel_id=1, source_target_pairs={{0,1},{1,0},{2,3},{3,2},{4,5},{5,4},{6,7},{7,6},{8,9},{9,8},{10,11... | collective-permute-start | bytes 1572872 | tf_op jit(solution)/shard_map/ppermute | solution.py:90
  65.2 5.8 %collective-permute-start.16 = (bf16[128,1536]{1,0:T(8,128)(2,1)S(1)}, bf16[128,1536]{1,0:T(8,128)(2,1)S(1)}, u32[]{:S(2)}, u32[]{:S(2)}) collective-permute-start(bf16[128,1536]{1,0:T(8,128)(2,1)S(1)} %pad_maximum_fusion.2), channel_id=1, source_target_pairs={{0,12},{4,8},{8,4},{12,0},{16,28},{20,24},{24,20},{28,16},{1,13},{... | collective-permute-start | bytes 1179656 | tf_op jit(solution)/shard_map/ppermute | solution.py:295
  71.1 15.5 %collective-permute-done.10.refs_7_ = bf16[128,1024]{1,0:T(8,128)(2,1)S(1)} collective-permute-done((bf16[128,1024]{1,0:T(8,128)(2,1)S(1)}, bf16[128,1024]{1,0:T(8,128)(2,1)S(1)}, u32[]{:S(2)}, u32[]{:S(2)}) %collective-permute-start.10) | collective-permute-done | bytes 262176 | tf_op jit(solution)/shard_map/ppermute | solution.py:295
  86.6 7.7 %collective-permute-done.11.refs_8_ = bf16[128,1024]{1,0:T(8,128)(2,1)S(1)} collective-permute-done((bf16[128,1024]{1,0:T(8,128)(2,1)S(1)}, bf16[128,1024]{1,0:T(8,128)(2,1)S(1)}, u32[]{:S(2)}, u32[]{:S(2)}) %collective-permute-start.11) | collective-permute-done | bytes 262176 | tf_op jit(solution)/shard_map/ppermute | solution.py:295
  95.0 3.9 %collective-permute-start.13 = (bf16[128,1024]{1,0:T(8,128)(2,1)S(1)}, bf16[128,1024]{1,0:T(8,128)(2,1)S(1)}, u32[]{:S(2)}, u32[]{:S(2)}) collective-permute-start(bf16[128,1024]{1,0:T(8,128)(2,1)S(1)} %get-tuple-element.56), channel_id=1, source_target_pairs={{0,28},{4,24},{8,20},{12,16},{16,12},{20,8},{24,4},{28,0},{1,29},{... | collective-permute-start | bytes 786440 | tf_op jit(solution)/shard_map/ppermute | solution.py:295
  98.8 8.4 %long_attend.1 = bf16[128,8192]{1,0:T(8,128)(2,1)} custom-call(s32[1]{0:T(128)} %bitcast.own_ref, bf16[128,64,128]{2,1,0:T(8,128)(2,1)S(1)} %copy-done, bf16[8,128,256]{2,1,0:T(8,128)(2,1)S(1)} %bitcast.8, bf16[8,128,256]{2,1,0:T(8,128)(2,1)S(1)} %collective-permute-done.7.refs_1_, bf16[8,128,256]{2,1,0:T(8,128)(2,1)S(1)} %collective-permute-done.8.refs_2_, ...), custom_call_target="tpu_custom_call" | custom-call | tf_op jit(solution)/shard_map/long_attend/pallas_call | solution.py:62
  107.2 2.9 %collective-permute-done.13.refs_10_ = bf16[128,1024]{1,0:T(8,128)(2,1)S(1)} collective-permute-done((bf16[128,1024]{1,0:T(8,128)(2,1)S(1)}, bf16[128,1024]{1,0:T(8,128)(2,1)S(1)}, u32[]{:S(2)}, u32[]{:S(2)}) %collective-permute-start.13) | collective-permute-done | bytes 262176 | tf_op jit(solution)/shard_map/ppermute | solution.py:295
  110.8 8.7 %collective-permute-done.15.refs_12_ = bf16[128,1536]{1,0:T(8,128)(2,1)S(1)} collective-permute-done((bf16[128,1536]{1,0:T(8,128)(2,1)S(1)}, bf16[128,1536]{1,0:T(8,128)(2,1)S(1)}, u32[]{:S(2)}, u32[]{:S(2)}) %collective-permute-start.15) | collective-permute-done | bytes 393248 | tf_op jit(solution)/shard_map/ppermute | solution.py:295
  119.5 0.9 copy-done.4
  120.5 0.9 copy-done.8
  121.4 0.9 copy-done.10
  122.3 0.9 copy-done.12
  123.2 2.7 %lay.1 = bf16[8,128,2048]{2,1,0:T(8,128)(2,1)} custom-call(s32[2]{0:T(128)S(1)} %pad_add_fusion.place_ref, bf16[128,512]{1,0:T(8,128)(2,1)S(1)} %get-tuple-element.59.refs_0_, bf16[128,512]{1,0:T(8,128)(2,1)S(1)} %copy-done.6, bf16[128,512]{1,0:T(8,128)(2,1)S(1)} %copy-done.8, bf16[128,512]{1,0:T(8,128)(2,1)S(1)} %copy-done.10, ...), custom_call_target="tpu_custom_call" | custom-call | tf_op jit(solution)/shard_map/lay/pallas_call | solution.py:256
  (64 shorter events, 5.5 us)
Async XLA Ops:
  3.3 11.4 %collective-permute-start.2 = (bf16[128,768]{1,0:T(8,128)(2,1)}, bf16[128,768]{1,0:T(8,128)(2,1)S(1)}, u32[]{:S(2)}, u32[]{:S(2)}) collective-permute-start(bf16[128,768]{1,0:T(8,128)(2,1)} %get-tuple-element.37), channel_id=1, source_target_pairs={{0,3},{1,2},{2,1},{3,0},{4,7},{5,6},{6,5},{7,4},{8,11},{9,10},{10,... | collective-permute-start | bytes 589832 | tf_op jit(solution)/shard_map/ppermute | solution.py:295
  4.1 11.1 %collective-permute-start.1 = (bf16[128,768]{1,0:T(8,128)(2,1)}, bf16[128,768]{1,0:T(8,128)(2,1)S(1)}, u32[]{:S(2)}, u32[]{:S(2)}) collective-permute-start(bf16[128,768]{1,0:T(8,128)(2,1)} %get-tuple-element.35), channel_id=1, source_target_pairs={{0,2},{1,3},{2,0},{3,1},{4,6},{5,7},{6,4},{7,5},{8,10},{9,11},{10,... | collective-permute-start | bytes 589832 | tf_op jit(solution)/shard_map/ppermute | solution.py:295
  5.4 9.9 %collective-permute-start = (bf16[128,768]{1,0:T(8,128)(2,1)}, bf16[128,768]{1,0:T(8,128)(2,1)S(1)}, u32[]{:S(2)}, u32[]{:S(2)}) collective-permute-start(bf16[128,768]{1,0:T(8,128)(2,1)} %get-tuple-element.33), channel_id=1, source_target_pairs={{0,1},{1,0},{2,3},{3,2},{4,5},{5,4},{6,7},{7,6},{8,9},{9,8},{10,11... | collective-permute-start | bytes 589832 | tf_op jit(solution)/shard_map/ppermute | solution.py:295
  9.4 4.3 %copy-start.22 = (bf16[128,8,256]{2,1,0:T(8,128)(2,1)S(1)}, bf16[128,8,256]{2,1,0:T(8,128)(2,1)}, u32[]{:S(2)}) copy-start(bf16[128,8,256]{2,1,0:T(8,128)(2,1)} %param.7) | copy-start | bytes 1572868
  9.4 5.8 %copy-start.19 = (bf16[128,768]{1,0:T(8,128)(2,1)S(1)}, bf16[128,768]{1,0:T(8,128)(2,1)}, u32[]{:S(2)}) copy-start(bf16[128,768]{1,0:T(8,128)(2,1)} %get-tuple-element.32.refs_0_.refs_1_) | copy-start | bytes 589828
  9.4 5.8 %copy-start.20 = (s32[8,8]{1,0:T(8,128)S(1)}, s32[8,8]{1,0:T(8,128)}, u32[]{:S(2)}) copy-start(s32[8,8]{1,0:T(8,128)} %lengths_ref.5) | copy-start | bytes 772
  9.4 5.8 %copy-start.21 = (s32[8,8]{1,0:T(8,128)S(1)}, s32[8,8]{1,0:T(8,128)}, u32[]{:S(2)}) copy-start(s32[8,8]{1,0:T(8,128)} %targets_ref.5) | copy-start | bytes 772
  9.4 25.2 %all-to-all-start = ((bf16[4,128,1792]{2,1,0:T(8,128)(2,1)}), bf16[4,128,1792]{2,1,0:T(8,128)(2,1)S(1)}, u32[]{:S(2)}, u32[]{:S(2)}) async-start(bf16[4,128,1792]{2,1,0:T(8,128)(2,1)} %prepare.2), calls=%async_computation | async-start | bytes 3670016 | tf_op jit(solution)/shard_map/all_to_all | solution.py:301
  21.1 23.2 %collective-permute-start.3 = (bf16[128,512]{1,0:T(8,128)(2,1)}, bf16[128,512]{1,0:T(8,128)(2,1)S(1)}, u32[]{:S(2)}, u32[]{:S(2)}) collective-permute-start(bf16[128,512]{1,0:T(8,128)(2,1)} %get-tuple-element.43), channel_id=1, source_target_pairs={{0,16},{4,20},{8,24},{12,28},{16,0},{20,4},{24,8},{28,12},{1,17},{... | collective-permute-start | bytes 393224 | tf_op jit(solution)/shard_map/ppermute | solution.py:295
  21.1 23.9 %collective-permute-start.4 = (bf16[128,512]{1,0:T(8,128)(2,1)}, bf16[128,512]{1,0:T(8,128)(2,1)S(1)}, u32[]{:S(2)}, u32[]{:S(2)}) collective-permute-start(bf16[128,512]{1,0:T(8,128)(2,1)} %get-tuple-element.44), channel_id=1, source_target_pairs={{0,20},{4,16},{8,28},{12,24},{16,4},{20,0},{24,12},{28,8},{1,21},{... | collective-permute-start | bytes 393224 | tf_op jit(solution)/shard_map/ppermute | solution.py:295
  24.4 21.2 %collective-permute-start.5 = (bf16[128,512]{1,0:T(8,128)(2,1)}, bf16[128,512]{1,0:T(8,128)(2,1)S(1)}, u32[]{:S(2)}, u32[]{:S(2)}) collective-permute-start(bf16[128,512]{1,0:T(8,128)(2,1)} %get-tuple-element.45), channel_id=1, source_target_pairs={{0,24},{4,28},{8,16},{12,20},{16,8},{20,12},{24,0},{28,4},{1,25},{... | collective-permute-start | bytes 393224 | tf_op jit(solution)/shard_map/ppermute | solution.py:295
  24.4 21.2 %collective-permute-start.6 = (bf16[128,512]{1,0:T(8,128)(2,1)}, bf16[128,512]{1,0:T(8,128)(2,1)S(1)}, u32[]{:S(2)}, u32[]{:S(2)}) collective-permute-start(bf16[128,512]{1,0:T(8,128)(2,1)} %get-tuple-element.46), channel_id=1, source_target_pairs={{0,28},{4,24},{8,20},{12,16},{16,12},{20,8},{24,4},{28,0},{1,29},{... | collective-permute-start | bytes 393224 | tf_op jit(solution)/shard_map/ppermute | solution.py:295
  37.8 1.0 copy-start.2
  38.8 80.7 %all-to-all-start.1 = ((bf16[8,128,512]{2,1,0:T(8,128)(2,1)}), bf16[8,128,512]{2,1,0:T(8,128)(2,1)S(1)}, u32[]{:S(2)}, u32[]{:S(2)}) async-start(bf16[8,128,512]{2,1,0:T(8,128)(2,1)} %copy-done.2), calls=%async_computation.1 | async-start | bytes 2097152 | tf_op jit(solution)/shard_map/all_to_all | solution.py:336
  44.3 6.5 %copy-start.1 = (bf16[128,8,256]{2,0,1:T(8,128)(2,1)S(1)}, bf16[128,8,256]{2,0,1:T(8,128)(2,1)}, u32[]{:S(2)}) copy-start(bf16[128,8,256]{2,0,1:T(8,128)(2,1)} %copy.10) | copy-start | bytes 1572868
  44.3 14.6 %copy-start.18 = (bf16[128,512]{1,0:T(8,128)(2,1)S(1)}, bf16[128,512]{1,0:T(8,128)(2,1)}, u32[]{:S(2)}) copy-start(bf16[128,512]{1,0:T(8,128)(2,1)} %copy-done.17) | copy-start | bytes 393220
  44.3 20.9 %copy-start.16 = (bf16[128,512]{1,0:T(8,128)(2,1)S(1)}, bf16[128,512]{1,0:T(8,128)(2,1)}, u32[]{:S(2)}) copy-start(bf16[128,512]{1,0:T(8,128)(2,1)} %copy-done.15) | copy-start | bytes 393220
  44.3 26.8 %copy-start.14 = (bf16[128,512]{1,0:T(8,128)(2,1)S(1)}, bf16[128,512]{1,0:T(8,128)(2,1)}, u32[]{:S(2)}) copy-start(bf16[128,512]{1,0:T(8,128)(2,1)} %copy-done.13) | copy-start | bytes 393220
  45.6 5.1 %copy-start.9 = (bf16[128,512]{1,0:T(8,128)(2,1)}, bf16[128,512]{1,0:T(8,128)(2,1)S(1)}, u32[]{:S(2)}) copy-start(bf16[128,512]{1,0:T(8,128)(2,1)S(1)} %collective-permute-done.5.refs_3_) | copy-start | bytes 393220
  45.7 5.1 %copy-start.11 = (bf16[128,512]{1,0:T(8,128)(2,1)}, bf16[128,512]{1,0:T(8,128)(2,1)S(1)}, u32[]{:S(2)}) copy-start(bf16[128,512]{1,0:T(8,128)(2,1)S(1)} %collective-permute-done.6.refs_4_) | copy-start | bytes 393220
  50.8 48.1 %copy-start = (bf16[128,64,128]{2,1,0:T(8,128)(2,1)S(1)}, bf16[128,64,128]{2,1,0:T(8,128)(2,1)}, u32[]{:S(2)}) copy-start(bf16[128,64,128]{2,1,0:T(8,128)(2,1)} %q_ref.4) | copy-start | bytes 6291460
  50.8 12.3 %collective-permute-start.7 = (bf16[8,128,256]{2,1,0:T(8,128)(2,1)S(1)}, bf16[8,128,256]{2,1,0:T(8,128)(2,1)S(1)}, u32[]{:S(2)}, u32[]{:S(2)}) collective-permute-start(bf16[8,128,256]{2,1,0:T(8,128)(2,1)S(1)} %bitcast.6), channel_id=1, source_target_pairs={{0,2},{1,3},{2,0},{3,1},{4,6},{5,7},{6,4},{7,5},{8,10},{9,11},{10,... | collective-permute-start | bytes 1572872 | tf_op jit(solution)/shard_map/ppermute | solution.py:90
  52.0 34.6 %collective-permute-start.10 = (bf16[128,1024]{1,0:T(8,128)(2,1)S(1)}, bf16[128,1024]{1,0:T(8,128)(2,1)S(1)}, u32[]{:S(2)}, u32[]{:S(2)}) collective-permute-start(bf16[128,1024]{1,0:T(8,128)(2,1)S(1)} %get-tuple-element.53), channel_id=1, source_target_pairs={{0,16},{4,20},{8,24},{12,28},{16,0},{20,4},{24,8},{28,12},{1,17},{... | collective-permute-start | bytes 786440 | tf_op jit(solution)/shard_map/ppermute | solution.py:295
  54.4 40.0 %collective-permute-start.11 = (bf16[128,1024]{1,0:T(8,128)(2,1)S(1)}, bf16[128,1024]{1,0:T(8,128)(2,1)S(1)}, u32[]{:S(2)}, u32[]{:S(2)}) collective-permute-start(bf16[128,1024]{1,0:T(8,128)(2,1)S(1)} %get-tuple-element.54), channel_id=1, source_target_pairs={{0,20},{4,16},{8,28},{12,24},{16,4},{20,0},{24,12},{28,8},{1,21},{... | collective-permute-start | bytes 786440 | tf_op jit(solution)/shard_map/ppermute | solution.py:295
  57.7 36.7 %collective-permute-start.8 = (bf16[8,128,256]{2,1,0:T(8,128)(2,1)S(1)}, bf16[8,128,256]{2,1,0:T(8,128)(2,1)S(1)}, u32[]{:S(2)}, u32[]{:S(2)}) collective-permute-start(bf16[8,128,256]{2,1,0:T(8,128)(2,1)S(1)} %bitcast.7), channel_id=1, source_target_pairs={{0,1},{1,0},{2,3},{3,2},{4,5},{5,4},{6,7},{7,6},{8,9},{9,8},{10,11... | collective-permute-start | bytes 1572872 | tf_op jit(solution)/shard_map/ppermute | solution.py:90
  63.1 31.9 %collective-permute-start.9 = (bf16[8,128,256]{2,1,0:T(8,128)(2,1)S(1)}, bf16[8,128,256]{2,1,0:T(8,128)(2,1)S(1)}, u32[]{:S(2)}, u32[]{:S(2)}) collective-permute-start(bf16[8,128,256]{2,1,0:T(8,128)(2,1)S(1)} %collective-permute-done.7.refs_1_), channel_id=1, source_target_pairs={{0,1},{1,0},{2,3},{3,2},{4,5},{5,4},{6,7},{7,6},{8,9},{9,8},{10,11... | collective-permute-start | bytes 1572872 | tf_op jit(solution)/shard_map/ppermute | solution.py:90
  65.2 45.6 %collective-permute-start.16 = (bf16[128,1536]{1,0:T(8,128)(2,1)S(1)}, bf16[128,1536]{1,0:T(8,128)(2,1)S(1)}, u32[]{:S(2)}, u32[]{:S(2)}) collective-permute-start(bf16[128,1536]{1,0:T(8,128)(2,1)S(1)} %pad_maximum_fusion.2), channel_id=1, source_target_pairs={{0,12},{4,8},{8,4},{12,0},{16,28},{20,24},{24,20},{28,16},{1,13},{... | collective-permute-start | bytes 1179656 | tf_op jit(solution)/shard_map/ppermute | solution.py:295
  71.1 48.4 %copy-start.6 = (bf16[128,512]{1,0:T(8,128)(2,1)S(1)}, bf16[128,512]{1,0:T(8,128)(2,1)}, u32[]{:S(2)}) copy-start(bf16[128,512]{1,0:T(8,128)(2,1)} %copy-done.5) | copy-start | bytes 393220
  86.6 32.9 %collective-permute-start.15 = (bf16[128,1536]{1,0:T(8,128)(2,1)S(1)}, bf16[128,1536]{1,0:T(8,128)(2,1)S(1)}, u32[]{:S(2)}, u32[]{:S(2)}) collective-permute-start(bf16[128,1536]{1,0:T(8,128)(2,1)S(1)} %pad_maximum_fusion.1), channel_id=1, source_target_pairs={{0,8},{4,12},{8,0},{12,4},{16,24},{20,28},{24,16},{28,20},{1,9},{5... | collective-permute-start | bytes 1179656 | tf_op jit(solution)/shard_map/ppermute | solution.py:295
  94.4 25.1 %collective-permute-start.14 = (bf16[128,1536]{1,0:T(8,128)(2,1)S(1)}, bf16[128,1536]{1,0:T(8,128)(2,1)S(1)}, u32[]{:S(2)}, u32[]{:S(2)}) collective-permute-start(bf16[128,1536]{1,0:T(8,128)(2,1)S(1)} %pad_maximum_fusion), channel_id=1, source_target_pairs={{0,4},{4,0},{8,12},{12,8},{16,20},{20,16},{24,28},{28,24},{1,5},{5... | collective-permute-start | bytes 1179656 | tf_op jit(solution)/shard_map/ppermute | solution.py:295
  94.4 12.8 %collective-permute-start.12 = (bf16[128,1024]{1,0:T(8,128)(2,1)S(1)}, bf16[128,1024]{1,0:T(8,128)(2,1)S(1)}, u32[]{:S(2)}, u32[]{:S(2)}) collective-permute-start(bf16[128,1024]{1,0:T(8,128)(2,1)S(1)} %get-tuple-element.55), channel_id=1, source_target_pairs={{0,24},{4,28},{8,16},{12,20},{16,8},{20,12},{24,0},{28,4},{1,25},{... | collective-permute-start | bytes 786440 | tf_op jit(solution)/shard_map/ppermute | solution.py:295
  95.0 15.1 %collective-permute-start.13 = (bf16[128,1024]{1,0:T(8,128)(2,1)S(1)}, bf16[128,1024]{1,0:T(8,128)(2,1)S(1)}, u32[]{:S(2)}, u32[]{:S(2)}) collective-permute-start(bf16[128,1024]{1,0:T(8,128)(2,1)S(1)} %get-tuple-element.56), channel_id=1, source_target_pairs={{0,28},{4,24},{8,20},{12,16},{16,12},{20,8},{24,4},{28,0},{1,29},{... | collective-permute-start | bytes 786440 | tf_op jit(solution)/shard_map/ppermute | solution.py:295
  (10 other events, 7.7 us)

commit v5 on v4

--- a/solution.py
+++ b/solution.py
@@ -101,6 +101,7 @@
     _, tokens, here, size = q_in.shape
     kv_heads = kv_ref.shape[1]
     kv_here = kv_heads // count
+    tile_low, tile_high = low // 8 * 8, min(here, -(-high // 8) * 8)
     goes = [k if len(out_refs) == 1 else own_ref[0] ^ k for k in range(count)]
     copies = [pltpu.make_async_copy(kv_ref, kv_in, sems.at[count])]
     for k in range(count):
@@ -115,10 +116,10 @@
     for k in range(count):
         out_ref = out_refs[0].at[k] if len(out_refs) == 1 else out_refs[k]
         copies[k + 1].wait()
-        split_heads(q_scratch, q_in[k])
+        split_heads(q_scratch, q_in[k, :, tile_low:tile_high, :])
         at = 0
         for h in range(low, high):
-            picked = q_scratch[pl.ds(h, tokens, stride=here), :]
+            picked = q_scratch[pl.ds(h - tile_low, tokens, stride=tile_high - tile_low), :]
             out_ref[:, at : at + size] = picked.astype(out_ref.dtype)
             at += size
         for c in range(kv_low, kv_high):
@@ -143,7 +144,7 @@
         scratch_shapes=[
             pltpu.VMEM((count, tokens, heads // count, size), queries.dtype),
             pltpu.VMEM(pairs.shape, pairs.dtype),
-            pltpu.VMEM((tokens * heads // count, size), jnp.float32),
+            pltpu.VMEM((tokens * (min(heads // count, -(-high // 8) * 8) - low // 8 * 8), size), jnp.float32),
             pltpu.VMEM((2, tokens * kv_heads, size), jnp.float32),
             pltpu.SemaphoreType.DMA((count + 1,)),
         ],

time: 126 us -> 126 us (level)
  no operation moved by 1% of the time
where the time goes in v5:
time: 126 us
  waiting for transfers between devices  46.5 us (37%)
  starting transfers between devices  39.1 us (31%)
  Pallas kernels  29.7 us (24%)
  local copies, waits for them, and re-layouts  9.57 us (8%)
    ppermute x14, waiting for transfers between devices, hop(): lax.ppermute(block, axis, [(i, i ^ k) for i in range(lax.axis_size(axis))])  35.4 us
    ppermute x14, starting transfers between devices, hop(): lax.ppermute(block, axis, [(i, i ^ k) for i in range(lax.axis_size(axis))])  24.8 us
    pallas_call x3, Pallas kernels, slots_attend(): pl.pallas_call(functools.partial(slots_kernel, sets=sets, outs=outs, part...  12.2 us
    unnamed x47, local copies, waits for them, and re-layouts  9.57 us
    pallas_call x1, Pallas kernels, long_attend(): pl.pallas_call(functools.partial(long_kernel, order=order, scale=LOG2_E /...  8.37 us
    all_to_all x1, waiting for transfers between devices, on_device(): lax.all_to_all(sent[1][0], 'head', split_axis=0, concat_axis=0, tiled=True)  7.03 us
    pallas_call x2, Pallas kernels, prepare(): pl.pallas_call(functools.partial(prepare_kernel, count=count, low=low, hi...  6.5 us
    all_to_all x1, starting transfers between devices, on_device(): lax.all_to_all(slots[i][0], 'grp', split_axis=0, concat_axis=0, tiled=True)  5.49 us
  transfers between devices with their start and end apart: 19, of which 7 were waited for; matrix products, arithmetic and copies ran while one was open for 1% of the time, Pallas kernels for 19%

profile of v5, /device:TPU:27, one launch (start us, length us, event | category | flops | bytes accessed | tf_op | source)
XLA Modules:
  0.0 126.0 jit_solution(6867500162649518025)
XLA Ops:
  0.6 2.6 %prepare.3 = (bf16[128,768]{1,0:T(8,128)(2,1)}, bf16[128,768]{1,0:T(8,128)(2,1)}, bf16[128,768]{1,0:T(8,128)(2,1)}, bf16[128,768]{1,0:T(8,128)(2,1)}) custom-call(s32[1]{0:T(128)} %bitcast.own_ref, bf16[128,64,128]{2,1,0:T(8,128)(2,1)} %q_ref.3, bf16[128,8,256]{2,1,0:T(8,128)(2,1)} %kv_ref.3), custom_call_target="tpu_custom_call" | custom-call | tf_op jit(solution)/shard_map/prepare/pallas_call | solution.py:137
  3.3 0.9 collective-permute-start.2
  4.1 1.2 collective-permute-start.1
  5.5 3.9 %prepare.2 = bf16[4,128,1792]{2,1,0:T(8,128)(2,1)} custom-call(s32[1]{0:T(128)} %bitcast.own_ref, bf16[128,64,128]{2,1,0:T(8,128)(2,1)} %q_ref.3, bf16[128,8,256]{2,1,0:T(8,128)(2,1)} %kv_ref.3), custom_call_target="tpu_custom_call" | custom-call | tf_op jit(solution)/shard_map/prepare/pallas_call | solution.py:137
  9.4 4.3 %all-to-all-start = ((bf16[4,128,1792]{2,1,0:T(8,128)(2,1)}), bf16[4,128,1792]{2,1,0:T(8,128)(2,1)S(1)}, u32[]{:S(2)}, u32[]{:S(2)}) async-start(bf16[4,128,1792]{2,1,0:T(8,128)(2,1)} %prepare.2), calls=%async_computation | async-start | bytes 3670016 | tf_op jit(solution)/shard_map/all_to_all | solution.py:302
  13.7 0.9 copy.10
  15.2 3.9 %slots_attend.3 = (bf16[128,512]{1,0:T(8,128)(2,1)S(1)}, bf16[128,512]{1,0:T(8,128)(2,1)S(1)}, bf16[128,512]{1,0:T(8,128)(2,1)S(1)}, bf16[128,512]{1,0:T(8,128)(...) custom-call(s32[2]{0:T(128)S(1)} %pad_add_fusion.place_ref, ...), custom_call_target="tpu_custom_call" | custom-call | flops 99999997952 | tf_op jit(solution)/shard_map/slots_attend/pallas_call | solution.py:220
  21.1 3.3 %collective-permute-start.4 = (bf16[128,512]{1,0:T(8,128)(2,1)}, bf16[128,512]{1,0:T(8,128)(2,1)S(1)}, u32[]{:S(2)}, u32[]{:S(2)}) collective-permute-start(bf16[128,512]{1,0:T(8,128)(2,1)} %get-tuple-element.44), channel_id=1, source_target_pairs={{0,20},{4,16},{8,28},{12,24},{16,4},{20,0},{24,12},{28,8},{1,21},{... | collective-permute-start | bytes 393224 | tf_op jit(solution)/shard_map/ppermute | solution.py:296
  24.4 3.2 %collective-permute-start.6 = (bf16[128,512]{1,0:T(8,128)(2,1)}, bf16[128,512]{1,0:T(8,128)(2,1)S(1)}, u32[]{:S(2)}, u32[]{:S(2)}) collective-permute-start(bf16[128,512]{1,0:T(8,128)(2,1)} %get-tuple-element.46), channel_id=1, source_target_pairs={{0,28},{4,24},{8,20},{12,16},{16,12},{20,8},{24,4},{28,0},{1,29},{... | collective-permute-start | bytes 393224 | tf_op jit(solution)/shard_map/ppermute | solution.py:296
  27.6 7.0 %all-to-all-done.refs_0_ = bf16[4,128,1792]{2,1,0:T(8,128)(2,1)S(1)} async-done(((bf16[4,128,1792]{2,1,0:T(8,128)(2,1)}), bf16[4,128,1792]{2,1,0:T(8,128)(2,1)S(1)}, u32[]{:S(2)}, u32[]{:S(2)}) %all-to-all-start) | async-done | bytes 1835040 | tf_op jit(solution)/shard_map/all_to_all | solution.py:302
  34.6 3.2 %slots_attend.4 = bf16[8,128,512]{2,1,0:T(8,128)(2,1)S(1)} custom-call(s32[2]{0:T(128)S(1)} %pad_add_fusion.place_ref, s32[8,8]{1,0:T(8,128)S(1)} %copy-done.20, s32[8,8]{1,0:T(8,128)S(1)} %copy-done.21, bf16[4,128,1792]{2,1,0:T(8,128)(2,1)S(1)} %all-to-all-done.refs_0_, bf16[128,768]{1,0:T(8,128)(2,1)S(1)} %copy-done.19, ...), custom_call_target="tpu_custom_call" | custom-call | flops 99999997952 | tf_op jit(solution)/shard_map/slots_attend/pallas_call | solution.py:220
  37.8 1.0 copy-done.2
  38.8 5.5 %all-to-all-start.1 = ((bf16[8,128,512]{2,1,0:T(8,128)(2,1)}), bf16[8,128,512]{2,1,0:T(8,128)(2,1)S(1)}, u32[]{:S(2)}, u32[]{:S(2)}) async-start(bf16[8,128,512]{2,1,0:T(8,128)(2,1)} %copy-done.2), calls=%async_computation.1 | async-start | bytes 2097152 | tf_op jit(solution)/shard_map/all_to_all | solution.py:337
  45.7 5.1 %slots_attend.5 = (bf16[128,1024]{1,0:T(8,128)(2,1)S(1)}, bf16[128,1024]{1,0:T(8,128)(2,1)S(1)}, bf16[128,1024]{1,0:T(8,128)(2,1)S(1)}, bf16[128,1024]{1,0:T(8,1...) custom-call(s32[2]{0:T(128)S(1)} %pad_add_fusion.place_ref, ...), custom_call_target="tpu_custom_call" | custom-call | flops 99999997952 | tf_op jit(solution)/shard_map/slots_attend/pallas_call | solution.py:220
  50.8 1.2 collective-permute-start.7
  52.0 2.4 %collective-permute-start.10 = (bf16[128,1024]{1,0:T(8,128)(2,1)S(1)}, bf16[128,1024]{1,0:T(8,128)(2,1)S(1)}, u32[]{:S(2)}, u32[]{:S(2)}) collective-permute-start(bf16[128,1024]{1,0:T(8,128)(2,1)S(1)} %get-tuple-element.53), channel_id=1, source_target_pairs={{0,16},{4,20},{8,24},{12,28},{16,0},{20,4},{24,8},{28,12},{1,17},{... | collective-permute-start | bytes 786440 | tf_op jit(solution)/shard_map/ppermute | solution.py:296
  54.4 3.3 %collective-permute-start.11 = (bf16[128,1024]{1,0:T(8,128)(2,1)S(1)}, bf16[128,1024]{1,0:T(8,128)(2,1)S(1)}, u32[]{:S(2)}, u32[]{:S(2)}) collective-permute-start(bf16[128,1024]{1,0:T(8,128)(2,1)S(1)} %get-tuple-element.54), channel_id=1, source_target_pairs={{0,20},{4,16},{8,28},{12,24},{16,4},{20,0},{24,12},{28,8},{1,21},{... | collective-permute-start | bytes 786440 | tf_op jit(solution)/shard_map/ppermute | solution.py:296
  57.7 1.2 collective-permute-start.8
  59.0 4.1 %collective-permute-done.7.refs_1_ = bf16[8,128,256]{2,1,0:T(8,128)(2,1)S(1)} collective-permute-done((bf16[8,128,256]{2,1,0:T(8,128)(2,1)S(1)}, bf16[8,128,256]{2,1,0:T(8,128)(2,1)S(1)}, u32[]{:S(2)}, u32[]{:S(2)}) %collective-permute-start.7) | collective-permute-done | bytes 524320 | tf_op jit(solution)/shard_map/ppermute | solution.py:90
  63.1 2.1 %collective-permute-start.9 = (bf16[8,128,256]{2,1,0:T(8,128)(2,1)S(1)}, bf16[8,128,256]{2,1,0:T(8,128)(2,1)S(1)}, u32[]{:S(2)}, u32[]{:S(2)}) collective-permute-start(bf16[8,128,256]{2,1,0:T(8,128)(2,1)S(1)} %collective-permute-done.7.refs_1_), channel_id=1, source_target_pairs={{0,1},{1,0},{2,3},{3,2},{4,5},{5,4},{6,7},{7,6},{8,9},{9,8},{10,11... | collective-permute-start | bytes 1572872 | tf_op jit(solution)/shard_map/ppermute | solution.py:90
  65.2 5.8 %collective-permute-start.16 = (bf16[128,1536]{1,0:T(8,128)(2,1)S(1)}, bf16[128,1536]{1,0:T(8,128)(2,1)S(1)}, u32[]{:S(2)}, u32[]{:S(2)}) collective-permute-start(bf16[128,1536]{1,0:T(8,128)(2,1)S(1)} %pad_maximum_fusion.2), channel_id=1, source_target_pairs={{0,12},{4,8},{8,4},{12,0},{16,28},{20,24},{24,20},{28,16},{1,13},{... | collective-permute-start | bytes 1179656 | tf_op jit(solution)/shard_map/ppermute | solution.py:296
  71.1 15.5 %collective-permute-done.10.refs_7_ = bf16[128,1024]{1,0:T(8,128)(2,1)S(1)} collective-permute-done((bf16[128,1024]{1,0:T(8,128)(2,1)S(1)}, bf16[128,1024]{1,0:T(8,128)(2,1)S(1)}, u32[]{:S(2)}, u32[]{:S(2)}) %collective-permute-start.10) | collective-permute-done | bytes 262176 | tf_op jit(solution)/shard_map/ppermute | solution.py:296
  86.7 7.7 %collective-permute-done.11.refs_8_ = bf16[128,1024]{1,0:T(8,128)(2,1)S(1)} collective-permute-done((bf16[128,1024]{1,0:T(8,128)(2,1)S(1)}, bf16[128,1024]{1,0:T(8,128)(2,1)S(1)}, u32[]{:S(2)}, u32[]{:S(2)}) %collective-permute-start.11) | collective-permute-done | bytes 262176 | tf_op jit(solution)/shard_map/ppermute | solution.py:296
  95.0 3.8 %collective-permute-start.13 = (bf16[128,1024]{1,0:T(8,128)(2,1)S(1)}, bf16[128,1024]{1,0:T(8,128)(2,1)S(1)}, u32[]{:S(2)}, u32[]{:S(2)}) collective-permute-start(bf16[128,1024]{1,0:T(8,128)(2,1)S(1)} %get-tuple-element.56), channel_id=1, source_target_pairs={{0,28},{4,24},{8,20},{12,16},{16,12},{20,8},{24,4},{28,0},{1,29},{... | collective-permute-start | bytes 786440 | tf_op jit(solution)/shard_map/ppermute | solution.py:296
  98.8 8.4 %long_attend.1 = bf16[128,8192]{1,0:T(8,128)(2,1)} custom-call(s32[1]{0:T(128)} %bitcast.own_ref, bf16[128,64,128]{2,1,0:T(8,128)(2,1)S(1)} %copy-done, bf16[8,128,256]{2,1,0:T(8,128)(2,1)S(1)} %bitcast.8, bf16[8,128,256]{2,1,0:T(8,128)(2,1)S(1)} %collective-permute-done.7.refs_1_, bf16[8,128,256]{2,1,0:T(8,128)(2,1)S(1)} %collective-permute-done.8.refs_2_, ...), custom_call_target="tpu_custom_call" | custom-call | tf_op jit(solution)/shard_map/long_attend/pallas_call | solution.py:62
  107.2 2.9 %collective-permute-done.13.refs_10_ = bf16[128,1024]{1,0:T(8,128)(2,1)S(1)} collective-permute-done((bf16[128,1024]{1,0:T(8,128)(2,1)S(1)}, bf16[128,1024]{1,0:T(8,128)(2,1)S(1)}, u32[]{:S(2)}, u32[]{:S(2)}) %collective-permute-start.13) | collective-permute-done | bytes 262176 | tf_op jit(solution)/shard_map/ppermute | solution.py:296
  110.8 8.7 %collective-permute-done.15.refs_12_ = bf16[128,1536]{1,0:T(8,128)(2,1)S(1)} collective-permute-done((bf16[128,1536]{1,0:T(8,128)(2,1)S(1)}, bf16[128,1536]{1,0:T(8,128)(2,1)S(1)}, u32[]{:S(2)}, u32[]{:S(2)}) %collective-permute-start.15) | collective-permute-done | bytes 393248 | tf_op jit(solution)/shard_map/ppermute | solution.py:296
  119.5 0.9 copy-done.4
  120.5 0.9 copy-done.8
  121.4 0.9 copy-done.10
  122.3 0.9 copy-done.12
  123.2 2.7 %lay.1 = bf16[8,128,2048]{2,1,0:T(8,128)(2,1)} custom-call(s32[2]{0:T(128)S(1)} %pad_add_fusion.place_ref, bf16[128,512]{1,0:T(8,128)(2,1)S(1)} %get-tuple-element.59.refs_0_, bf16[128,512]{1,0:T(8,128)(2,1)S(1)} %copy-done.6, bf16[128,512]{1,0:T(8,128)(2,1)S(1)} %copy-done.8, bf16[128,512]{1,0:T(8,128)(2,1)S(1)} %copy-done.10, ...), custom_call_target="tpu_custom_call" | custom-call | tf_op jit(solution)/shard_map/lay/pallas_call | solution.py:257
  (64 shorter events, 5.6 us)
Async XLA Ops:
  3.3 11.4 %collective-permute-start.2 = (bf16[128,768]{1,0:T(8,128)(2,1)}, bf16[128,768]{1,0:T(8,128)(2,1)S(1)}, u32[]{:S(2)}, u32[]{:S(2)}) collective-permute-start(bf16[128,768]{1,0:T(8,128)(2,1)} %get-tuple-element.37), channel_id=1, source_target_pairs={{0,3},{1,2},{2,1},{3,0},{4,7},{5,6},{6,5},{7,4},{8,11},{9,10},{10,... | collective-permute-start | bytes 589832 | tf_op jit(solution)/shard_map/ppermute | solution.py:296
  4.1 11.1 %collective-permute-start.1 = (bf16[128,768]{1,0:T(8,128)(2,1)}, bf16[128,768]{1,0:T(8,128)(2,1)S(1)}, u32[]{:S(2)}, u32[]{:S(2)}) collective-permute-start(bf16[128,768]{1,0:T(8,128)(2,1)} %get-tuple-element.35), channel_id=1, source_target_pairs={{0,2},{1,3},{2,0},{3,1},{4,6},{5,7},{6,4},{7,5},{8,10},{9,11},{10,... | collective-permute-start | bytes 589832 | tf_op jit(solution)/shard_map/ppermute | solution.py:296
  5.4 9.9 %collective-permute-start = (bf16[128,768]{1,0:T(8,128)(2,1)}, bf16[128,768]{1,0:T(8,128)(2,1)S(1)}, u32[]{:S(2)}, u32[]{:S(2)}) collective-permute-start(bf16[128,768]{1,0:T(8,128)(2,1)} %get-tuple-element.33), channel_id=1, source_target_pairs={{0,1},{1,0},{2,3},{3,2},{4,5},{5,4},{6,7},{7,6},{8,9},{9,8},{10,11... | collective-permute-start | bytes 589832 | tf_op jit(solution)/shard_map/ppermute | solution.py:296
  9.4 4.3 %copy-start.22 = (bf16[128,8,256]{2,1,0:T(8,128)(2,1)S(1)}, bf16[128,8,256]{2,1,0:T(8,128)(2,1)}, u32[]{:S(2)}) copy-start(bf16[128,8,256]{2,1,0:T(8,128)(2,1)} %param.7) | copy-start | bytes 1572868
  9.4 5.8 %copy-start.19 = (bf16[128,768]{1,0:T(8,128)(2,1)S(1)}, bf16[128,768]{1,0:T(8,128)(2,1)}, u32[]{:S(2)}) copy-start(bf16[128,768]{1,0:T(8,128)(2,1)} %get-tuple-element.32.refs_0_.refs_1_) | copy-start | bytes 589828
  9.4 5.8 %copy-start.20 = (s32[8,8]{1,0:T(8,128)S(1)}, s32[8,8]{1,0:T(8,128)}, u32[]{:S(2)}) copy-start(s32[8,8]{1,0:T(8,128)} %lengths_ref.5) | copy-start | bytes 772
  9.4 5.8 %copy-start.21 = (s32[8,8]{1,0:T(8,128)S(1)}, s32[8,8]{1,0:T(8,128)}, u32[]{:S(2)}) copy-start(s32[8,8]{1,0:T(8,128)} %targets_ref.5) | copy-start | bytes 772
  9.4 25.2 %all-to-all-start = ((bf16[4,128,1792]{2,1,0:T(8,128)(2,1)}), bf16[4,128,1792]{2,1,0:T(8,128)(2,1)S(1)}, u32[]{:S(2)}, u32[]{:S(2)}) async-start(bf16[4,128,1792]{2,1,0:T(8,128)(2,1)} %prepare.2), calls=%async_computation | async-start | bytes 3670016 | tf_op jit(solution)/shard_map/all_to_all | solution.py:302
  21.1 23.2 %collective-permute-start.3 = (bf16[128,512]{1,0:T(8,128)(2,1)}, bf16[128,512]{1,0:T(8,128)(2,1)S(1)}, u32[]{:S(2)}, u32[]{:S(2)}) collective-permute-start(bf16[128,512]{1,0:T(8,128)(2,1)} %get-tuple-element.43), channel_id=1, source_target_pairs={{0,16},{4,20},{8,24},{12,28},{16,0},{20,4},{24,8},{28,12},{1,17},{... | collective-permute-start | bytes 393224 | tf_op jit(solution)/shard_map/ppermute | solution.py:296
  21.1 23.9 %collective-permute-start.4 = (bf16[128,512]{1,0:T(8,128)(2,1)}, bf16[128,512]{1,0:T(8,128)(2,1)S(1)}, u32[]{:S(2)}, u32[]{:S(2)}) collective-permute-start(bf16[128,512]{1,0:T(8,128)(2,1)} %get-tuple-element.44), channel_id=1, source_target_pairs={{0,20},{4,16},{8,28},{12,24},{16,4},{20,0},{24,12},{28,8},{1,21},{... | collective-permute-start | bytes 393224 | tf_op jit(solution)/shard_map/ppermute | solution.py:296
  24.4 21.2 %collective-permute-start.5 = (bf16[128,512]{1,0:T(8,128)(2,1)}, bf16[128,512]{1,0:T(8,128)(2,1)S(1)}, u32[]{:S(2)}, u32[]{:S(2)}) collective-permute-start(bf16[128,512]{1,0:T(8,128)(2,1)} %get-tuple-element.45), channel_id=1, source_target_pairs={{0,24},{4,28},{8,16},{12,20},{16,8},{20,12},{24,0},{28,4},{1,25},{... | collective-permute-start | bytes 393224 | tf_op jit(solution)/shard_map/ppermute | solution.py:296
  24.4 21.2 %collective-permute-start.6 = (bf16[128,512]{1,0:T(8,128)(2,1)}, bf16[128,512]{1,0:T(8,128)(2,1)S(1)}, u32[]{:S(2)}, u32[]{:S(2)}) collective-permute-start(bf16[128,512]{1,0:T(8,128)(2,1)} %get-tuple-element.46), channel_id=1, source_target_pairs={{0,28},{4,24},{8,20},{12,16},{16,12},{20,8},{24,4},{28,0},{1,29},{... | collective-permute-start | bytes 393224 | tf_op jit(solution)/shard_map/ppermute | solution.py:296
  37.8 1.0 copy-start.2
  38.8 80.7 %all-to-all-start.1 = ((bf16[8,128,512]{2,1,0:T(8,128)(2,1)}), bf16[8,128,512]{2,1,0:T(8,128)(2,1)S(1)}, u32[]{:S(2)}, u32[]{:S(2)}) async-start(bf16[8,128,512]{2,1,0:T(8,128)(2,1)} %copy-done.2), calls=%async_computation.1 | async-start | bytes 2097152 | tf_op jit(solution)/shard_map/all_to_all | solution.py:337
  44.3 6.5 %copy-start.1 = (bf16[128,8,256]{2,0,1:T(8,128)(2,1)S(1)}, bf16[128,8,256]{2,0,1:T(8,128)(2,1)}, u32[]{:S(2)}) copy-start(bf16[128,8,256]{2,0,1:T(8,128)(2,1)} %copy.10) | copy-start | bytes 1572868
  44.3 14.6 %copy-start.18 = (bf16[128,512]{1,0:T(8,128)(2,1)S(1)}, bf16[128,512]{1,0:T(8,128)(2,1)}, u32[]{:S(2)}) copy-start(bf16[128,512]{1,0:T(8,128)(2,1)} %copy-done.17) | copy-start | bytes 393220
  44.3 20.9 %copy-start.16 = (bf16[128,512]{1,0:T(8,128)(2,1)S(1)}, bf16[128,512]{1,0:T(8,128)(2,1)}, u32[]{:S(2)}) copy-start(bf16[128,512]{1,0:T(8,128)(2,1)} %copy-done.15) | copy-start | bytes 393220
  44.3 26.8 %copy-start.14 = (bf16[128,512]{1,0:T(8,128)(2,1)S(1)}, bf16[128,512]{1,0:T(8,128)(2,1)}, u32[]{:S(2)}) copy-start(bf16[128,512]{1,0:T(8,128)(2,1)} %copy-done.13) | copy-start | bytes 393220
  45.6 5.1 %copy-start.9 = (bf16[128,512]{1,0:T(8,128)(2,1)}, bf16[128,512]{1,0:T(8,128)(2,1)S(1)}, u32[]{:S(2)}) copy-start(bf16[128,512]{1,0:T(8,128)(2,1)S(1)} %collective-permute-done.5.refs_3_) | copy-start | bytes 393220
  45.7 5.1 %copy-start.11 = (bf16[128,512]{1,0:T(8,128)(2,1)}, bf16[128,512]{1,0:T(8,128)(2,1)S(1)}, u32[]{:S(2)}) copy-start(bf16[128,512]{1,0:T(8,128)(2,1)S(1)} %collective-permute-done.6.refs_4_) | copy-start | bytes 393220
  50.8 48.1 %copy-start = (bf16[128,64,128]{2,1,0:T(8,128)(2,1)S(1)}, bf16[128,64,128]{2,1,0:T(8,128)(2,1)}, u32[]{:S(2)}) copy-start(bf16[128,64,128]{2,1,0:T(8,128)(2,1)} %q_ref.4) | copy-start | bytes 6291460
  50.8 12.3 %collective-permute-start.7 = (bf16[8,128,256]{2,1,0:T(8,128)(2,1)S(1)}, bf16[8,128,256]{2,1,0:T(8,128)(2,1)S(1)}, u32[]{:S(2)}, u32[]{:S(2)}) collective-permute-start(bf16[8,128,256]{2,1,0:T(8,128)(2,1)S(1)} %bitcast.6), channel_id=1, source_target_pairs={{0,2},{1,3},{2,0},{3,1},{4,6},{5,7},{6,4},{7,5},{8,10},{9,11},{10,... | collective-permute-start | bytes 1572872 | tf_op jit(solution)/shard_map/ppermute | solution.py:90
  52.0 34.6 %collective-permute-start.10 = (bf16[128,1024]{1,0:T(8,128)(2,1)S(1)}, bf16[128,1024]{1,0:T(8,128)(2,1)S(1)}, u32[]{:S(2)}, u32[]{:S(2)}) collective-permute-start(bf16[128,1024]{1,0:T(8,128)(2,1)S(1)} %get-tuple-element.53), channel_id=1, source_target_pairs={{0,16},{4,20},{8,24},{12,28},{16,0},{20,4},{24,8},{28,12},{1,17},{... | collective-permute-start | bytes 786440 | tf_op jit(solution)/shard_map/ppermute | solution.py:296
  54.4 40.0 %collective-permute-start.11 = (bf16[128,1024]{1,0:T(8,128)(2,1)S(1)}, bf16[128,1024]{1,0:T(8,128)(2,1)S(1)}, u32[]{:S(2)}, u32[]{:S(2)}) collective-permute-start(bf16[128,1024]{1,0:T(8,128)(2,1)S(1)} %get-tuple-element.54), channel_id=1, source_target_pairs={{0,20},{4,16},{8,28},{12,24},{16,4},{20,0},{24,12},{28,8},{1,21},{... | collective-permute-start | bytes 786440 | tf_op jit(solution)/shard_map/ppermute | solution.py:296
  57.7 36.7 %collective-permute-start.8 = (bf16[8,128,256]{2,1,0:T(8,128)(2,1)S(1)}, bf16[8,128,256]{2,1,0:T(8,128)(2,1)S(1)}, u32[]{:S(2)}, u32[]{:S(2)}) collective-permute-start(bf16[8,128,256]{2,1,0:T(8,128)(2,1)S(1)} %bitcast.7), channel_id=1, source_target_pairs={{0,1},{1,0},{2,3},{3,2},{4,5},{5,4},{6,7},{7,6},{8,9},{9,8},{10,11... | collective-permute-start | bytes 1572872 | tf_op jit(solution)/shard_map/ppermute | solution.py:90
  63.1 31.9 %collective-permute-start.9 = (bf16[8,128,256]{2,1,0:T(8,128)(2,1)S(1)}, bf16[8,128,256]{2,1,0:T(8,128)(2,1)S(1)}, u32[]{:S(2)}, u32[]{:S(2)}) collective-permute-start(bf16[8,128,256]{2,1,0:T(8,128)(2,1)S(1)} %collective-permute-done.7.refs_1_), channel_id=1, source_target_pairs={{0,1},{1,0},{2,3},{3,2},{4,5},{5,4},{6,7},{7,6},{8,9},{9,8},{10,11... | collective-permute-start | bytes 1572872 | tf_op jit(solution)/shard_map/ppermute | solution.py:90
  65.2 45.6 %collective-permute-start.16 = (bf16[128,1536]{1,0:T(8,128)(2,1)S(1)}, bf16[128,1536]{1,0:T(8,128)(2,1)S(1)}, u32[]{:S(2)}, u32[]{:S(2)}) collective-permute-start(bf16[128,1536]{1,0:T(8,128)(2,1)S(1)} %pad_maximum_fusion.2), channel_id=1, source_target_pairs={{0,12},{4,8},{8,4},{12,0},{16,28},{20,24},{24,20},{28,16},{1,13},{... | collective-permute-start | bytes 1179656 | tf_op jit(solution)/shard_map/ppermute | solution.py:296
  71.1 48.4 %copy-start.6 = (bf16[128,512]{1,0:T(8,128)(2,1)S(1)}, bf16[128,512]{1,0:T(8,128)(2,1)}, u32[]{:S(2)}) copy-start(bf16[128,512]{1,0:T(8,128)(2,1)} %copy-done.5) | copy-start | bytes 393220
  86.7 32.9 %collective-permute-start.15 = (bf16[128,1536]{1,0:T(8,128)(2,1)S(1)}, bf16[128,1536]{1,0:T(8,128)(2,1)S(1)}, u32[]{:S(2)}, u32[]{:S(2)}) collective-permute-start(bf16[128,1536]{1,0:T(8,128)(2,1)S(1)} %pad_maximum_fusion.1), channel_id=1, source_target_pairs={{0,8},{4,12},{8,0},{12,4},{16,24},{20,28},{24,16},{28,20},{1,9},{5... | collective-permute-start | bytes 1179656 | tf_op jit(solution)/shard_map/ppermute | solution.py:296
  94.4 25.1 %collective-permute-start.14 = (bf16[128,1536]{1,0:T(8,128)(2,1)S(1)}, bf16[128,1536]{1,0:T(8,128)(2,1)S(1)}, u32[]{:S(2)}, u32[]{:S(2)}) collective-permute-start(bf16[128,1536]{1,0:T(8,128)(2,1)S(1)} %pad_maximum_fusion), channel_id=1, source_target_pairs={{0,4},{4,0},{8,12},{12,8},{16,20},{20,16},{24,28},{28,24},{1,5},{5... | collective-permute-start | bytes 1179656 | tf_op jit(solution)/shard_map/ppermute | solution.py:296
  94.4 12.8 %collective-permute-start.12 = (bf16[128,1024]{1,0:T(8,128)(2,1)S(1)}, bf16[128,1024]{1,0:T(8,128)(2,1)S(1)}, u32[]{:S(2)}, u32[]{:S(2)}) collective-permute-start(bf16[128,1024]{1,0:T(8,128)(2,1)S(1)} %get-tuple-element.55), channel_id=1, source_target_pairs={{0,24},{4,28},{8,16},{12,20},{16,8},{20,12},{24,0},{28,4},{1,25},{... | collective-permute-start | bytes 786440 | tf_op jit(solution)/shard_map/ppermute | solution.py:296
  95.0 15.1 %collective-permute-start.13 = (bf16[128,1024]{1,0:T(8,128)(2,1)S(1)}, bf16[128,1024]{1,0:T(8,128)(2,1)S(1)}, u32[]{:S(2)}, u32[]{:S(2)}) collective-permute-start(bf16[128,1024]{1,0:T(8,128)(2,1)S(1)} %get-tuple-element.56), channel_id=1, source_target_pairs={{0,28},{4,24},{8,20},{12,16},{16,12},{20,8},{24,4},{28,0},{1,29},{... | collective-permute-start | bytes 786440 | tf_op jit(solution)/shard_map/ppermute | solution.py:296
  (10 other events, 7.7 us)
